TPU v7x, 512 devices: a whole 4x4x16 slice. The times are simulated.
512 devices in a mesh: space: 64 (over z_hi, x, y), filt: 8 (over z_lo, core).
Axes of the slice: x: 4, y: 4, z: 16 (z_hi: 4, z_lo: 4; z = z_hi * 4 + z_lo), core: 2. Of those that a mesh axis runs over, the one named last changes fastest.
Arguments:
- volume: bfloat16 [64, 128, 8, 128], P('filt', 'space'), may hold values from -6 to 6
- weight: bfloat16 [27, 64, 128], P(None, None, 'filt'), may hold values from -0.21875 to 0.21875
- bias: float32 [128], P('filt'), may hold values from -3 to 3
- grad_out: bfloat16 [128, 128, 8, 128], P('filt', 'space'), may hold values from -6 to 6
Outputs:
- output: bfloat16 [128, 128, 8, 128], P('filt', 'space')
- grad_volume: bfloat16 [64, 128, 8, 128], P('filt', 'space')
- grad_weight: float32 [27, 64, 128], P(None, None, 'filt')
- grad_bias: float32 [128], P('filt')
All inputs are finite; a program needn't handle non-finite values.
Results may differ from a plain program's by a relative error of at most 0.0012.
Values may be sent and summed in bfloat16 or wider, within the bound.
No kernel may reach another device: no remote copies, remote signals or barrier semaphores. Data moves between devices by JAX's collectives and lax.ppermute only.
A program may use at most 64 MiB of HBM per device.

v0:
```python
import math

import jax
import jax.numpy as jnp
from jax import lax
from jax.sharding import PartitionSpec as P


def with_halo(cells, sides, width):
    for axis, dim in sides:
        count = lax.axis_size(axis)
        ends = count - 1
        head = lax.slice_in_dim(cells, 0, width, axis=dim)
        tail = lax.slice_in_dim(cells, cells.shape[dim] - width, cells.shape[dim], axis=dim)
        cells = jnp.concatenate(
            [
                lax.ppermute(tail, axis, [(i, (i + 1) % count) for i in range(ends)]),
                cells,
                lax.ppermute(head, axis, [((i + 1) % count, i) for i in range(ends)]),
            ],
            axis=dim,
        )
    return cells


def pad_plane(field):
    return jnp.pad(field, ((0, 0), (0, 0), (1, 1), (1, 1)))


def window(field, first, second, third, depth, rows, cols):
    return field[:, first : first + depth, second : second + rows, third : third + cols]


def depth_stack(field, starts, second, third, depth, rows, cols):
    return jnp.stack([window(field, first, second, third, depth, rows, cols) for first in starts])


def back_taps(taps_part, grad_pad, depth, rows, cols):
    total = jnp.zeros((taps_part.shape[1], depth, rows, cols), jnp.float32)
    for plane in range(9):
        b, c = (plane // 3, plane % 3)
        moved = depth_stack(grad_pad, (2, 1, 0), 2 - b, 2 - c, depth, rows, cols)
        total = total + jnp.einsum(
            "aco,aodhw->cdhw", taps_part[plane::9], moved, preferred_element_type=jnp.float32
        )
    return total


def local(volume, weight, bias, grad_out):
    depth = volume.shape[1]
    rows = volume.shape[2]
    cols = volume.shape[3]
    local_out = grad_out.shape[0]
    gathered = lax.all_gather(volume, "filt", axis=0, tiled=True)
    deep = with_halo(gathered, (("space", 1),), 1)
    padded = pad_plane(deep)
    total = jnp.zeros((local_out, depth, rows, cols), jnp.float32)
    grad_slots = [None] * 27
    for plane in range(9):
        b, c = (plane // 3, plane % 3)
        moved = depth_stack(padded, (0, 1, 2), b, c, depth, rows, cols)
        total = total + jnp.einsum(
            "aco,acdhw->odhw", weight[plane::9], moved, preferred_element_type=jnp.float32
        )
        three = jnp.einsum("acdhw,odhw->aco", moved, grad_out, preferred_element_type=jnp.float32)
        for a in range(3):
            grad_slots[9 * a + plane] = three[a]
    output = (total + bias[:, None, None, None]).astype(jnp.bfloat16)
    local_weight = jnp.stack(grad_slots)
    local_bias = jnp.sum(grad_out.astype(jnp.float32), axis=(1, 2, 3))
    summed_weight, summed_bias = lax.psum((local_weight, local_bias), "space")
    scale = 1.0 / math.sqrt(depth * lax.axis_size("space") * rows * cols)
    grad_weight = summed_weight * scale
    grad_bias = summed_bias * scale
    grad_deep = with_halo(grad_out, (("space", 1),), 1)
    grad_pad = pad_plane(grad_deep)
    grad_sum = lax.psum_scatter(
        back_taps(weight, grad_pad, depth, rows, cols), "filt", scatter_dimension=0, tiled=True
    )
    grad_volume = grad_sum.astype(jnp.bfloat16)
    return (output, grad_volume, grad_weight, grad_bias)


def solution(mesh):
    in_specs = (
        P("filt", "space", None, None),
        P(None, None, "filt"),
        P("filt"),
        P("filt", "space", None, None),
    )
    out_specs = (
        P("filt", "space", None, None),
        P("filt", "space", None, None),
        P(None, None, "filt"),
        P("filt"),
    )
    return jax.shard_map(local, mesh=mesh, in_specs=in_specs, out_specs=out_specs, check_vma=False)
```

profile of v0, /device:TPU:22, one launch (start us, length us, event | category | flops | bytes accessed | tf_op | source)
XLA Modules:
  0.0 1097.1 jit_solution(17635651127511497013)
XLA Ops:
  8.0 0.9 copy.230
  8.9 2.4 collective-permute-start.3
  11.3 3.5 collective-permute-start.2
  14.8 0.8 copy.8
  15.6 14.1 %all_gather.3 = bf16[64,2,8,128]{3,0,2,1:T(8,128)(2,1)S(1)} all-gather(bf16[8,2,8,128]{3,0,2,1:T(8,128)(2,1)S(1)} %copy.8), channel_id=1, replica_groups=mesh['space'=64,'filt'=8] {'filt'}, dimensions={0}, use_global_device_ids=true | all-gather | bytes 294912 | tf_op jit(solution)/shard_map/all_gather | solution.py:54
  29.7 11.3 %collective-permute-start = (bf16[64,1,8,128]{3,0,2,1:T(8,128)(2,1)S(1)}, bf16[64,1,8,128]{3,0,2,1:T(8,128)(2,1)S(1)}, u32[]{:S(2)}, u32[]{:S(2)}) collective-permute-start(bf16[64,1,8,128]{3,0,2,1:T(8,128)(2,1)S(1)} %get-tuple-element.58), channel_id=1, source_target_pairs={{0,8},{8,16},{16,24},{24,32},{32,40},{40,48},{48,56},{56,64},{64,7... | collective-permute-start | bytes 393224 | tf_op jit(solution)/shard_map/ppermute | solution.py:17
  41.0 1.9 collective-permute-start.1
  42.9 1.0 convert_reduce_fusion
  44.0 215.4 %psum.15 = f32[16]{0:T(128)S(1)} all-reduce(f32[16]{0:T(128)S(1)} %convert_reduce_fusion), channel_id=1, replica_groups=mesh['space'=64,'filt'=8] {'space'}, use_global_device_ids=true, to_apply=%region_3.4 | all-reduce | flops 16 | bytes 128 | tf_op jit(solution)/shard_map/psum | solution.py:71
  260.1 0.7 slice_bitcast_fusion.46
  260.8 0.9 slice_bitcast_fusion.47
  261.8 1.1 fusion.72
  262.9 1.1 fusion.66
  264.0 1.1 fusion.70
  265.1 1.1 fusion.68
  266.2 1.1 fusion.64
  267.3 1.1 fusion.60
  268.3 1.1 fusion.62
  269.4 1.1 convolution_bitcast_fusion
  271.5 1.3 slice_bitcast_fusion.20
  273.2 0.6 constant_dynamic-update-slice_fusion.26
  276.7 0.6 constant_dynamic-update-slice_fusion.25
  277.3 0.6 constant_dynamic-update-slice_fusion.24
  277.9 0.6 constant_dynamic-update-slice_fusion.23
  279.0 0.6 constant_dynamic-update-slice_fusion.22
  279.6 0.6 constant_dynamic-update-slice_fusion.21
  280.2 0.6 constant_dynamic-update-slice_fusion.20
  281.2 0.6 constant_dynamic-update-slice_fusion.19
  281.8 0.6 constant_dynamic-update-slice_fusion.18
  282.4 0.6 constant_dynamic-update-slice_fusion.17
  283.0 0.6 constant_dynamic-update-slice_fusion.16
  283.6 0.6 constant_dynamic-update-slice_fusion.15
  284.2 0.6 constant_dynamic-update-slice_fusion.14
  284.8 0.6 constant_dynamic-update-slice_fusion.13
  285.4 0.6 constant_dynamic-update-slice_fusion.12
  286.0 0.6 constant_dynamic-update-slice_fusion.11
  286.6 0.6 constant_dynamic-update-slice_fusion.10
  287.8 0.6 constant_dynamic-update-slice_fusion.8
  289.6 0.6 constant_dynamic-update-slice_fusion.5
  291.4 0.6 constant_dynamic-update-slice_fusion.2
  293.3 3.4 fusion.14
  296.8 1.3 fusion.34
  299.8 0.9 copy-done.3
  302.1 0.6 copy.44
  302.7 783.8 %all-reduce.4.cloned.1.call-done = f32[27,64,16]{1,2,0:T(8,128)} async-done(((f32[27,64,16]{1,2,0:T(8,128)}), f32[27,64,16]{1,2,0:T(8,128)}) %all-reduce.4.cloned.1.call-update) | async-done | bytes 110608 | tf_op jit(solution)/shard_map/psum | solution.py:71
  1086.6 1.6 broadcast_multiply_fusion
  1088.2 0.8 convert_element_type.14
  1089.1 0.6 copy.45
  (98 shorter events, 13.2 us)
Async XLA Ops:
  8.0 1078.6 %all-reduce.4.cloned.1.call-start = ((), (), s32[]{:S(2)}) async-start(), calls=%async_computation.2 | async-start | bytes 442368 | tf_op jit(solution)/shard_map/psum | solution.py:71
  8.9 251.0 %collective-permute-start.3 = (bf16[16,1,8,128]{3,0,2,1:T(8,128)(2,1)S(1)}, bf16[16,1,8,128]{3,0,2,1:T(8,128)(2,1)S(1)}, u32[]{:S(2)}, u32[]{:S(2)}) collective-permute-start(bf16[16,1,8,128]{3,0,2,1:T(8,128)(2,1)S(1)} %get-tuple-element.62), channel_id=1, source_target_pairs={{8,0},{16,8},{24,16},{32,24},{40,32},{48,40},{56,48},{64,56},{72,6... | collective-permute-start | bytes 98312 | tf_op jit(solution)/shard_map/ppermute | solution.py:19
  11.3 248.6 %collective-permute-start.2 = (bf16[16,1,8,128]{3,0,2,1:T(8,128)(2,1)S(1)}, bf16[16,1,8,128]{3,0,2,1:T(8,128)(2,1)S(1)}, u32[]{:S(2)}, u32[]{:S(2)}) collective-permute-start(bf16[16,1,8,128]{3,0,2,1:T(8,128)(2,1)S(1)} %get-tuple-element.63), channel_id=1, source_target_pairs={{0,8},{8,16},{16,24},{24,32},{32,40},{40,48},{48,56},{56,64},{64,7... | collective-permute-start | bytes 98312 | tf_op jit(solution)/shard_map/ppermute | solution.py:17
  29.7 240.9 %collective-permute-start = (bf16[64,1,8,128]{3,0,2,1:T(8,128)(2,1)S(1)}, bf16[64,1,8,128]{3,0,2,1:T(8,128)(2,1)S(1)}, u32[]{:S(2)}, u32[]{:S(2)}) collective-permute-start(bf16[64,1,8,128]{3,0,2,1:T(8,128)(2,1)S(1)} %get-tuple-element.58), channel_id=1, source_target_pairs={{0,8},{8,16},{16,24},{24,32},{32,40},{40,48},{48,56},{56,64},{64,7... | collective-permute-start | bytes 393224 | tf_op jit(solution)/shard_map/ppermute | solution.py:17
  41.0 229.5 %collective-permute-start.1 = (bf16[64,1,8,128]{3,0,2,1:T(8,128)(2,1)S(1)}, bf16[64,1,8,128]{3,0,2,1:T(8,128)(2,1)S(1)}, u32[]{:S(2)}, u32[]{:S(2)}) collective-permute-start(bf16[64,1,8,128]{3,0,2,1:T(8,128)(2,1)S(1)} %get-tuple-element.59), channel_id=1, source_target_pairs={{8,0},{16,8},{24,16},{32,24},{40,32},{48,40},{56,48},{64,56},{72,6... | collective-permute-start | bytes 393224 | tf_op jit(solution)/shard_map/ppermute | solution.py:19
  260.8 1.0 copy-start.9
  270.5 0.9 copy-start.5
  270.5 0.9 copy-start.7
  271.5 1.4 copy-start.11
  271.5 1.4 copy-start.13
  271.5 1.4 copy-start.15
  271.5 1.4 copy-start.4
  272.8 8.1 copy-start.17
  272.8 8.1 copy-start.19
  272.8 8.0 copy-start.21
  275.9 2.7 copy-start
  275.9 2.7 copy-start.2
  275.9 2.6 copy-start.6
  276.0 2.6 copy-start.8
  278.6 2.6 copy-start.23
  278.6 2.6 copy-start.24
  293.3 795.0 %reduce-scatter.2.cloned.1.call-start = ((), (), s32[]{:S(2)}) async-start(), calls=%async_computation.1 | async-start | bytes 589824 | tf_op jit(solution)/shard_map/reduce_scatter | solution.py:77
  296.8 1.3 copy-start.10
  298.4 1.0 copy-start.18
  298.4 1.0 copy-start.20
  298.4 1.1 copy-start.22
  299.5 1.1 copy-start.3
  299.5 1.4 copy-start.1
  300.7 1.0 copy-start.12
  300.7 1.1 copy-start.14
  300.7 1.2 copy-start.16
  300.7 1.2 copy-start.25
Sparse Core Ops, SparseCore 0:
  293.4 793.1 all-reduce.3
Sparse Core Ops, SparseCore 1:
  296.9 51.2 reduce-scatter.1
where the time goes:
time: 1100 us
  waiting for transfers between devices  784 us (71%)
  blocking collectives  230 us (21%)
  local copies, waits for them, and re-layouts  24.4 us (2%)
  starting transfers between devices  19.2 us (2%)
  matrix products  18.9 us (2%)
  between operations  15.8 us (1%)
    psum x1, waiting for transfers between devices, local(): summed_weight, summed_bias = lax.psum((local_weight, local_bias), 'space')  784 us
    psum x1, blocking collectives, local(): summed_weight, summed_bias = lax.psum((local_weight, local_bias), 'space')  215 us
  transfers between devices with their start and end apart: 6, of which 1 were waited for; matrix products, arithmetic and copies ran while one was open for 2% of the time, Pallas kernels for 0%

commit v1 on v0

v1 whole, which is shorter than its diff:
```python
import math

import jax
import jax.numpy as jnp
from jax import lax
from jax.experimental import pallas as pl
from jax.experimental.pallas import tpu as pltpu
from jax.sharding import PartitionSpec as P

F32 = jnp.float32
BF16 = jnp.bfloat16


def dot(left, right):
    return lax.dot_general(left, right, (((1,), (0,)), ((), ())), preferred_element_type=F32)


def dot_lanes(left, right):
    return lax.dot_general(left, right, (((1,), (1,)), ((), ())), preferred_element_type=F32)


def slide(rows, step):
    size = rows.shape[-1]
    axis = rows.ndim - 1
    turned = pltpu.roll(rows, (-step) % size, axis)
    lane = lax.broadcasted_iota(jnp.int32, rows.shape, axis)
    edge = size - 1 if step > 0 else 0
    return jnp.where(lane == edge, 0.0, turned)


def kernel(
    vol_ref, grad_ref, before_ref, after_ref, taps_ref,
    sums_ref, back_ref, out_ref, low_ref, high_ref,
    vpad, gpad, mid,
):
    depth, rows, chans, cols = vol_ref.shape
    outs = grad_ref.shape[2]
    blank = jnp.zeros((chans, cols), BF16)
    for d in range(depth):
        vpad[d, 0] = blank
        vpad[d, rows + 1] = blank
        vpad[d, 1 : rows + 1] = vol_ref[d]
    blank = jnp.zeros((3 * outs, cols), BF16)
    bias_sum = jnp.zeros((outs, cols), F32)
    for p in range(depth + 2):
        gpad[p, 0] = blank
        gpad[p, rows + 1] = blank
        for h in range(rows):
            if p == 0:
                line = before_ref[0, h]
            elif p == depth + 1:
                line = after_ref[0, h]
            else:
                line = grad_ref[p - 1, h]
            wide = line.astype(F32)
            if 0 < p < depth + 1:
                bias_sum = bias_sum + wide
            gpad[p, h + 1, 0:outs] = slide(wide, 1).astype(BF16)
            gpad[p, h + 1, outs : 2 * outs] = line
            gpad[p, h + 1, 2 * outs : 3 * outs] = slide(wide, -1).astype(BF16)
    taps = taps_ref[...]
    ahead = jnp.concatenate(
        [
            jnp.concatenate([taps[9 * a + 3 * b + c] for b in range(3)], axis=1)
            for a in range(3)
            for c in range(3)
        ],
        axis=0,
    )
    flat = taps.reshape(27 * outs, chans)
    behind = flat.astype(F32).T.astype(BF16)
    acc = jnp.zeros((27 * outs, chans), F32)
    for d in range(depth):
        for h in range(0, rows, 2):
            stack = jnp.concatenate(
                [vpad[d, h + k : h + k + 3].reshape(3 * chans, cols) for k in range(2)], axis=1
            )
            part = dot(ahead, stack)
            for k in range(2):
                mid[d, h + k] = part[:, k * cols : (k + 1) * cols]
            moved = jnp.concatenate(
                [
                    jnp.concatenate(
                        [gpad[d + 2 - a, h + k + 2 - b] for a in range(3) for b in range(3)], axis=0
                    )
                    for k in range(2)
                ],
                axis=1,
            )
            back = dot(behind, moved)
            for k in range(2):
                for f in range(chans // 8):
                    back_ref[f, d, h + k] = back[8 * f : 8 * f + 8, k * cols : (k + 1) * cols]
            cells = jnp.concatenate([vol_ref[d, h], vol_ref[d, h + 1]], axis=1)
            acc = acc + dot_lanes(moved, cells)
    for e in range(-1, depth + 1):
        for h in range(rows):
            total = None
            for d in range(depth):
                a = d - e + 1
                if 0 <= a <= 2:
                    piece = mid[d, h, 3 * outs * a : 3 * outs * (a + 1)]
                    total = piece if total is None else total + piece
            line = (
                total[outs : 2 * outs]
                + slide(total[0:outs], -1)
                + slide(total[2 * outs : 3 * outs], 1)
            )
            if e < 0:
                low_ref[h] = line
            elif e == depth:
                high_ref[h] = line
            else:
                out_ref[e, h] = line
    half = cols // 2
    bias_half = bias_sum[:, :half] + bias_sum[:, half:]
    for r in range(14):
        first = acc[2 * r * outs : (2 * r + 1) * outs]
        second = bias_half if r == 13 else acc[(2 * r + 1) * outs : (2 * r + 2) * outs]
        sums_ref[r] = jnp.concatenate([first, second], axis=1)
    for r in range(14, 16):
        sums_ref[r] = jnp.zeros((outs, cols), F32)


def compute(vol, grad, before, after, taps):
    depth, rows, chans, cols = vol.shape
    outs = grad.shape[2]
    shapes = (
        jax.ShapeDtypeStruct((16, outs, cols), F32),
        jax.ShapeDtypeStruct((chans // 8, depth, rows, 8, cols), F32),
        jax.ShapeDtypeStruct((depth, rows, outs, cols), F32),
        jax.ShapeDtypeStruct((rows, outs, cols), F32),
        jax.ShapeDtypeStruct((rows, outs, cols), F32),
    )
    whole = pl.BlockSpec(memory_space=pltpu.VMEM)
    return pl.pallas_call(
        kernel,
        out_shape=shapes,
        in_specs=[whole] * 5,
        out_specs=(whole,) * 5,
        scratch_shapes=[
            pltpu.VMEM((depth, rows + 2, chans, cols), BF16),
            pltpu.VMEM((depth + 2, rows + 2, 3 * outs, cols), BF16),
            pltpu.VMEM((depth, rows, 9 * outs, cols), F32),
        ],
        compiler_params=pltpu.CompilerParams(vmem_limit_bytes=40 * 1024 * 1024),
    )(vol, grad, before, after, taps)


XY_GROUPS = [[16 * z + k for k in range(16)] for z in range(4)]
Z_GROUPS = [[16 * z + k for z in range(4)] for k in range(16)]
UP = [(i, i + 1) for i in range(63)]
DOWN = [(i + 1, i) for i in range(63)]


def local(volume, weight, bias, grad_out):
    depth, rows, cols = volume.shape[1:]
    grad = grad_out.transpose(1, 2, 0, 3)
    before = lax.ppermute(grad[depth - 1 :], "space", UP)
    after = lax.ppermute(grad[:1], "space", DOWN)
    vol = lax.all_gather(volume.transpose(1, 2, 0, 3), "filt", axis=2, tiled=True)
    sums, back, out, low, high = compute(vol, grad, before, after, weight.transpose(0, 2, 1))
    from_above = lax.ppermute(low, "space", DOWN)
    from_below = lax.ppermute(high, "space", UP)
    parts = lax.all_to_all(sums, "space", 0, 0, axis_index_groups=XY_GROUPS)
    mine = lax.psum(jnp.sum(parts, axis=0), "space", axis_index_groups=Z_GROUPS)
    every = lax.all_to_all(
        jnp.broadcast_to(mine[None], (16,) + mine.shape), "space", 0, 0, axis_index_groups=XY_GROUPS
    )
    scale = 1.0 / math.sqrt(depth * lax.axis_size("space") * rows * cols)
    outs = grad_out.shape[0]
    every = every * scale
    halves = every.reshape(16, outs, 2, cols // 2)
    grad_weight = halves.transpose(0, 2, 3, 1).reshape(32, cols // 2, outs)[:27]
    grad_bias = jnp.sum(every[13, :, cols // 2 :], axis=1)
    shares = lax.all_to_all(back, "filt", 0, 0)
    grad_volume = jnp.sum(shares, axis=0).astype(BF16).transpose(2, 0, 1, 3)
    out = out + jnp.concatenate([from_below[None], from_above[None]], axis=0) + bias[None, None, :, None]
    output = out.astype(BF16).transpose(2, 0, 1, 3)
    return (output, grad_volume, grad_weight, grad_bias)


def solution(mesh):
    in_specs = (
        P("filt", "space", None, None),
        P(None, None, "filt"),
        P("filt"),
        P("filt", "space", None, None),
    )
    out_specs = (
        P("filt", "space", None, None),
        P("filt", "space", None, None),
        P(None, None, "filt"),
        P("filt"),
    )
    return jax.shard_map(local, mesh=mesh, in_specs=in_specs, out_specs=out_specs, check_vma=False)
```

time: 1100 us -> 102 us (0.09)
  the two profiles are of different devices: /device:TPU:22 before, /device:TPU:94 now
where the time goes in v1:
time: 102 us
  blocking collectives  53.4 us (52%)
  starting transfers between devices  30 us (29%)
  waiting for transfers between devices  11.2 us (11%)
  local copies, waits for them, and re-layouts  3.73 us (4%)
  Pallas kernels  1.9 us (2%)
    psum x1, blocking collectives, local(): mine = lax.psum(jnp.sum(parts, axis=0), 'space', axis_index_groups=Z_GROUPS)  19.5 us
    all_gather x1, blocking collectives, local(): lax.all_gather(volume.transpose(1, 2, 0, 3), 'filt', axis=2, tiled=True)  11.8 us
    all_to_all x1, blocking collectives, local(): lax.all_to_all(jnp.broadcast_to(mine[None], (16,) + mine.shape), 'space',...  11.3 us
    ppermute x1, starting transfers between devices, local(): from_below = lax.ppermute(high, 'space', UP)  11.1 us
    ppermute x1, waiting for transfers between devices, local(): from_above = lax.ppermute(low, 'space', DOWN)  10.7 us
    all_to_all x1, blocking collectives, local(): parts = lax.all_to_all(sums, 'space', 0, 0, axis_index_groups=XY_GROUPS)  10.7 us
    ppermute x1, starting transfers between devices, local(): before = lax.ppermute(grad[depth - 1:], 'space', UP)  8.67 us
    all_to_all x1, starting transfers between devices, local(): shares = lax.all_to_all(back, 'filt', 0, 0)  5.47 us
  transfers between devices with their start and end apart: 5, of which 2 were waited for; matrix products, arithmetic and copies ran while one was open for 2% of the time, Pallas kernels for 0%

profile of v1, /device:TPU:94, one launch (start us, length us, event | category | flops | bytes accessed | tf_op | source)
XLA Modules:
  0.0 101.8 jit_solution(13897570858478928110)
XLA Ops:
  0.6 0.9 copy.25
  1.5 0.0 copy-start.1
  1.5 8.7 %collective-permute-start = (bf16[1,8,16,128]{3,2,1,0:T(8,128)(2,1)S(1)}, bf16[1,8,16,128]{3,2,1,0:T(8,128)(2,1)S(1)}, u32[]{:S(2)}, u32[]{:S(2)}) collective-permute-start(bf16[1,8,16,128]{3,2,1,0:T(8,128)(2,1)S(1)} %get-tuple-element.31), channel_id=1, source_target_pairs={{0,8},{8,16},{16,24},{24,32},{32,40},{40,48},{48,56},{56,64},{64,7... | collective-permute-start | bytes 98312 | tf_op jit(solution)/shard_map/ppermute | solution.py:159
  10.2 1.9 %collective-permute-start.1 = (bf16[1,8,16,128]{3,2,1,0:T(8,128)(2,1)S(1)}, bf16[1,8,16,128]{3,2,1,0:T(8,128)(2,1)S(1)}, u32[]{:S(2)}, u32[]{:S(2)}) collective-permute-start(bf16[1,8,16,128]{3,2,1,0:T(8,128)(2,1)S(1)} %get-tuple-element.30), channel_id=1, source_target_pairs={{8,0},{16,8},{24,16},{32,24},{40,32},{48,40},{56,48},{64,56},{72,6... | collective-permute-start | bytes 98312 | tf_op jit(solution)/shard_map/ppermute | solution.py:160
  12.1 0.0 copy-done.1
  12.2 0.0 copy-start
  12.2 11.8 %all_gather.3.vol_ref = bf16[2,8,64,128]{3,2,1,0:T(8,128)(2,1)S(1)} all-gather(bf16[2,8,8,128]{3,2,1,0:T(8,128)(2,1)S(1)} %bitcast.22), channel_id=1, replica_groups=mesh['space'=64,'filt'=8] {'filt'}, dimensions={2}, use_global_device_ids=true | all-gather | bytes 294912 | tf_op jit(solution)/shard_map/all_gather | solution.py:161
  24.0 0.0 collective-permute-done.before_ref
  24.0 0.4 collective-permute-done.1.after_ref
  24.4 0.0 copy-done
  24.4 1.9 %shard_map.75 = (f32[16,16,128]{2,1,0:T(8,128)S(1)}, f32[8,2,8,8,128]{4,3,2,1,0:T(8,128)}, f32[2,8,16,128]{3,2,1,0:T(8,128)S(1)}, f32[8,16,128]{2,1,0:T(8,128)S(1)}, f32[8,16,128]{2,1,0:T(8,128)S(1)}) custom-call(bf16[2,8,64,128]{3,2,1,0:T(8,128)(2,1)S(1)} %all_gather.3.vol_ref, bf16[2,8,16,128]{3,2,1,0:T(8,128)(2,1)S(1)} %bitcast.17, ...), custom_call_target="tpu_custom_call" | custom-call | tf_op jit(solution)/shard_map/pallas_call | solution.py:136
  26.3 10.7 %all_to_all.15 = f32[16,16,128]{2,1,0:T(8,128)S(1)} all-to-all(f32[16,16,128]{2,1,0:T(8,128)S(1)} %get-tuple-element.13), channel_id=1, replica_groups={{0,8,16,24,32,40,48,56,64,72,80,88,96,104,112,120},{128,136,144,152,160..., dimensions={0} | all-to-all | bytes 262144 | tf_op jit(solution)/shard_map/all_to_all | solution.py:165
  37.0 19.5 %psum.7 = f32[16,128]{1,0:T(8,128)S(1)} all-reduce(f32[16,128]{1,0:T(8,128)S(1)} %reduce_sum.28), channel_id=1, replica_groups={{0,128,256,384},{8,136,264,392},{16,144,272,400},{24,152,280,408},{32,1..., use_global_device_ids=true, to_apply=%region_2.0 | all-reduce | flops 2048 | bytes 16384 | tf_op jit(solution)/shard_map/psum | solution.py:166
  56.6 11.3 %all_to_all.16 = f32[16,16,128]{2,1,0:T(8,128)S(1)} all-to-all(f32[16,16,128]{2,1,0:T(8,128)S(1)} %broadcast_in_dim.15), channel_id=1, replica_groups={{0,8,16,24,32,40,48,56,64,72,80,88,96,104,112,120},{128,136,144,152,160..., dimensions={0} | all-to-all | bytes 262144 | tf_op jit(solution)/shard_map/all_to_all | solution.py:167
  67.9 5.5 %all-to-all-start = ((f32[8,2,8,8,128]{4,3,2,1,0:T(8,128)}), f32[8,2,8,8,128]{4,3,2,1,0:T(8,128)S(1)}, u32[]{:S(2)}, u32[]{:S(2)}) async-start(f32[8,2,8,8,128]{4,3,2,1,0:T(8,128)} %get-tuple-element.12), calls=%async_computation | async-start | bytes 1048576 | tf_op jit(solution)/shard_map/all_to_all | solution.py:176
  73.4 2.8 %collective-permute-start.3 = (f32[8,16,128]{2,1,0:T(8,128)S(1)}, f32[8,16,128]{2,1,0:T(8,128)S(1)}, u32[]{:S(2)}, u32[]{:S(2)}) collective-permute-start(f32[8,16,128]{2,1,0:T(8,128)S(1)} %get-tuple-element.11), channel_id=1, source_target_pairs={{8,0},{16,8},{24,16},{32,24},{40,32},{48,40},{56,48},{64,56},{72,6... | collective-permute-start | bytes 196616 | tf_op jit(solution)/shard_map/ppermute | solution.py:163
  76.2 11.1 %collective-permute-start.2 = (f32[8,16,128]{2,1,0:T(8,128)S(1)}, f32[8,16,128]{2,1,0:T(8,128)S(1)}, u32[]{:S(2)}, u32[]{:S(2)}) collective-permute-start(f32[8,16,128]{2,1,0:T(8,128)S(1)} %get-tuple-element.10), channel_id=1, source_target_pairs={{0,8},{8,16},{16,24},{24,32},{32,40},{40,48},{48,56},{56,64},{64,7... | collective-permute-start | bytes 196616 | tf_op jit(solution)/shard_map/ppermute | solution.py:164
  87.4 10.7 %collective-permute-done.3 = f32[8,16,128]{2,1,0:T(8,128)S(1)} collective-permute-done((f32[8,16,128]{2,1,0:T(8,128)S(1)}, f32[8,16,128]{2,1,0:T(8,128)S(1)}, u32[]{:S(2)}, u32[]{:S(2)}) %collective-permute-start.3) | collective-permute-done | bytes 65568 | tf_op jit(solution)/shard_map/ppermute | solution.py:163
  98.1 0.0 collective-permute-done.2
  98.1 0.0 copy-start.2
  98.1 0.7 copy-done.2
  98.8 0.1 fusion.2
  98.8 0.6 copy.21
  99.5 0.2 reshape.16
  99.7 0.7 slice.18
  100.4 0.7 slice_reduce_fusion
  101.1 0.0 all-to-all-done
  101.2 0.6 copy.22
  (7 shorter events, 0.1 us)
Async XLA Ops:
  1.5 10.6 %copy-start.1 = (bf16[8,2,8,128]{3,2,1,0:T(8,128)(2,1)S(1)}, bf16[8,2,8,128]{3,2,1,0:T(8,128)(2,1)}, u32[]{:S(2)}) copy-start(bf16[8,2,8,128]{3,2,1,0:T(8,128)(2,1)} %param.4) | copy-start | bytes 98308
  1.5 22.5 %collective-permute-start = (bf16[1,8,16,128]{3,2,1,0:T(8,128)(2,1)S(1)}, bf16[1,8,16,128]{3,2,1,0:T(8,128)(2,1)S(1)}, u32[]{:S(2)}, u32[]{:S(2)}) collective-permute-start(bf16[1,8,16,128]{3,2,1,0:T(8,128)(2,1)S(1)} %get-tuple-element.31), channel_id=1, source_target_pairs={{0,8},{8,16},{16,24},{24,32},{32,40},{40,48},{48,56},{56,64},{64,7... | collective-permute-start | bytes 98312 | tf_op jit(solution)/shard_map/ppermute | solution.py:159
  10.2 14.2 %collective-permute-start.1 = (bf16[1,8,16,128]{3,2,1,0:T(8,128)(2,1)S(1)}, bf16[1,8,16,128]{3,2,1,0:T(8,128)(2,1)S(1)}, u32[]{:S(2)}, u32[]{:S(2)}) collective-permute-start(bf16[1,8,16,128]{3,2,1,0:T(8,128)(2,1)S(1)} %get-tuple-element.30), channel_id=1, source_target_pairs={{8,0},{16,8},{24,16},{32,24},{40,32},{48,40},{56,48},{64,56},{72,6... | collective-permute-start | bytes 98312 | tf_op jit(solution)/shard_map/ppermute | solution.py:160
  12.2 12.3 %copy-start = (bf16[27,64,16]{1,2,0:T(8,128)(2,1)S(1)}, bf16[27,64,16]{1,2,0:T(8,128)(2,1)}, u32[]{:S(2)}) copy-start(bf16[27,64,16]{1,2,0:T(8,128)(2,1)} %param.5) | copy-start | bytes 165892
  67.9 33.2 %all-to-all-start = ((f32[8,2,8,8,128]{4,3,2,1,0:T(8,128)}), f32[8,2,8,8,128]{4,3,2,1,0:T(8,128)S(1)}, u32[]{:S(2)}, u32[]{:S(2)}) async-start(f32[8,2,8,8,128]{4,3,2,1,0:T(8,128)} %get-tuple-element.12), calls=%async_computation | async-start | bytes 1048576 | tf_op jit(solution)/shard_map/all_to_all | solution.py:176
  73.4 24.7 %collective-permute-start.3 = (f32[8,16,128]{2,1,0:T(8,128)S(1)}, f32[8,16,128]{2,1,0:T(8,128)S(1)}, u32[]{:S(2)}, u32[]{:S(2)}) collective-permute-start(f32[8,16,128]{2,1,0:T(8,128)S(1)} %get-tuple-element.11), channel_id=1, source_target_pairs={{8,0},{16,8},{24,16},{32,24},{40,32},{48,40},{56,48},{64,56},{72,6... | collective-permute-start | bytes 196616 | tf_op jit(solution)/shard_map/ppermute | solution.py:163
  76.2 21.9 %collective-permute-start.2 = (f32[8,16,128]{2,1,0:T(8,128)S(1)}, f32[8,16,128]{2,1,0:T(8,128)S(1)}, u32[]{:S(2)}, u32[]{:S(2)}) collective-permute-start(f32[8,16,128]{2,1,0:T(8,128)S(1)} %get-tuple-element.10), channel_id=1, source_target_pairs={{0,8},{8,16},{16,24},{24,32},{32,40},{40,48},{48,56},{56,64},{64,7... | collective-permute-start | bytes 196616 | tf_op jit(solution)/shard_map/ppermute | solution.py:164
  98.1 0.7 copy-start.2

commit v2 on v1

--- a/solution.py
+++ b/solution.py
@@ -33,13 +33,15 @@
     sums_ref, back_ref, out_ref, low_ref, high_ref,
     vpad, gpad, mid,
 ):
-    depth, rows, chans, cols = vol_ref.shape
+    peers, depth, rows, share, cols = vol_ref.shape
+    chans = peers * share
     outs = grad_ref.shape[2]
     blank = jnp.zeros((chans, cols), BF16)
     for d in range(depth):
         vpad[d, 0] = blank
         vpad[d, rows + 1] = blank
-        vpad[d, 1 : rows + 1] = vol_ref[d]
+        for h in range(rows):
+            vpad[d, h + 1] = jnp.concatenate([vol_ref[s, d, h] for s in range(peers)], axis=0)
     blank = jnp.zeros((3 * outs, cols), BF16)
     bias_sum = jnp.zeros((outs, cols), F32)
     for p in range(depth + 2):
@@ -91,7 +93,7 @@
             for k in range(2):
                 for f in range(chans // 8):
                     back_ref[f, d, h + k] = back[8 * f : 8 * f + 8, k * cols : (k + 1) * cols]
-            cells = jnp.concatenate([vol_ref[d, h], vol_ref[d, h + 1]], axis=1)
+            cells = jnp.concatenate([vpad[d, h + 1], vpad[d, h + 2]], axis=1)
             acc = acc + dot_lanes(moved, cells)
     for e in range(-1, depth + 1):
         for h in range(rows):
@@ -123,7 +125,8 @@
 
 
 def compute(vol, grad, before, after, taps):
-    depth, rows, chans, cols = vol.shape
+    peers, depth, rows, share, cols = vol.shape
+    chans = peers * share
     outs = grad.shape[2]
     shapes = (
         jax.ShapeDtypeStruct((16, outs, cols), F32),
@@ -149,21 +152,31 @@
 
 XY_GROUPS = [[16 * z + k for k in range(16)] for z in range(4)]
 Z_GROUPS = [[16 * z + k for z in range(4)] for k in range(16)]
-UP = [(i, i + 1) for i in range(63)]
-DOWN = [(i + 1, i) for i in range(63)]
+EVEN = [(i, i ^ 1) for i in range(64)]
+ODD = [(i, ((i + 1) ^ 1) - 1) for i in range(1, 63)]
+
+
+def swap_edges(head, tail):
+    odd = (lax.axis_index("space") % 2) == 1
+    inner = lax.ppermute(jnp.where(odd, head, tail), "space", EVEN)
+    outer = lax.ppermute(jnp.where(odd, tail, head), "space", ODD)
+    return jnp.where(odd, inner, outer), jnp.where(odd, outer, inner)
 
 
 def local(volume, weight, bias, grad_out):
     depth, rows, cols = volume.shape[1:]
     grad = grad_out.transpose(1, 2, 0, 3)
-    before = lax.ppermute(grad[depth - 1 :], "space", UP)
-    after = lax.ppermute(grad[:1], "space", DOWN)
-    vol = lax.all_gather(volume.transpose(1, 2, 0, 3), "filt", axis=2, tiled=True)
+    before, after = swap_edges(grad[:1], grad[depth - 1 :])
+    own = volume.transpose(1, 2, 0, 3)
+    vol = lax.all_to_all(jnp.broadcast_to(own[None], (8,) + own.shape), "filt", 0, 0)
     sums, back, out, low, high = compute(vol, grad, before, after, weight.transpose(0, 2, 1))
-    from_above = lax.ppermute(low, "space", DOWN)
-    from_below = lax.ppermute(high, "space", UP)
+    from_below, from_above = swap_edges(low, high)
+    shares = lax.all_to_all(back, "filt", 0, 0)
     parts = lax.all_to_all(sums, "space", 0, 0, axis_index_groups=XY_GROUPS)
     mine = lax.psum(jnp.sum(parts, axis=0), "space", axis_index_groups=Z_GROUPS)
+    mine, shares, from_below, from_above = lax.optimization_barrier(
+        (mine, shares, from_below, from_above)
+    )
     every = lax.all_to_all(
         jnp.broadcast_to(mine[None], (16,) + mine.shape), "space", 0, 0, axis_index_groups=XY_GROUPS
     )
@@ -173,7 +186,6 @@
     halves = every.reshape(16, outs, 2, cols // 2)
     grad_weight = halves.transpose(0, 2, 3, 1).reshape(32, cols // 2, outs)[:27]
     grad_bias = jnp.sum(every[13, :, cols // 2 :], axis=1)
-    shares = lax.all_to_all(back, "filt", 0, 0)
     grad_volume = jnp.sum(shares, axis=0).astype(BF16).transpose(2, 0, 1, 3)
     out = out + jnp.concatenate([from_below[None], from_above[None]], axis=0) + bias[None, None, :, None]
     output = out.astype(BF16).transpose(2, 0, 1, 3)

time: 102 us -> 101 us (level)
  the two profiles are of different devices: /device:TPU:94 before, /device:TPU:64 now
where the time goes in v2:
time: 101 us; the launch traced here: 100 us
  blocking collectives  46.7 us (46%)
  starting transfers between devices  34.4 us (34%)
  waiting for transfers between devices  10.3 us (10%)
  local copies, waits for them, and re-layouts  5.04 us (5%)
  Pallas kernels  1.92 us (2%)
    psum x1, blocking collectives, local(): mine = lax.psum(jnp.sum(parts, axis=0), 'space', axis_index_groups=Z_GROUPS)  27.2 us
    all_to_all x1, blocking collectives, local(): parts = lax.all_to_all(sums, 'space', 0, 0, axis_index_groups=XY_GROUPS)  19.4 us
    all_to_all x1, starting transfers between devices, local(): lax.all_to_all(jnp.broadcast_to(mine[None], (16,) + mine.shape), 'space',...  11.2 us
    all_to_all x1, starting transfers between devices, local(): lax.all_to_all(jnp.broadcast_to(own[None], (8,) + own.shape), 'filt', 0, 0)  8.49 us
    ppermute x2, starting transfers between devices, swap_edges(): inner = lax.ppermute(jnp.where(odd, head, tail), 'space', EVEN)  8.13 us
    all_to_all x1, waiting for transfers between devices, local(): lax.all_to_all(jnp.broadcast_to(mine[None], (16,) + mine.shape), 'space',...  5.8 us
    all_to_all x1, starting transfers between devices, local(): shares = lax.all_to_all(back, 'filt', 0, 0)  5.09 us
    ppermute x2, waiting for transfers between devices, swap_edges(): inner = lax.ppermute(jnp.where(odd, head, tail), 'space', EVEN)  4.51 us
  transfers between devices with their start and end apart: 7, of which 3 were waited for; matrix products, arithmetic and copies ran while one was open for 1% of the time, Pallas kernels for 0%

profile of v2, /device:TPU:64, one launch (start us, length us, event | category | flops | bytes accessed | tf_op | source)
XLA Modules:
  0.0 100.0 jit_solution(18401256124462036918)
XLA Ops:
  0.6 0.8 copy.18
  1.4 0.8 broadcast_in_dim.8
  2.2 0.0 copy-start.1
  2.2 8.5 %all-to-all-start = ((bf16[8,2,8,8,128]{4,3,2,1,0:T(8,128)(2,1)}), bf16[8,2,8,8,128]{4,3,2,1,0:T(8,128)(2,1)S(1)}, u32[]{:S(2)}, u32[]{:S(2)}) async-start(bf16[8,2,8,8,128]{4,3,2,1,0:T(8,128)(2,1)} %broadcast_in_dim.8), calls=%async_computation | async-start | bytes 524288 | tf_op jit(solution)/shard_map/all_to_all | solution.py:171
  10.6 0.0 copy-done.1
  10.7 0.0 copy-start
  10.7 0.8 collective-permute-start.1
  11.5 3.5 %collective-permute-start = (bf16[1,8,16,128]{3,2,1,0:T(8,128)(2,1)S(1)}, bf16[1,8,16,128]{3,2,1,0:T(8,128)(2,1)S(1)}, u32[]{:S(2)}, u32[]{:S(2)}) collective-permute-start(bf16[1,8,16,128]{3,2,1,0:T(8,128)(2,1)S(1)} %get-tuple-element.45), channel_id=1, source_target_pairs={{0,8},{8,0},{16,24},{24,16},{32,40},{40,32},{48,56},{56,48},{64,72... | collective-permute-start | bytes 98312 | tf_op jit(solution)/shard_map/ppermute | solution.py:161
  15.0 0.0 collective-permute-done.1
  15.0 2.3 %collective-permute-done = bf16[1,8,16,128]{3,2,1,0:T(8,128)(2,1)S(1)} collective-permute-done((bf16[1,8,16,128]{3,2,1,0:T(8,128)(2,1)S(1)}, bf16[1,8,16,128]{3,2,1,0:T(8,128)(2,1)S(1)}, u32[]{:S(2)}, u32[]{:S(2)}) %collective-permute-start) | collective-permute-done | bytes 32800 | tf_op jit(solution)/shard_map/ppermute | solution.py:161
  17.3 0.0 all-to-all-done.vol_ref
  17.3 0.0 copy-done
  17.3 1.9 %shard_map.75 = (f32[16,16,128]{2,1,0:T(8,128)S(1)}, f32[8,2,8,8,128]{4,3,2,1,0:T(8,128)}, f32[2,8,16,128]{3,2,1,0:T(8,128)S(1)}, f32[8,16,128]{2,1,0:T(8,128)S(1)}, f32[8,16,128]{2,1,0:T(8,128)S(1)}) custom-call(bf16[8,2,8,8,128]{4,3,2,1,0:T(8,128)(2,1)S(1)} %all-to-all-done.vol_ref, bf16[2,8,16,128]{3,2,1,0:T(8,128)(2,1)S(1)} %bitcast.15, ...), custom_call_target="tpu_custom_call" | custom-call | tf_op jit(solution)/shard_map/pallas_call | solution.py:139
  19.3 19.4 %all_to_all.20 = f32[16,16,128]{2,1,0:T(8,128)S(1)} all-to-all(f32[16,16,128]{2,1,0:T(8,128)S(1)} %get-tuple-element.14), channel_id=1, replica_groups={{0,8,16,24,32,40,48,56,64,72,80,88,96,104,112,120},{128,136,144,152,160..., dimensions={0} | all-to-all | bytes 262144 | tf_op jit(solution)/shard_map/all_to_all | solution.py:175
  38.7 5.1 %all-to-all-start.2 = ((f32[8,2,8,8,128]{4,3,2,1,0:T(8,128)}), f32[8,2,8,8,128]{4,3,2,1,0:T(8,128)S(1)}, u32[]{:S(2)}, u32[]{:S(2)}) async-start(f32[8,2,8,8,128]{4,3,2,1,0:T(8,128)} %get-tuple-element.15), calls=%async_computation.2 | async-start | bytes 1048576 | tf_op jit(solution)/shard_map/all_to_all | solution.py:174
  43.8 0.7 collective-permute-start.3
  44.5 4.6 %collective-permute-start.2 = (f32[8,16,128]{2,1,0:T(8,128)S(1)}, f32[8,16,128]{2,1,0:T(8,128)S(1)}, u32[]{:S(2)}, u32[]{:S(2)}) collective-permute-start(f32[8,16,128]{2,1,0:T(8,128)S(1)} %get-tuple-element.41), channel_id=1, source_target_pairs={{0,8},{8,0},{16,24},{24,16},{32,40},{40,32},{48,56},{56,48},{64,72... | collective-permute-start | bytes 196616 | tf_op jit(solution)/shard_map/ppermute | solution.py:161
  49.1 0.0 collective-permute-done.3
  49.1 2.2 %collective-permute-done.2 = f32[8,16,128]{2,1,0:T(8,128)S(1)} collective-permute-done((f32[8,16,128]{2,1,0:T(8,128)S(1)}, f32[8,16,128]{2,1,0:T(8,128)S(1)}, u32[]{:S(2)}, u32[]{:S(2)}) %collective-permute-start.2) | collective-permute-done | bytes 65568 | tf_op jit(solution)/shard_map/ppermute | solution.py:161
  51.4 27.2 %psum.7 = f32[16,128]{1,0:T(8,128)S(1)} all-reduce(f32[16,128]{1,0:T(8,128)S(1)} %reduce_sum.27), channel_id=1, replica_groups={{0,128,256,384},{8,136,264,392},{16,144,272,400},{24,152,280,408},{32,1..., use_global_device_ids=true, to_apply=%region_1.2 | all-reduce | flops 2048 | bytes 16384 | tf_op jit(solution)/shard_map/psum | solution.py:176
  78.6 0.0 all-to-all-done.2
  78.6 0.7 broadcast_in_dim.22
  79.3 11.2 %all-to-all-start.3 = ((f32[16,16,128]{2,1,0:T(8,128)}), f32[16,16,128]{2,1,0:T(8,128)S(1)}, u32[]{:S(2)}, u32[]{:S(2)}) async-start(f32[16,16,128]{2,1,0:T(8,128)} %broadcast_in_dim.22), calls=%async_computation.3 | async-start | bytes 262144 | tf_op jit(solution)/shard_map/all_to_all | solution.py:180
  90.6 0.0 copy-start.2
  90.6 0.6 copy-done.2
  91.2 0.1 fusion.2
  91.3 0.6 copy.21
  92.0 0.6 copy.22
  92.6 5.8 %all-to-all-done.3 = f32[16,16,128]{2,1,0:T(8,128)S(1)} async-done(((f32[16,16,128]{2,1,0:T(8,128)}), f32[16,16,128]{2,1,0:T(8,128)S(1)}, u32[]{:S(2)}, u32[]{:S(2)}) %all-to-all-start.3) | async-done | bytes 131104 | tf_op jit(solution)/shard_map/all_to_all | solution.py:180
  98.4 0.7 slice_reduce_fusion
  99.1 0.2 reshape.17
  99.3 0.7 slice.18
  (9 shorter events, 0.1 us)
Async XLA Ops:
  2.2 8.5 %copy-start.1 = (bf16[16,2,8,128]{3,2,1,0:T(8,128)(2,1)S(1)}, bf16[16,2,8,128]{3,2,1,0:T(8,128)(2,1)}, u32[]{:S(2)}) copy-start(bf16[16,2,8,128]{3,2,1,0:T(8,128)(2,1)} %param.7) | copy-start | bytes 196612
  2.2 15.2 %all-to-all-start = ((bf16[8,2,8,8,128]{4,3,2,1,0:T(8,128)(2,1)}), bf16[8,2,8,8,128]{4,3,2,1,0:T(8,128)(2,1)S(1)}, u32[]{:S(2)}, u32[]{:S(2)}) async-start(bf16[8,2,8,8,128]{4,3,2,1,0:T(8,128)(2,1)} %broadcast_in_dim.8), calls=%async_computation | async-start | bytes 524288 | tf_op jit(solution)/shard_map/all_to_all | solution.py:171
  10.7 6.7 %copy-start = (bf16[27,64,16]{1,2,0:T(8,128)(2,1)S(1)}, bf16[27,64,16]{1,2,0:T(8,128)(2,1)}, u32[]{:S(2)}) copy-start(bf16[27,64,16]{1,2,0:T(8,128)(2,1)} %param.5) | copy-start | bytes 165892
  10.7 4.3 %collective-permute-start.1 = (bf16[1,8,16,128]{3,2,1,0:T(8,128)(2,1)S(1)}, bf16[1,8,16,128]{3,2,1,0:T(8,128)(2,1)S(1)}, u32[]{:S(2)}, u32[]{:S(2)}) collective-permute-start(bf16[1,8,16,128]{3,2,1,0:T(8,128)(2,1)S(1)} %get-tuple-element.44), channel_id=1, source_target_pairs={{8,16},{16,8},{24,32},{32,24},{40,48},{48,40},{56,64},{64,56},{72,... | collective-permute-start | bytes 98312 | tf_op jit(solution)/shard_map/ppermute | solution.py:162
  11.5 5.8 %collective-permute-start = (bf16[1,8,16,128]{3,2,1,0:T(8,128)(2,1)S(1)}, bf16[1,8,16,128]{3,2,1,0:T(8,128)(2,1)S(1)}, u32[]{:S(2)}, u32[]{:S(2)}) collective-permute-start(bf16[1,8,16,128]{3,2,1,0:T(8,128)(2,1)S(1)} %get-tuple-element.45), channel_id=1, source_target_pairs={{0,8},{8,0},{16,24},{24,16},{32,40},{40,32},{48,56},{56,48},{64,72... | collective-permute-start | bytes 98312 | tf_op jit(solution)/shard_map/ppermute | solution.py:161
  38.7 39.9 %all-to-all-start.2 = ((f32[8,2,8,8,128]{4,3,2,1,0:T(8,128)}), f32[8,2,8,8,128]{4,3,2,1,0:T(8,128)S(1)}, u32[]{:S(2)}, u32[]{:S(2)}) async-start(f32[8,2,8,8,128]{4,3,2,1,0:T(8,128)} %get-tuple-element.15), calls=%async_computation.2 | async-start | bytes 1048576 | tf_op jit(solution)/shard_map/all_to_all | solution.py:174
  43.8 5.3 %collective-permute-start.3 = (f32[8,16,128]{2,1,0:T(8,128)S(1)}, f32[8,16,128]{2,1,0:T(8,128)S(1)}, u32[]{:S(2)}, u32[]{:S(2)}) collective-permute-start(f32[8,16,128]{2,1,0:T(8,128)S(1)} %get-tuple-element.40), channel_id=1, source_target_pairs={{8,16},{16,8},{24,32},{32,24},{40,48},{48,40},{56,64},{64,56},{72,... | collective-permute-start | bytes 196616 | tf_op jit(solution)/shard_map/ppermute | solution.py:162
  44.5 6.9 %collective-permute-start.2 = (f32[8,16,128]{2,1,0:T(8,128)S(1)}, f32[8,16,128]{2,1,0:T(8,128)S(1)}, u32[]{:S(2)}, u32[]{:S(2)}) collective-permute-start(f32[8,16,128]{2,1,0:T(8,128)S(1)} %get-tuple-element.41), channel_id=1, source_target_pairs={{0,8},{8,0},{16,24},{24,16},{32,40},{40,32},{48,56},{56,48},{64,72... | collective-permute-start | bytes 196616 | tf_op jit(solution)/shard_map/ppermute | solution.py:161
  79.3 19.1 %all-to-all-start.3 = ((f32[16,16,128]{2,1,0:T(8,128)}), f32[16,16,128]{2,1,0:T(8,128)S(1)}, u32[]{:S(2)}, u32[]{:S(2)}) async-start(f32[16,16,128]{2,1,0:T(8,128)} %broadcast_in_dim.22), calls=%async_computation.3 | async-start | bytes 262144 | tf_op jit(solution)/shard_map/all_to_all | solution.py:180
  90.6 0.7 copy-start.2

commit v3 on v2

v3 whole, which is shorter than its diff:
```python
import math

import jax
import jax.numpy as jnp
from jax import lax
from jax.experimental import pallas as pl
from jax.experimental.pallas import tpu as pltpu
from jax.sharding import PartitionSpec as P

F32 = jnp.float32
BF16 = jnp.bfloat16
WHOLE = pl.BlockSpec(memory_space=pltpu.VMEM)
PARAMS = pltpu.CompilerParams(vmem_limit_bytes=40 * 1024 * 1024)


def dot(left, right):
    return lax.dot_general(left, right, (((1,), (0,)), ((), ())), preferred_element_type=F32)


def dot_lanes(left, right):
    return lax.dot_general(left, right, (((1,), (1,)), ((), ())), preferred_element_type=F32)


def slide(rows, step):
    size = rows.shape[-1]
    axis = rows.ndim - 1
    turned = pltpu.roll(rows, (-step) % size, axis)
    lane = lax.broadcasted_iota(jnp.int32, rows.shape, axis)
    edge = size - 1 if step > 0 else 0
    return jnp.where(lane == edge, 0.0, turned)


def gradients(vol_ref, grad_ref, before_ref, after_ref, taps_ref, sums_ref, pack_ref, gpad):
    peers, depth, rows, share, cols = vol_ref.shape
    outs = grad_ref.shape[2]
    blank = jnp.zeros((3 * outs, cols), BF16)
    bias_sum = jnp.zeros((outs, cols), F32)
    for p in range(depth + 2):
        gpad[p, 0] = blank
        gpad[p, rows + 1] = blank
        for h in range(rows):
            if p == 0:
                line = before_ref[h, 0:outs]
            elif p == depth + 1:
                line = after_ref[h, 0:outs]
            else:
                line = grad_ref[p - 1, h]
            wide = line.astype(F32)
            if 0 < p < depth + 1:
                bias_sum = bias_sum + wide
            gpad[p, h + 1, 0:outs] = slide(wide, 1).astype(BF16)
            gpad[p, h + 1, outs : 2 * outs] = line
            gpad[p, h + 1, 2 * outs : 3 * outs] = slide(wide, -1).astype(BF16)
    taps = taps_ref[...]
    chans = taps.shape[2]
    behind = taps.reshape(27 * outs, chans).astype(F32).T.astype(BF16)
    acc = jnp.zeros((27 * outs, chans), F32)
    for d in range(depth):
        for h in range(0, rows, 2):
            moved = jnp.concatenate(
                [
                    jnp.concatenate(
                        [gpad[d + 2 - a, h + k + 2 - b] for a in range(3) for b in range(3)], axis=0
                    )
                    for k in range(2)
                ],
                axis=1,
            )
            back = dot(behind, moved)
            for k in range(2):
                for f in range(peers):
                    value = back[share * f : share * (f + 1), k * cols : (k + 1) * cols]
                    high = value.astype(BF16)
                    pack_ref[f, 0, d, h + k] = high
                    pack_ref[f, 1, d, h + k] = (value - high.astype(F32)).astype(BF16)
            cells = jnp.concatenate(
                [
                    jnp.concatenate([vol_ref[s, d, h + k] for s in range(peers)], axis=0)
                    for k in range(2)
                ],
                axis=1,
            )
            acc = acc + dot_lanes(moved, cells)
    for h in range(rows):
        for d, side in enumerate((before_ref, after_ref)):
            line = side[h, outs : outs + share]
            for f in range(peers):
                pack_ref[f, 2, d, h] = line
    half = cols // 2
    bias_half = bias_sum[:, :half] + bias_sum[:, half:]
    for r in range(14):
        first = acc[2 * r * outs : (2 * r + 1) * outs]
        second = bias_half if r == 13 else acc[(2 * r + 1) * outs : (2 * r + 2) * outs]
        sums_ref[r] = jnp.concatenate([first, second], axis=1)
    for r in range(14, 16):
        sums_ref[r] = jnp.zeros((outs, cols), F32)


def finish(vol_ref, pack_ref, taps_ref, bias_ref, out_ref, back_ref, vpad):
    peers, depth, rows, share, cols = vol_ref.shape
    taps = taps_ref[...]
    outs, chans = taps.shape[1:]
    blank = jnp.zeros((chans, cols), BF16)
    for p in range(depth + 2):
        vpad[p, 0] = blank
        vpad[p, rows + 1] = blank
        for h in range(rows):
            if p == 0:
                lines = [pack_ref[s, 2, 0, h] for s in range(peers)]
            elif p == depth + 1:
                lines = [pack_ref[s, 2, 1, h] for s in range(peers)]
            else:
                lines = [vol_ref[s, p - 1, h] for s in range(peers)]
            vpad[p, h + 1] = jnp.concatenate(lines, axis=0)
    ahead = jnp.concatenate(
        [
            jnp.concatenate([taps[9 * a + 3 * b + c] for a in range(3) for b in range(3)], axis=1)
            for c in range(3)
        ],
        axis=0,
    )
    bias = jnp.broadcast_to(bias_ref[...], (outs, cols))
    for d in range(depth):
        lines = []
        for h in range(0, rows, 2):
            stack = jnp.concatenate(
                [
                    vpad[d : d + 3, h + k : h + k + 3].reshape(9 * chans, cols)
                    for k in range(2)
                ],
                axis=1,
            )
            part = dot(ahead, stack)
            for k in range(2):
                total = part[:, k * cols : (k + 1) * cols]
                lines.append(
                    total[outs : 2 * outs]
                    + slide(total[0:outs], -1)
                    + slide(total[2 * outs : 3 * outs], 1)
                    + bias
                )
        block = jnp.stack(lines)
        out_ref[:, d] = jnp.swapaxes(block, 0, 1).astype(BF16)
        lines = []
        for h in range(rows):
            total = None
            for s in range(peers):
                value = pack_ref[s, 0, d, h].astype(F32) + pack_ref[s, 1, d, h].astype(F32)
                total = value if total is None else total + value
            lines.append(total)
        back_ref[:, d] = jnp.swapaxes(jnp.stack(lines), 0, 1).astype(BF16)


def unpack(scale, every_ref, weight_ref, bias_ref):
    outs, cols = every_ref.shape[1:]
    half = cols // 2
    for t in range(27):
        r, side = t // 2, t % 2
        weight_ref[t] = every_ref[r, :, half * side : half * (side + 1)] * scale
    total = jnp.sum(every_ref[13, :, half:] * scale, axis=1, keepdims=True)
    wide = jnp.broadcast_to(total, (outs, cols))
    row = lax.broadcasted_iota(jnp.int32, (outs, cols), 0)
    lane = lax.broadcasted_iota(jnp.int32, (outs, cols), 1)
    flat = jnp.sum(jnp.where(row == lane, wide, 0.0), axis=0, keepdims=True)
    bias_ref[...] = flat[:, :outs]


XY_GROUPS = [[16 * z + k for k in range(16)] for z in range(4)]
Z_GROUPS = [[16 * z + k for z in range(4)] for k in range(16)]
EVEN = [(i, i ^ 1) for i in range(64)]
ODD = [(i, ((i + 1) ^ 1) - 1) for i in range(1, 63)]


def swap_edges(head, tail):
    odd = (lax.axis_index("space") % 2) == 1
    inner = lax.ppermute(jnp.where(odd, head, tail), "space", EVEN)
    outer = lax.ppermute(jnp.where(odd, tail, head), "space", ODD)
    return jnp.where(odd, inner, outer), jnp.where(odd, outer, inner)


def local(volume, weight, bias, grad_out):
    share, depth, rows, cols = volume.shape
    outs = grad_out.shape[0]
    chans = weight.shape[1]
    taps = weight.transpose(0, 2, 1)
    grad = grad_out.transpose(1, 2, 0, 3)
    own = volume.transpose(1, 2, 0, 3)
    both = jnp.concatenate([grad, own], axis=2)
    before, after = swap_edges(both[0], both[depth - 1])
    vol = lax.all_to_all(jnp.broadcast_to(own[None], (8,) + own.shape), "filt", 0, 0)
    sums, pack = pl.pallas_call(
        gradients,
        out_shape=(
            jax.ShapeDtypeStruct((16, outs, cols), F32),
            jax.ShapeDtypeStruct((8, 3, depth, rows, share, cols), BF16),
        ),
        in_specs=[WHOLE] * 5,
        out_specs=(WHOLE,) * 2,
        scratch_shapes=[pltpu.VMEM((depth + 2, rows + 2, 3 * outs, cols), BF16)],
        compiler_params=PARAMS,
    )(vol, grad, before, after, taps)
    parts = lax.all_to_all(sums, "space", 0, 0, axis_index_groups=XY_GROUPS)
    shares = lax.all_to_all(pack, "filt", 0, 0)
    mine = lax.psum(jnp.sum(parts, axis=0), "space", axis_index_groups=Z_GROUPS)
    mine, shares = lax.optimization_barrier((mine, shares))
    every = lax.all_to_all(
        jnp.broadcast_to(mine[None], (16,) + mine.shape), "space", 0, 0, axis_index_groups=XY_GROUPS
    )
    output, grad_volume = pl.pallas_call(
        finish,
        out_shape=(
            jax.ShapeDtypeStruct((outs, depth, rows, cols), BF16),
            jax.ShapeDtypeStruct((share, depth, rows, cols), BF16),
        ),
        in_specs=[WHOLE] * 4,
        out_specs=(WHOLE,) * 2,
        scratch_shapes=[pltpu.VMEM((depth + 2, rows + 2, chans, cols), BF16)],
        compiler_params=PARAMS,
    )(vol, shares, taps, bias[:, None])
    scale = 1.0 / math.sqrt(depth * lax.axis_size("space") * rows * cols)
    grad_taps, grad_bias = pl.pallas_call(
        lambda *refs: unpack(scale, *refs),
        out_shape=(
            jax.ShapeDtypeStruct((27, outs, cols // 2), F32),
            jax.ShapeDtypeStruct((1, outs), F32),
        ),
        in_specs=[WHOLE],
        out_specs=(WHOLE,) * 2,
        compiler_params=PARAMS,
    )(every)
    return (output, grad_volume, grad_taps.transpose(0, 2, 1), grad_bias.reshape(outs))


def solution(mesh):
    in_specs = (
        P("filt", "space", None, None),
        P(None, None, "filt"),
        P("filt"),
        P("filt", "space", None, None),
    )
    out_specs = (
        P("filt", "space", None, None),
        P("filt", "space", None, None),
        P(None, None, "filt"),
        P("filt"),
    )
    return jax.shard_map(local, mesh=mesh, in_specs=in_specs, out_specs=out_specs, check_vma=False)
```

time: 101 us -> 92.3 us (0.914)
  the two profiles are of different devices: /device:TPU:64 before, /device:TPU:32 now
where the time goes in v3:
time: 92.3 us; the launch traced here: 91.7 us
  blocking collectives  54.3 us (59%)
  starting transfers between devices  18.7 us (20%)
  waiting for transfers between devices  10.9 us (12%)
  Pallas kernels  4.02 us (4%)
  local copies, waits for them, and re-layouts  2.96 us (3%)
    psum x1, blocking collectives, local(): mine = lax.psum(jnp.sum(parts, axis=0), 'space', axis_index_groups=Z_GROUPS)  31.9 us
    all_to_all x1, blocking collectives, local(): parts = lax.all_to_all(sums, 'space', 0, 0, axis_index_groups=XY_GROUPS)  22.4 us
    all_to_all x1, starting transfers between devices, local(): lax.all_to_all(jnp.broadcast_to(own[None], (8,) + own.shape), 'filt', 0, 0)  8.93 us
    all_to_all x1, waiting for transfers between devices, local(): lax.all_to_all(jnp.broadcast_to(mine[None], (16,) + mine.shape), 'space',...  5.8 us
    all_to_all x1, starting transfers between devices, local(): lax.all_to_all(jnp.broadcast_to(mine[None], (16,) + mine.shape), 'space',...  3.6 us
    all_to_all x1, starting transfers between devices, local(): shares = lax.all_to_all(pack, 'filt', 0, 0)  3.5 us
    ppermute x1, waiting for transfers between devices, swap_edges(): inner = lax.ppermute(jnp.where(odd, head, tail), 'space', EVEN)  3.38 us
    ppermute x1, starting transfers between devices, swap_edges(): inner = lax.ppermute(jnp.where(odd, head, tail), 'space', EVEN)  2.05 us
  transfers between devices with their start and end apart: 5, of which 3 were waited for; matrix products, arithmetic and copies ran while one was open for 0% of the time, Pallas kernels for 1%

profile of v3, /device:TPU:32, one launch (start us, length us, event | category | flops | bytes accessed | tf_op | source)
XLA Modules:
  0.0 91.7 jit_solution(2883194982460629502)
XLA Ops:
  0.6 0.8 copy.14
  1.4 0.8 broadcast_in_dim.6
  2.2 0.0 copy-start.1
  2.2 8.9 %all-to-all-start = ((bf16[8,2,8,8,128]{4,3,2,1,0:T(8,128)(2,1)}), bf16[8,2,8,8,128]{4,3,2,1,0:T(8,128)(2,1)S(1)}, u32[]{:S(2)}, u32[]{:S(2)}) async-start(bf16[8,2,8,8,128]{4,3,2,1,0:T(8,128)(2,1)} %broadcast_in_dim.6), calls=%async_computation | async-start | bytes 524288 | tf_op jit(solution)/shard_map/all_to_all | solution.py:190
  11.1 0.0 copy-done.1
  11.2 0.0 copy-start
  11.2 2.1 %collective-permute-start = (bf16[8,24,128]{2,1,0:T(8,128)(2,1)S(1)}, bf16[8,24,128]{2,1,0:T(8,128)(2,1)S(1)}, u32[]{:S(2)}, u32[]{:S(2)}) collective-permute-start(bf16[8,24,128]{2,1,0:T(8,128)(2,1)S(1)} %get-tuple-element.23), channel_id=1, source_target_pairs={{0,8},{8,0},{16,24},{24,16},{32,40},{40,32},{48,56},{56,48},{64,72... | collective-permute-start | bytes 147464 | tf_op jit(solution)/shard_map/ppermute | solution.py:176
  13.2 0.7 collective-permute-start.1
  13.9 3.4 %collective-permute-done = bf16[8,24,128]{2,1,0:T(8,128)(2,1)S(1)} collective-permute-done((bf16[8,24,128]{2,1,0:T(8,128)(2,1)S(1)}, bf16[8,24,128]{2,1,0:T(8,128)(2,1)S(1)}, u32[]{:S(2)}, u32[]{:S(2)}) %collective-permute-start) | collective-permute-done | bytes 49184 | tf_op jit(solution)/shard_map/ppermute | solution.py:176
  17.3 0.0 collective-permute-done.1
  17.3 1.7 %all-to-all-done.vol_ref = bf16[8,2,8,8,128]{4,3,2,1,0:T(8,128)(2,1)S(1)} async-done(((bf16[8,2,8,8,128]{4,3,2,1,0:T(8,128)(2,1)}), bf16[8,2,8,8,128]{4,3,2,1,0:T(8,128)(2,1)S(1)}, u32[]{:S(2)}, u32[]{:S(2)}) %all-to-all-start) | async-done | bytes 262176 | tf_op jit(solution)/shard_map/all_to_all | solution.py:190
  19.0 0.0 copy-done
  19.0 1.9 %shard_map.75 = (f32[16,16,128]{2,1,0:T(8,128)S(1)}, bf16[8,3,2,8,8,128]{5,4,3,2,1,0:T(8,128)(2,1)}) custom-call(bf16[8,2,8,8,128]{4,3,2,1,0:T(8,128)(2,1)S(1)} %all-to-all-done.vol_ref, bf16[2,8,16,128]{3,2,1,0:T(8,128)(2,1)S(1)} %bitcast.15, bf16[8,24,128]{2,1,0:T(8,128)(2,1)S(1)} %get-tuple-element.21.before_ref, ...), custom_call_target="tpu_custom_call" | custom-call | tf_op jit(solution)/shard_map/pallas_call | solution.py:191
  20.9 22.4 %all_to_all.20 = f32[16,16,128]{2,1,0:T(8,128)S(1)} all-to-all(f32[16,16,128]{2,1,0:T(8,128)S(1)} %get-tuple-element.12), channel_id=1, replica_groups={{0,8,16,24,32,40,48,56,64,72,80,88,96,104,112,120},{128,136,144,152,160..., dimensions={0} | all-to-all | bytes 262144 | tf_op jit(solution)/shard_map/all_to_all | solution.py:202
  43.3 3.5 %all-to-all-start.2 = ((bf16[8,3,2,8,8,128]{5,4,3,2,1,0:T(8,128)(2,1)}), bf16[8,3,2,8,8,128]{5,4,3,2,1,0:T(8,128)(2,1)S(1)}, u32[]{:S(2)}, u32[]{:S(2)}) async-start(bf16[8,3,2,8,8,128]{5,4,3,2,1,0:T(8,128)(2,1)} %get-tuple-element.13), calls=%async_computation.2 | async-start | bytes 1572864 | tf_op jit(solution)/shard_map/all_to_all | solution.py:203
  46.9 31.9 %psum.7 = f32[16,128]{1,0:T(8,128)S(1)} all-reduce(f32[16,128]{1,0:T(8,128)S(1)} %reduce_sum.9), channel_id=1, replica_groups={{0,128,256,384},{8,136,264,392},{16,144,272,400},{24,152,280,408},{32,1..., use_global_device_ids=true, to_apply=%region_1.2 | all-reduce | flops 2048 | bytes 16384 | tf_op jit(solution)/shard_map/psum | solution.py:204
  78.7 0.0 all-to-all-done.2.pack_ref
  78.8 0.7 broadcast_in_dim.8
  79.4 3.6 %all-to-all-start.3 = ((f32[16,16,128]{2,1,0:T(8,128)}), f32[16,16,128]{2,1,0:T(8,128)S(1)}, u32[]{:S(2)}, u32[]{:S(2)}) async-start(f32[16,16,128]{2,1,0:T(8,128)} %broadcast_in_dim.8), calls=%async_computation.3 | async-start | bytes 262144 | tf_op jit(solution)/shard_map/all_to_all | solution.py:206
  83.0 0.0 copy-start.2
  83.0 0.6 copy-done.2
  83.7 0.1 copy.10.bias_ref
  83.8 1.3 %shard_map.76 = (bf16[16,2,8,128]{3,2,1,0:T(8,128)(2,1)}, bf16[8,2,8,128]{3,2,1,0:T(8,128)(2,1)}) custom-call(bf16[8,2,8,8,128]{4,3,2,1,0:T(8,128)(2,1)S(1)} %all-to-all-done.vol_ref, bf16[8,3,2,8,8,128]{5,4,3,2,1,0:T(8,128)(2,1)S(1)} %all-to-all-done.2.pack_ref, bf16[27,16,64]{2,1,0:T(8,128)(2,1)S(1)} %bitcast.17, f32[16,1]{1,0:T(8,128)S(1)} %copy.10.bias_ref), custom_call_target="tpu_custom_call" | custom-call | tf_op jit(solution)/shard_map/pallas_call | solution.py:209
  85.1 5.8 %all-to-all-done.3.refs_0_ = f32[16,16,128]{2,1,0:T(8,128)S(1)} async-done(((f32[16,16,128]{2,1,0:T(8,128)}), f32[16,16,128]{2,1,0:T(8,128)S(1)}, u32[]{:S(2)}, u32[]{:S(2)}) %all-to-all-start.3) | async-done | bytes 131104 | tf_op jit(solution)/shard_map/all_to_all | solution.py:206
  90.9 0.8 shard_map.77
  (4 shorter events, 0.1 us)
Async XLA Ops:
  2.2 8.9 %copy-start.1 = (bf16[16,2,8,128]{3,2,1,0:T(8,128)(2,1)S(1)}, bf16[16,2,8,128]{3,2,1,0:T(8,128)(2,1)}, u32[]{:S(2)}) copy-start(bf16[16,2,8,128]{3,2,1,0:T(8,128)(2,1)} %param.7) | copy-start | bytes 196612
  2.2 16.8 %all-to-all-start = ((bf16[8,2,8,8,128]{4,3,2,1,0:T(8,128)(2,1)}), bf16[8,2,8,8,128]{4,3,2,1,0:T(8,128)(2,1)S(1)}, u32[]{:S(2)}, u32[]{:S(2)}) async-start(bf16[8,2,8,8,128]{4,3,2,1,0:T(8,128)(2,1)} %broadcast_in_dim.6), calls=%async_computation | async-start | bytes 524288 | tf_op jit(solution)/shard_map/all_to_all | solution.py:190
  11.2 7.9 %copy-start = (bf16[27,64,16]{1,2,0:T(8,128)(2,1)S(1)}, bf16[27,64,16]{1,2,0:T(8,128)(2,1)}, u32[]{:S(2)}) copy-start(bf16[27,64,16]{1,2,0:T(8,128)(2,1)} %param.5) | copy-start | bytes 165892
  11.2 6.1 %collective-permute-start = (bf16[8,24,128]{2,1,0:T(8,128)(2,1)S(1)}, bf16[8,24,128]{2,1,0:T(8,128)(2,1)S(1)}, u32[]{:S(2)}, u32[]{:S(2)}) collective-permute-start(bf16[8,24,128]{2,1,0:T(8,128)(2,1)S(1)} %get-tuple-element.23), channel_id=1, source_target_pairs={{0,8},{8,0},{16,24},{24,16},{32,40},{40,32},{48,56},{56,48},{64,72... | collective-permute-start | bytes 147464 | tf_op jit(solution)/shard_map/ppermute | solution.py:176
  13.2 4.1 %collective-permute-start.1 = (bf16[8,24,128]{2,1,0:T(8,128)(2,1)S(1)}, bf16[8,24,128]{2,1,0:T(8,128)(2,1)S(1)}, u32[]{:S(2)}, u32[]{:S(2)}) collective-permute-start(bf16[8,24,128]{2,1,0:T(8,128)(2,1)S(1)} %get-tuple-element.22), channel_id=1, source_target_pairs={{8,16},{16,8},{24,32},{32,24},{40,48},{48,40},{56,64},{64,56},{72,... | collective-permute-start | bytes 147464 | tf_op jit(solution)/shard_map/ppermute | solution.py:177
  43.3 35.4 %all-to-all-start.2 = ((bf16[8,3,2,8,8,128]{5,4,3,2,1,0:T(8,128)(2,1)}), bf16[8,3,2,8,8,128]{5,4,3,2,1,0:T(8,128)(2,1)S(1)}, u32[]{:S(2)}, u32[]{:S(2)}) async-start(bf16[8,3,2,8,8,128]{5,4,3,2,1,0:T(8,128)(2,1)} %get-tuple-element.13), calls=%async_computation.2 | async-start | bytes 1572864 | tf_op jit(solution)/shard_map/all_to_all | solution.py:203
  79.4 11.4 %all-to-all-start.3 = ((f32[16,16,128]{2,1,0:T(8,128)}), f32[16,16,128]{2,1,0:T(8,128)S(1)}, u32[]{:S(2)}, u32[]{:S(2)}) async-start(f32[16,16,128]{2,1,0:T(8,128)} %broadcast_in_dim.8), calls=%async_computation.3 | async-start | bytes 262144 | tf_op jit(solution)/shard_map/all_to_all | solution.py:206
  83.0 0.7 copy-start.2

commit v4 on v3

--- a/solution.py
+++ b/solution.py
@@ -30,9 +30,10 @@
     return jnp.where(lane == edge, 0.0, turned)
 
 
-def gradients(vol_ref, grad_ref, before_ref, after_ref, taps_ref, sums_ref, pack_ref, gpad):
+def weight_sums(vol_ref, grad_ref, before_ref, after_ref, sums_ref, gpad):
     peers, depth, rows, share, cols = vol_ref.shape
     outs = grad_ref.shape[2]
+    chans = peers * share
     blank = jnp.zeros((3 * outs, cols), BF16)
     bias_sum = jnp.zeros((outs, cols), F32)
     for p in range(depth + 2):
@@ -51,28 +52,9 @@
             gpad[p, h + 1, 0:outs] = slide(wide, 1).astype(BF16)
             gpad[p, h + 1, outs : 2 * outs] = line
             gpad[p, h + 1, 2 * outs : 3 * outs] = slide(wide, -1).astype(BF16)
-    taps = taps_ref[...]
-    chans = taps.shape[2]
-    behind = taps.reshape(27 * outs, chans).astype(F32).T.astype(BF16)
     acc = jnp.zeros((27 * outs, chans), F32)
     for d in range(depth):
         for h in range(0, rows, 2):
-            moved = jnp.concatenate(
-                [
-                    jnp.concatenate(
-                        [gpad[d + 2 - a, h + k + 2 - b] for a in range(3) for b in range(3)], axis=0
-                    )
-                    for k in range(2)
-                ],
-                axis=1,
-            )
-            back = dot(behind, moved)
-            for k in range(2):
-                for f in range(peers):
-                    value = back[share * f : share * (f + 1), k * cols : (k + 1) * cols]
-                    high = value.astype(BF16)
-                    pack_ref[f, 0, d, h + k] = high
-                    pack_ref[f, 1, d, h + k] = (value - high.astype(F32)).astype(BF16)
             cells = jnp.concatenate(
                 [
                     jnp.concatenate([vol_ref[s, d, h + k] for s in range(peers)], axis=0)
@@ -80,12 +62,7 @@
                 ],
                 axis=1,
             )
-            acc = acc + dot_lanes(moved, cells)
-    for h in range(rows):
-        for d, side in enumerate((before_ref, after_ref)):
-            line = side[h, outs : outs + share]
-            for f in range(peers):
-                pack_ref[f, 2, d, h] = line
+            acc = acc + dot_lanes(moved_rows(gpad, d, h), cells)
     half = cols // 2
     bias_half = bias_sum[:, :half] + bias_sum[:, half:]
     for r in range(14):
@@ -96,19 +73,91 @@
         sums_ref[r] = jnp.zeros((outs, cols), F32)
 
 
-def finish(vol_ref, pack_ref, taps_ref, bias_ref, out_ref, back_ref, vpad):
+def moved_rows(gpad, d, h):
+    return jnp.concatenate(
+        [
+            jnp.concatenate(
+                [gpad[d + 2 - a, h + k + 2 - b] for a in range(3) for b in range(3)], axis=0
+            )
+            for k in range(2)
+        ],
+        axis=1,
+    )
+
+
+def split(value):
+    high = value.astype(BF16)
+    return high, (value - high.astype(F32)).astype(BF16)
+
+
+def shares_first(
+    me_ref, moved_ref, taps_ref, before_ref, after_ref, keep_ref, send_ref, turned
+):
+    _, depth, rows, share, cols = keep_ref.shape
+    outs, chans = taps_ref.shape[1:]
+    turned[...] = taps_ref[...].reshape(27 * outs, chans).astype(F32).T
+    me = me_ref[0]
+    behind = jnp.concatenate(
+        [
+            turned[pl.ds(pl.multiple_of(share * jnp.bitwise_xor(me, r), share), share)]
+            for r in range(8)
+        ],
+        axis=0,
+    ).astype(BF16)
+    for d in range(depth):
+        for h in range(0, rows, 2):
+            back = dot(behind, moved_rows(moved_ref, d, h))
+            for k in range(2):
+                for r in range(8):
+                    value = back[share * r : share * (r + 1), k * cols : (k + 1) * cols]
+                    if r < 4:
+                        keep_ref[r, d, h + k] = value
+                    else:
+                        high, low = split(value)
+                        send_ref[2 * (r - 4), d, h + k] = high
+                        send_ref[2 * (r - 4) + 1, d, h + k] = low
+    for h in range(rows):
+        send_ref[8, 0, h] = before_ref[h, outs : outs + share]
+        send_ref[8, 1, h] = after_ref[h, outs : outs + share]
+
+
+def shares_next(keep_ref, sent_ref, got_ref, kept_ref, send_ref):
+    blocks = keep_ref.shape[0]
+    half = blocks // 2
+    for r in range(blocks):
+        value = keep_ref[r] + got_ref[2 * r].astype(F32) + got_ref[2 * r + 1].astype(F32)
+        if r < half:
+            kept_ref[r] = value
+        else:
+            high, low = split(value)
+            send_ref[2 * (r - half)] = high
+            send_ref[2 * (r - half) + 1] = low
+    place = 2 * half
+    for ref in (sent_ref, got_ref):
+        for n in range(2 * blocks, ref.shape[0]):
+            send_ref[place] = ref[n]
+            place += 1
+
+
+def finish(
+    me_ref, vol_ref, keep_ref, sent_ref, got_ref, taps_ref, bias_ref, out_ref, back_ref, halo, vpad
+):
     peers, depth, rows, share, cols = vol_ref.shape
     taps = taps_ref[...]
     outs, chans = taps.shape[1:]
+    me = me_ref[0]
+    for place, r in enumerate((0, 4, 2, 6)):
+        halo[jnp.bitwise_xor(me, r)] = sent_ref[2 + place]
+        halo[jnp.bitwise_xor(me, r + 1)] = got_ref[2 + place]
     blank = jnp.zeros((chans, cols), BF16)
     for p in range(depth + 2):
         vpad[p, 0] = blank
         vpad[p, rows + 1] = blank
         for h in range(rows):
             if p == 0:
-                lines = [pack_ref[s, 2, 0, h] for s in range(peers)]
+                lines = [halo[s, 0, h] for s in range(peers)]
             elif p == depth + 1:
-                lines = [pack_ref[s, 2, 1, h] for s in range(peers)]
+                lines = [halo[s, 1, h] for s in range(peers)]
             else:
                 lines = [vol_ref[s, p - 1, h] for s in range(peers)]
             vpad[p, h + 1] = jnp.concatenate(lines, axis=0)
@@ -139,16 +188,9 @@
                     + slide(total[2 * outs : 3 * outs], 1)
                     + bias
                 )
-        block = jnp.stack(lines)
-        out_ref[:, d] = jnp.swapaxes(block, 0, 1).astype(BF16)
-        lines = []
-        for h in range(rows):
-            total = None
-            for s in range(peers):
-                value = pack_ref[s, 0, d, h].astype(F32) + pack_ref[s, 1, d, h].astype(F32)
-                total = value if total is None else total + value
-            lines.append(total)
-        back_ref[:, d] = jnp.swapaxes(jnp.stack(lines), 0, 1).astype(BF16)
+        out_ref[:, d] = jnp.swapaxes(jnp.stack(lines), 0, 1).astype(BF16)
+        total = keep_ref[0, d] + got_ref[0, d].astype(F32) + got_ref[1, d].astype(F32)
+        back_ref[:, d] = jnp.swapaxes(total, 0, 1).astype(BF16)
 
 
 def unpack(scale, every_ref, weight_ref, bias_ref):
@@ -178,6 +220,23 @@
     return jnp.where(odd, inner, outer), jnp.where(odd, outer, inner)
 
 
+def swap_pairs(bit):
+    return [(f, f ^ bit) for f in range(8)]
+
+
+def shares_step(blocks, block):
+    return pl.pallas_call(
+        shares_next,
+        out_shape=(
+            jax.ShapeDtypeStruct((blocks,) + block, F32),
+            jax.ShapeDtypeStruct((6,) + block, BF16),
+        ),
+        in_specs=[WHOLE] * 3,
+        out_specs=(WHOLE,) * 2,
+        compiler_params=PARAMS,
+    )
+
+
 def local(volume, weight, bias, grad_out):
     share, depth, rows, cols = volume.shape
     outs = grad_out.shape[0]
@@ -185,24 +244,42 @@
     taps = weight.transpose(0, 2, 1)
     grad = grad_out.transpose(1, 2, 0, 3)
     own = volume.transpose(1, 2, 0, 3)
+    me = lax.axis_index("filt").astype(jnp.int32).reshape(1)
     both = jnp.concatenate([grad, own], axis=2)
     before, after = swap_edges(both[0], both[depth - 1])
     vol = lax.all_to_all(jnp.broadcast_to(own[None], (8,) + own.shape), "filt", 0, 0)
-    sums, pack = pl.pallas_call(
-        gradients,
+    block = (depth, rows, share, cols)
+    sums, moved = pl.pallas_call(
+        weight_sums,
         out_shape=(
             jax.ShapeDtypeStruct((16, outs, cols), F32),
-            jax.ShapeDtypeStruct((8, 3, depth, rows, share, cols), BF16),
-        ),
-        in_specs=[WHOLE] * 5,
-        out_specs=(WHOLE,) * 2,
-        scratch_shapes=[pltpu.VMEM((depth + 2, rows + 2, 3 * outs, cols), BF16)],
-        compiler_params=PARAMS,
-    )(vol, grad, before, after, taps)
+            jax.ShapeDtypeStruct((depth + 2, rows + 2, 3 * outs, cols), BF16),
+        ),
+        in_specs=[WHOLE] * 4,
+        out_specs=(WHOLE,) * 2,
+        compiler_params=PARAMS,
+    )(vol, grad, before, after)
     parts = lax.all_to_all(sums, "space", 0, 0, axis_index_groups=XY_GROUPS)
-    shares = lax.all_to_all(pack, "filt", 0, 0)
-    mine = lax.psum(jnp.sum(parts, axis=0), "space", axis_index_groups=Z_GROUPS)
-    mine, shares = lax.optimization_barrier((mine, shares))
+    keep, send = pl.pallas_call(
+        shares_first,
+        out_shape=(
+            jax.ShapeDtypeStruct((4,) + block, F32),
+            jax.ShapeDtypeStruct((9,) + block, BF16),
+        ),
+        in_specs=[pl.BlockSpec(memory_space=pltpu.SMEM)] + [WHOLE] * 4,
+        out_specs=(WHOLE,) * 2,
+        scratch_shapes=[pltpu.VMEM((chans, 27 * outs), F32)],
+        compiler_params=PARAMS,
+    )(me, moved, taps, before, after)
+    got = lax.ppermute(send, "filt", swap_pairs(4))
+    mine = jnp.sum(parts, axis=0)
+    mine, got = lax.optimization_barrier((mine, got))
+    keep, send = shares_step(2, block)(keep, send, got)
+    got = lax.ppermute(send, "filt", swap_pairs(2))
+    mine = lax.psum(mine, "space", axis_index_groups=Z_GROUPS)
+    mine, got = lax.optimization_barrier((mine, got))
+    keep, send = shares_step(1, block)(keep, send, got)
+    got = lax.ppermute(send, "filt", swap_pairs(1))
     every = lax.all_to_all(
         jnp.broadcast_to(mine[None], (16,) + mine.shape), "space", 0, 0, axis_index_groups=XY_GROUPS
     )
@@ -212,11 +289,15 @@
             jax.ShapeDtypeStruct((outs, depth, rows, cols), BF16),
             jax.ShapeDtypeStruct((share, depth, rows, cols), BF16),
         ),
-        in_specs=[WHOLE] * 4,
-        out_specs=(WHOLE,) * 2,
-        scratch_shapes=[pltpu.VMEM((depth + 2, rows + 2, chans, cols), BF16)],
-        compiler_params=PARAMS,
-    )(vol, shares, taps, bias[:, None])
+        in_specs=[pl.BlockSpec(memory_space=pltpu.SMEM)] + [WHOLE] * 6,
+        out_specs=(WHOLE,) * 2,
+        scratch_shapes=[
+            pltpu.VMEM((8,) + block, BF16),
+            pltpu.VMEM((depth + 2, rows + 2, chans, cols), BF16),
+        ],
+        compiler_params=PARAMS,
+    )(me, vol, keep, send, got, taps, bias[:, None])
+    every, output, grad_volume = lax.optimization_barrier((every, output, grad_volume))
     scale = 1.0 / math.sqrt(depth * lax.axis_size("space") * rows * cols)
     grad_taps, grad_bias = pl.pallas_call(
         lambda *refs: unpack(scale, *refs),

time: 92.3 us -> 81.6 us (0.88)
  the two profiles are of different devices: /device:TPU:32 before, /device:TPU:1 now
where the time goes in v4:
time: 81.6 us; the launch traced here: 81 us
  blocking collectives  37.5 us (46%)
  starting transfers between devices  26.5 us (32%)
  waiting for transfers between devices  9.66 us (12%)
  Pallas kernels  3.51 us (4%)
  local copies, waits for them, and re-layouts  3.1 us (4%)
    all_to_all x1, blocking collectives, local(): parts = lax.all_to_all(sums, 'space', 0, 0, axis_index_groups=XY_GROUPS)  19 us
    psum x1, blocking collectives, local(): mine = lax.psum(mine, 'space', axis_index_groups=Z_GROUPS)  18.5 us
    all_to_all x1, starting transfers between devices, local(): lax.all_to_all(jnp.broadcast_to(own[None], (8,) + own.shape), 'filt', 0, 0)  10.3 us
    ppermute x1, starting transfers between devices, local(): got = lax.ppermute(send, 'filt', swap_pairs(1))  5.17 us
    all_to_all x1, waiting for transfers between devices, local(): lax.all_to_all(jnp.broadcast_to(mine[None], (16,) + mine.shape), 'space',...  4.65 us
    all_to_all x1, starting transfers between devices, local(): lax.all_to_all(jnp.broadcast_to(mine[None], (16,) + mine.shape), 'space',...  3.51 us
    all_to_all x1, waiting for transfers between devices, local(): lax.all_to_all(jnp.broadcast_to(own[None], (8,) + own.shape), 'filt', 0, 0)  3.14 us
    ppermute x1, starting transfers between devices, swap_edges(): inner = lax.ppermute(jnp.where(odd, head, tail), 'space', EVEN)  2.96 us
  transfers between devices with their start and end apart: 7, of which 3 were waited for; matrix products, arithmetic and copies ran while one was open for 1% of the time, Pallas kernels for 2%

profile of v4, /device:TPU:1, one launch (start us, length us, event | category | flops | bytes accessed | tf_op | source)
XLA Modules:
  0.0 81.0 jit_solution(370309433487552898)
XLA Ops:
  0.6 0.8 copy.14
  1.4 0.8 broadcast_in_dim.6
  2.2 0.0 copy-start.1
  2.2 10.3 %all-to-all-start = ((bf16[8,2,8,8,128]{4,3,2,1,0:T(8,128)(2,1)}), bf16[8,2,8,8,128]{4,3,2,1,0:T(8,128)(2,1)S(1)}, u32[]{:S(2)}, u32[]{:S(2)}) async-start(bf16[8,2,8,8,128]{4,3,2,1,0:T(8,128)(2,1)} %broadcast_in_dim.6), calls=%async_computation | async-start | bytes 524288 | tf_op jit(solution)/shard_map/all_to_all | solution.py:250
  12.5 0.0 copy-done.1
  12.6 0.7 collective-permute-start.1
  13.2 3.0 %collective-permute-start = (bf16[8,24,128]{2,1,0:T(8,128)(2,1)S(1)}, bf16[8,24,128]{2,1,0:T(8,128)(2,1)S(1)}, u32[]{:S(2)}, u32[]{:S(2)}) collective-permute-start(bf16[8,24,128]{2,1,0:T(8,128)(2,1)S(1)} %get-tuple-element.45), channel_id=1, source_target_pairs={{0,8},{8,0},{16,24},{24,16},{32,40},{40,32},{48,56},{56,48},{64,72... | collective-permute-start | bytes 147464 | tf_op jit(solution)/shard_map/ppermute | solution.py:218
  16.2 0.0 collective-permute-done.1
  16.2 1.9 %collective-permute-done = bf16[8,24,128]{2,1,0:T(8,128)(2,1)S(1)} collective-permute-done((bf16[8,24,128]{2,1,0:T(8,128)(2,1)S(1)}, bf16[8,24,128]{2,1,0:T(8,128)(2,1)S(1)}, u32[]{:S(2)}, u32[]{:S(2)}) %collective-permute-start) | collective-permute-done | bytes 49184 | tf_op jit(solution)/shard_map/ppermute | solution.py:218
  18.1 3.1 %all-to-all-done.vol_ref = bf16[8,2,8,8,128]{4,3,2,1,0:T(8,128)(2,1)S(1)} async-done(((bf16[8,2,8,8,128]{4,3,2,1,0:T(8,128)(2,1)}), bf16[8,2,8,8,128]{4,3,2,1,0:T(8,128)(2,1)S(1)}, u32[]{:S(2)}, u32[]{:S(2)}) %all-to-all-start) | async-done | bytes 262176 | tf_op jit(solution)/shard_map/all_to_all | solution.py:250
  21.2 0.0 copy-start
  21.2 0.7 shard_map.75
  22.0 0.2 copy-done
  22.1 0.5 shard_map.76
  22.6 1.9 %collective-permute-start.2 = (bf16[9,2,8,8,128]{4,3,2,1,0:T(8,128)(2,1)S(1)}, bf16[9,2,8,8,128]{4,3,2,1,0:T(8,128)(2,1)S(1)}, u32[]{:S(2)}, u32[]{:S(2)}) collective-permute-start(bf16[9,2,8,8,128]{4,3,2,1,0:T(8,128)(2,1)S(1)} %get-tuple-element.25.sent_ref), channel_id=1, source_target_pairs={{0,4},{1,5},{2,6},{3,7},{4,0},{5,1},{6,2},{7,3},{8,12},{9,13},{10,... | collective-permute-start | bytes 884744 | tf_op jit(solution)/shard_map/ppermute | solution.py:274
  24.6 19.0 %all_to_all.15 = f32[16,16,128]{2,1,0:T(8,128)S(1)} all-to-all(f32[16,16,128]{2,1,0:T(8,128)S(1)} %get-tuple-element.23), channel_id=1, replica_groups={{0,8,16,24,32,40,48,56,64,72,80,88,96,104,112,120},{128,136,144,152,160..., dimensions={0} | all-to-all | bytes 262144 | tf_op jit(solution)/shard_map/all_to_all | solution.py:262
  43.5 0.0 collective-permute-done.2.got_ref
  43.5 0.1 shard_map.77
  43.6 1.9 %collective-permute-start.3 = (bf16[6,2,8,8,128]{4,3,2,1,0:T(8,128)(2,1)S(1)}, bf16[6,2,8,8,128]{4,3,2,1,0:T(8,128)(2,1)S(1)}, u32[]{:S(2)}, u32[]{:S(2)}) collective-permute-start(bf16[6,2,8,8,128]{4,3,2,1,0:T(8,128)(2,1)S(1)} %get-tuple-element.29.sent_ref), channel_id=1, source_target_pairs={{0,2},{1,3},{2,0},{3,1},{4,6},{5,7},{6,4},{7,5},{8,10},{9,11},{10,... | collective-permute-start | bytes 589832 | tf_op jit(solution)/shard_map/ppermute | solution.py:278
  45.5 18.5 %psum.7 = f32[16,128]{1,0:T(8,128)S(1)} all-reduce(f32[16,128]{1,0:T(8,128)S(1)} %reduce_sum.9), channel_id=1, replica_groups={{0,128,256,384},{8,136,264,392},{16,144,272,400},{24,152,280,408},{32,1..., use_global_device_ids=true, to_apply=%region_1.2 | all-reduce | flops 2048 | bytes 16384 | tf_op jit(solution)/shard_map/psum | solution.py:279
  64.1 0.0 collective-permute-done.3.got_ref
  64.1 5.2 %collective-permute-start.4 = (bf16[6,2,8,8,128]{4,3,2,1,0:T(8,128)(2,1)S(1)}, bf16[6,2,8,8,128]{4,3,2,1,0:T(8,128)(2,1)S(1)}, u32[]{:S(2)}, u32[]{:S(2)}) collective-permute-start(bf16[6,2,8,8,128]{4,3,2,1,0:T(8,128)(2,1)S(1)} %get-tuple-element.34.sent_ref), channel_id=1, source_target_pairs={{0,1},{1,0},{2,3},{3,2},{4,5},{5,4},{6,7},{7,6},{8,9},{9,8},{10,11... | collective-permute-start | bytes 589832 | tf_op jit(solution)/shard_map/ppermute | solution.py:282
  69.3 0.7 broadcast_in_dim.7
  69.9 3.5 %all-to-all-start.2 = ((f32[16,16,128]{2,1,0:T(8,128)}), f32[16,16,128]{2,1,0:T(8,128)S(1)}, u32[]{:S(2)}, u32[]{:S(2)}) async-start(f32[16,16,128]{2,1,0:T(8,128)} %broadcast_in_dim.7), calls=%async_computation.2 | async-start | bytes 262144 | tf_op jit(solution)/shard_map/all_to_all | solution.py:283
  73.5 0.0 copy-start.2
  73.5 0.6 copy-done.2
  74.1 0.1 copy.10.bias_ref
  74.2 0.0 collective-permute-done.4.got_ref
  74.2 1.3 %shard_map.79 = (bf16[16,2,8,128]{3,2,1,0:T(8,128)(2,1)}, bf16[8,2,8,128]{3,2,1,0:T(8,128)(2,1)}) custom-call(s32[1]{0:T(128)} %bitcast.4.me_ref, bf16[8,2,8,8,128]{4,3,2,1,0:T(8,128)(2,1)S(1)} %all-to-all-done.vol_ref, f32[1,2,8,8,128]{4,3,2,1,0:T(8,128)S(1)} %get-tuple-element.33.keep_ref, bf16[6,2,8,8,128]{4,3,2,1,0:T(8,128)(2,1)S(1)} %get-tuple-element.34.sent_ref, ...), custom_call_target="tpu_custom_call" | custom-call | tf_op jit(solution)/shard_map/pallas_call | solution.py:286
  75.5 4.7 %all-to-all-done.2.refs_0_ = f32[16,16,128]{2,1,0:T(8,128)S(1)} async-done(((f32[16,16,128]{2,1,0:T(8,128)}), f32[16,16,128]{2,1,0:T(8,128)S(1)}, u32[]{:S(2)}, u32[]{:S(2)}) %all-to-all-start.2) | async-done | bytes 131104 | tf_op jit(solution)/shard_map/all_to_all | solution.py:283
  80.2 0.8 %shard_map.80 = (f32[27,16,64]{2,1,0:T(8,128)}, f32[1,16]{1,0:T(1,128)}) custom-call(f32[16,16,128]{2,1,0:T(8,128)S(1)} %all-to-all-done.2.refs_0_), custom_call_target="tpu_custom_call" | custom-call | tf_op jit(solution)/shard_map/pallas_call | solution.py:302
  (5 shorter events, 0.1 us)
Async XLA Ops:
  2.2 10.3 %copy-start.1 = (bf16[16,2,8,128]{3,2,1,0:T(8,128)(2,1)S(1)}, bf16[16,2,8,128]{3,2,1,0:T(8,128)(2,1)}, u32[]{:S(2)}) copy-start(bf16[16,2,8,128]{3,2,1,0:T(8,128)(2,1)} %param.7) | copy-start | bytes 196612
  2.2 19.0 %all-to-all-start = ((bf16[8,2,8,8,128]{4,3,2,1,0:T(8,128)(2,1)}), bf16[8,2,8,8,128]{4,3,2,1,0:T(8,128)(2,1)S(1)}, u32[]{:S(2)}, u32[]{:S(2)}) async-start(bf16[8,2,8,8,128]{4,3,2,1,0:T(8,128)(2,1)} %broadcast_in_dim.6), calls=%async_computation | async-start | bytes 524288 | tf_op jit(solution)/shard_map/all_to_all | solution.py:250
  12.6 3.6 %collective-permute-start.1 = (bf16[8,24,128]{2,1,0:T(8,128)(2,1)S(1)}, bf16[8,24,128]{2,1,0:T(8,128)(2,1)S(1)}, u32[]{:S(2)}, u32[]{:S(2)}) collective-permute-start(bf16[8,24,128]{2,1,0:T(8,128)(2,1)S(1)} %get-tuple-element.44), channel_id=1, source_target_pairs={{8,16},{16,8},{24,32},{32,24},{40,48},{48,40},{56,64},{64,56},{72,... | collective-permute-start | bytes 147464 | tf_op jit(solution)/shard_map/ppermute | solution.py:219
  13.2 4.8 %collective-permute-start = (bf16[8,24,128]{2,1,0:T(8,128)(2,1)S(1)}, bf16[8,24,128]{2,1,0:T(8,128)(2,1)S(1)}, u32[]{:S(2)}, u32[]{:S(2)}) collective-permute-start(bf16[8,24,128]{2,1,0:T(8,128)(2,1)S(1)} %get-tuple-element.45), channel_id=1, source_target_pairs={{0,8},{8,0},{16,24},{24,16},{32,40},{40,32},{48,56},{56,48},{64,72... | collective-permute-start | bytes 147464 | tf_op jit(solution)/shard_map/ppermute | solution.py:218
  21.2 0.9 %copy-start = (bf16[27,64,16]{1,2,0:T(8,128)(2,1)S(1)}, bf16[27,64,16]{1,2,0:T(8,128)(2,1)}, u32[]{:S(2)}) copy-start(bf16[27,64,16]{1,2,0:T(8,128)(2,1)} %param.5) | copy-start | bytes 165892
  22.6 20.9 %collective-permute-start.2 = (bf16[9,2,8,8,128]{4,3,2,1,0:T(8,128)(2,1)S(1)}, bf16[9,2,8,8,128]{4,3,2,1,0:T(8,128)(2,1)S(1)}, u32[]{:S(2)}, u32[]{:S(2)}) collective-permute-start(bf16[9,2,8,8,128]{4,3,2,1,0:T(8,128)(2,1)S(1)} %get-tuple-element.25.sent_ref), channel_id=1, source_target_pairs={{0,4},{1,5},{2,6},{3,7},{4,0},{5,1},{6,2},{7,3},{8,12},{9,13},{10,... | collective-permute-start | bytes 884744 | tf_op jit(solution)/shard_map/ppermute | solution.py:274
  43.6 20.4 %collective-permute-start.3 = (bf16[6,2,8,8,128]{4,3,2,1,0:T(8,128)(2,1)S(1)}, bf16[6,2,8,8,128]{4,3,2,1,0:T(8,128)(2,1)S(1)}, u32[]{:S(2)}, u32[]{:S(2)}) collective-permute-start(bf16[6,2,8,8,128]{4,3,2,1,0:T(8,128)(2,1)S(1)} %get-tuple-element.29.sent_ref), channel_id=1, source_target_pairs={{0,2},{1,3},{2,0},{3,1},{4,6},{5,7},{6,4},{7,5},{8,10},{9,11},{10,... | collective-permute-start | bytes 589832 | tf_op jit(solution)/shard_map/ppermute | solution.py:278
  64.1 10.1 %collective-permute-start.4 = (bf16[6,2,8,8,128]{4,3,2,1,0:T(8,128)(2,1)S(1)}, bf16[6,2,8,8,128]{4,3,2,1,0:T(8,128)(2,1)S(1)}, u32[]{:S(2)}, u32[]{:S(2)}) collective-permute-start(bf16[6,2,8,8,128]{4,3,2,1,0:T(8,128)(2,1)S(1)} %get-tuple-element.34.sent_ref), channel_id=1, source_target_pairs={{0,1},{1,0},{2,3},{3,2},{4,5},{5,4},{6,7},{7,6},{8,9},{9,8},{10,11... | collective-permute-start | bytes 589832 | tf_op jit(solution)/shard_map/ppermute | solution.py:282
  69.9 10.2 %all-to-all-start.2 = ((f32[16,16,128]{2,1,0:T(8,128)}), f32[16,16,128]{2,1,0:T(8,128)S(1)}, u32[]{:S(2)}, u32[]{:S(2)}) async-start(f32[16,16,128]{2,1,0:T(8,128)} %broadcast_in_dim.7), calls=%async_computation.2 | async-start | bytes 262144 | tf_op jit(solution)/shard_map/all_to_all | solution.py:283
  73.5 0.7 copy-start.2

commit v5 on v4

--- a/solution.py
+++ b/solution.py
@@ -68,9 +68,9 @@
     for r in range(14):
         first = acc[2 * r * outs : (2 * r + 1) * outs]
         second = bias_half if r == 13 else acc[(2 * r + 1) * outs : (2 * r + 2) * outs]
-        sums_ref[r] = jnp.concatenate([first, second], axis=1)
+        sums_ref[r, 0:outs] = jnp.concatenate([first, second], axis=1)
     for r in range(14, 16):
-        sums_ref[r] = jnp.zeros((outs, cols), F32)
+        sums_ref[r, 0:outs] = jnp.zeros((outs, cols), F32)
 
 
 def moved_rows(gpad, d, h):
@@ -194,12 +194,12 @@
 
 
 def unpack(scale, every_ref, weight_ref, bias_ref):
-    outs, cols = every_ref.shape[1:]
+    outs, cols = every_ref.shape[2:]
     half = cols // 2
     for t in range(27):
         r, side = t // 2, t % 2
-        weight_ref[t] = every_ref[r, :, half * side : half * (side + 1)] * scale
-    total = jnp.sum(every_ref[13, :, half:] * scale, axis=1, keepdims=True)
+        weight_ref[t] = every_ref[r, 0, :, half * side : half * (side + 1)] * scale
+    total = jnp.sum(every_ref[13, 0, :, half:] * scale, axis=1, keepdims=True)
     wide = jnp.broadcast_to(total, (outs, cols))
     row = lax.broadcasted_iota(jnp.int32, (outs, cols), 0)
     lane = lax.broadcasted_iota(jnp.int32, (outs, cols), 1)
@@ -252,7 +252,7 @@
     sums, moved = pl.pallas_call(
         weight_sums,
         out_shape=(
-            jax.ShapeDtypeStruct((16, outs, cols), F32),
+            jax.ShapeDtypeStruct((16, 3 * outs, cols), F32),
             jax.ShapeDtypeStruct((depth + 2, rows + 2, 3 * outs, cols), BF16),
         ),
         in_specs=[WHOLE] * 4,
@@ -272,7 +272,7 @@
         compiler_params=PARAMS,
     )(me, moved, taps, before, after)
     got = lax.ppermute(send, "filt", swap_pairs(4))
-    mine = jnp.sum(parts, axis=0)
+    mine = jnp.sum(parts[:, :outs], axis=0)
     mine, got = lax.optimization_barrier((mine, got))
     keep, send = shares_step(2, block)(keep, send, got)
     got = lax.ppermute(send, "filt", swap_pairs(2))
@@ -281,7 +281,7 @@
     keep, send = shares_step(1, block)(keep, send, got)
     got = lax.ppermute(send, "filt", swap_pairs(1))
     every = lax.all_to_all(
-        jnp.broadcast_to(mine[None], (16,) + mine.shape), "space", 0, 0, axis_index_groups=XY_GROUPS
+        jnp.broadcast_to(mine[None, None], (16, 3) + mine.shape), "space", 0, 0, axis_index_groups=XY_GROUPS
     )
     output, grad_volume = pl.pallas_call(
         finish,

time: 81.6 us -> 88.2 us (1.081)
  the two profiles are of different devices: /device:TPU:1 before, /device:TPU:64 now
where the time goes in v5:
time: 88.2 us; the launch traced here: 87.6 us
  starting transfers between devices  41.7 us (47%)
  waiting for transfers between devices  20.1 us (23%)
  blocking collectives  18.3 us (21%)
  Pallas kernels  4.27 us (5%)
  local copies, waits for them, and re-layouts  2.42 us (3%)
    psum x1, blocking collectives, local(): mine = lax.psum(mine, 'space', axis_index_groups=Z_GROUPS)  18.3 us
    all_to_all x1, starting transfers between devices, local(): parts = lax.all_to_all(sums, 'space', 0, 0, axis_index_groups=XY_GROUPS)  13 us
    all_to_all x1, starting transfers between devices, local(): lax.all_to_all(jnp.broadcast_to(own[None], (8,) + own.shape), 'filt', 0, 0)  8.49 us
    all_to_all x1, waiting for transfers between devices, local(): parts = lax.all_to_all(sums, 'space', 0, 0, axis_index_groups=XY_GROUPS)  7.24 us
    all_to_all x1, starting transfers between devices, local(): lax.all_to_all(jnp.broadcast_to(mine[None, None], (16, 3) + mine.shape),...  6.93 us
    ppermute x1, starting transfers between devices, local(): got = lax.ppermute(send, 'filt', swap_pairs(2))  5.29 us
    ppermute x1, waiting for transfers between devices, local(): got = lax.ppermute(send, 'filt', swap_pairs(4))  4.6 us
    all_to_all x1, waiting for transfers between devices, local(): lax.all_to_all(jnp.broadcast_to(mine[None, None], (16, 3) + mine.shape),...  4.43 us
  transfers between devices with their start and end apart: 8, of which 5 were waited for; matrix products, arithmetic and copies ran while one was open for 0% of the time, Pallas kernels for 2%

profile of v5, /device:TPU:64, one launch (start us, length us, event | category | flops | bytes accessed | tf_op | source)
XLA Modules:
  0.0 87.6 jit_solution(16258057793921671607)
XLA Ops:
  0.6 0.8 copy.14
  1.4 0.7 broadcast_in_dim.6
  2.1 0.0 copy-start.1
  2.1 8.5 %all-to-all-start = ((bf16[8,2,8,8,128]{4,3,2,1,0:T(8,128)(2,1)}), bf16[8,2,8,8,128]{4,3,2,1,0:T(8,128)(2,1)S(1)}, u32[]{:S(2)}, u32[]{:S(2)}) async-start(bf16[8,2,8,8,128]{4,3,2,1,0:T(8,128)(2,1)} %broadcast_in_dim.6), calls=%async_computation | async-start | bytes 524288 | tf_op jit(solution)/shard_map/all_to_all | solution.py:250
  10.6 0.0 copy-done.1
  10.7 0.7 collective-permute-start.1
  11.4 3.5 %collective-permute-start = (bf16[8,24,128]{2,1,0:T(8,128)(2,1)S(1)}, bf16[8,24,128]{2,1,0:T(8,128)(2,1)S(1)}, u32[]{:S(2)}, u32[]{:S(2)}) collective-permute-start(bf16[8,24,128]{2,1,0:T(8,128)(2,1)S(1)} %get-tuple-element.45), channel_id=1, source_target_pairs={{0,8},{8,0},{16,24},{24,16},{32,40},{40,32},{48,56},{56,48},{64,72... | collective-permute-start | bytes 147464 | tf_op jit(solution)/shard_map/ppermute | solution.py:218
  14.9 0.0 collective-permute-done.1
  14.9 2.5 %collective-permute-done = bf16[8,24,128]{2,1,0:T(8,128)(2,1)S(1)} collective-permute-done((bf16[8,24,128]{2,1,0:T(8,128)(2,1)S(1)}, bf16[8,24,128]{2,1,0:T(8,128)(2,1)S(1)}, u32[]{:S(2)}, u32[]{:S(2)}) %collective-permute-start) | collective-permute-done | bytes 49184 | tf_op jit(solution)/shard_map/ppermute | solution.py:218
  17.4 0.0 all-to-all-done.vol_ref
  17.4 1.5 %shard_map.75 = (f32[16,48,128]{2,1,0:T(8,128)}, bf16[4,10,48,128]{3,2,1,0:T(8,128)(2,1)S(1)}) custom-call(bf16[8,2,8,8,128]{4,3,2,1,0:T(8,128)(2,1)S(1)} %all-to-all-done.vol_ref, bf16[2,8,16,128]{3,2,1,0:T(8,128)(2,1)S(1)} %bitcast.16, bf16[8,24,128]{2,1,0:T(8,128)(2,1)S(1)} %get-tuple-element.43.before_ref, ...), custom_call_target="tpu_custom_call" | custom-call | tf_op jit(solution)/shard_map/pallas_call | solution.py:252
  18.9 0.0 copy-start
  18.9 13.0 %all-to-all-start.1 = ((f32[16,48,128]{2,1,0:T(8,128)}), f32[16,48,128]{2,1,0:T(8,128)S(1)}, u32[]{:S(2)}, u32[]{:S(2)}) async-start(f32[16,48,128]{2,1,0:T(8,128)} %get-tuple-element.23), calls=%async_computation.1 | async-start | bytes 786432 | tf_op jit(solution)/shard_map/all_to_all | solution.py:262
  31.9 0.0 copy-done
  31.9 0.5 shard_map.76
  32.4 1.9 %collective-permute-start.2 = (bf16[9,2,8,8,128]{4,3,2,1,0:T(8,128)(2,1)S(1)}, bf16[9,2,8,8,128]{4,3,2,1,0:T(8,128)(2,1)S(1)}, u32[]{:S(2)}, u32[]{:S(2)}) collective-permute-start(bf16[9,2,8,8,128]{4,3,2,1,0:T(8,128)(2,1)S(1)} %get-tuple-element.25.sent_ref), channel_id=1, source_target_pairs={{0,4},{1,5},{2,6},{3,7},{4,0},{5,1},{6,2},{7,3},{8,12},{9,13},{10,... | collective-permute-start | bytes 884744 | tf_op jit(solution)/shard_map/ppermute | solution.py:274
  34.3 7.2 %all-to-all-done.1 = f32[16,48,128]{2,1,0:T(8,128)S(1)} async-done(((f32[16,48,128]{2,1,0:T(8,128)}), f32[16,48,128]{2,1,0:T(8,128)S(1)}, u32[]{:S(2)}, u32[]{:S(2)}) %all-to-all-start.1) | async-done | bytes 393248 | tf_op jit(solution)/shard_map/all_to_all | solution.py:262
  41.6 4.6 %collective-permute-done.2.got_ref = bf16[9,2,8,8,128]{4,3,2,1,0:T(8,128)(2,1)S(1)} collective-permute-done((bf16[9,2,8,8,128]{4,3,2,1,0:T(8,128)(2,1)S(1)}, bf16[9,2,8,8,128]{4,3,2,1,0:T(8,128)(2,1)S(1)}, u32[]{:S(2)}, u32[]{:S(2)}) %collective-permute-start.2) | collective-permute-done | bytes 294944 | tf_op jit(solution)/shard_map/ppermute | solution.py:274
  46.2 0.1 shard_map.77
  46.3 5.3 %collective-permute-start.3 = (bf16[6,2,8,8,128]{4,3,2,1,0:T(8,128)(2,1)S(1)}, bf16[6,2,8,8,128]{4,3,2,1,0:T(8,128)(2,1)S(1)}, u32[]{:S(2)}, u32[]{:S(2)}) collective-permute-start(bf16[6,2,8,8,128]{4,3,2,1,0:T(8,128)(2,1)S(1)} %get-tuple-element.29.sent_ref), channel_id=1, source_target_pairs={{0,2},{1,3},{2,0},{3,1},{4,6},{5,7},{6,4},{7,5},{8,10},{9,11},{10,... | collective-permute-start | bytes 589832 | tf_op jit(solution)/shard_map/ppermute | solution.py:278
  51.6 18.3 %psum.7 = f32[16,128]{1,0:T(8,128)S(1)} all-reduce(f32[16,128]{1,0:T(8,128)S(1)} %slice_reduce_fusion), channel_id=1, replica_groups={{0,128,256,384},{8,136,264,392},{16,144,272,400},{24,152,280,408},{32,1..., use_global_device_ids=true, to_apply=%region_1.2 | all-reduce | flops 2048 | bytes 16384 | tf_op jit(solution)/shard_map/psum | solution.py:279
  69.9 0.0 collective-permute-done.3.got_ref
  69.9 0.8 broadcast_in_dim.7
  70.7 6.9 %all-to-all-start.2 = ((f32[16,3,16,128]{3,2,1,0:T(8,128)}), f32[16,3,16,128]{3,2,1,0:T(8,128)S(1)}, u32[]{:S(2)}, u32[]{:S(2)}) async-start(f32[16,3,16,128]{3,2,1,0:T(8,128)} %broadcast_in_dim.7), calls=%async_computation.2 | async-start | bytes 786432 | tf_op jit(solution)/shard_map/all_to_all | solution.py:283
  77.7 0.0 copy-start.2
  77.7 1.9 %collective-permute-start.4 = (bf16[6,2,8,8,128]{4,3,2,1,0:T(8,128)(2,1)S(1)}, bf16[6,2,8,8,128]{4,3,2,1,0:T(8,128)(2,1)S(1)}, u32[]{:S(2)}, u32[]{:S(2)}) collective-permute-start(bf16[6,2,8,8,128]{4,3,2,1,0:T(8,128)(2,1)S(1)} %get-tuple-element.34.sent_ref), channel_id=1, source_target_pairs={{0,1},{1,0},{2,3},{3,2},{4,5},{5,4},{6,7},{7,6},{8,9},{9,8},{10,11... | collective-permute-start | bytes 589832 | tf_op jit(solution)/shard_map/ppermute | solution.py:282
  79.6 0.0 copy-done.2
  79.6 0.1 copy.10.bias_ref
  79.7 1.3 %collective-permute-done.4.got_ref = bf16[6,2,8,8,128]{4,3,2,1,0:T(8,128)(2,1)S(1)} collective-permute-done((bf16[6,2,8,8,128]{4,3,2,1,0:T(8,128)(2,1)S(1)}, bf16[6,2,8,8,128]{4,3,2,1,0:T(8,128)(2,1)S(1)}, u32[]{:S(2)}, u32[]{:S(2)}) %collective-permute-start.4) | collective-permute-done | bytes 196640 | tf_op jit(solution)/shard_map/ppermute | solution.py:282
  81.0 1.3 %shard_map.79 = (bf16[16,2,8,128]{3,2,1,0:T(8,128)(2,1)}, bf16[8,2,8,128]{3,2,1,0:T(8,128)(2,1)}) custom-call(s32[1]{0:T(128)} %bitcast.4.me_ref, bf16[8,2,8,8,128]{4,3,2,1,0:T(8,128)(2,1)S(1)} %all-to-all-done.vol_ref, f32[1,2,8,8,128]{4,3,2,1,0:T(8,128)S(1)} %get-tuple-element.33.keep_ref, bf16[6,2,8,8,128]{4,3,2,1,0:T(8,128)(2,1)S(1)} %get-tuple-element.34.sent_ref, ...), custom_call_target="tpu_custom_call" | custom-call | tf_op jit(solution)/shard_map/pallas_call | solution.py:286
  82.3 4.4 %all-to-all-done.2.refs_0_ = f32[16,3,16,128]{3,2,1,0:T(8,128)S(1)} async-done(((f32[16,3,16,128]{3,2,1,0:T(8,128)}), f32[16,3,16,128]{3,2,1,0:T(8,128)S(1)}, u32[]{:S(2)}, u32[]{:S(2)}) %all-to-all-start.2) | async-done | bytes 393248 | tf_op jit(solution)/shard_map/all_to_all | solution.py:283
  86.8 0.8 shard_map.80
  (5 shorter events, 0.1 us)
Async XLA Ops:
  2.1 8.5 %copy-start.1 = (bf16[16,2,8,128]{3,2,1,0:T(8,128)(2,1)S(1)}, bf16[16,2,8,128]{3,2,1,0:T(8,128)(2,1)}, u32[]{:S(2)}) copy-start(bf16[16,2,8,128]{3,2,1,0:T(8,128)(2,1)} %param.7) | copy-start | bytes 196612
  2.1 15.2 %all-to-all-start = ((bf16[8,2,8,8,128]{4,3,2,1,0:T(8,128)(2,1)}), bf16[8,2,8,8,128]{4,3,2,1,0:T(8,128)(2,1)S(1)}, u32[]{:S(2)}, u32[]{:S(2)}) async-start(bf16[8,2,8,8,128]{4,3,2,1,0:T(8,128)(2,1)} %broadcast_in_dim.6), calls=%async_computation | async-start | bytes 524288 | tf_op jit(solution)/shard_map/all_to_all | solution.py:250
  10.7 4.2 %collective-permute-start.1 = (bf16[8,24,128]{2,1,0:T(8,128)(2,1)S(1)}, bf16[8,24,128]{2,1,0:T(8,128)(2,1)S(1)}, u32[]{:S(2)}, u32[]{:S(2)}) collective-permute-start(bf16[8,24,128]{2,1,0:T(8,128)(2,1)S(1)} %get-tuple-element.44), channel_id=1, source_target_pairs={{8,16},{16,8},{24,32},{32,24},{40,48},{48,40},{56,64},{64,56},{72,... | collective-permute-start | bytes 147464 | tf_op jit(solution)/shard_map/ppermute | solution.py:219
  11.4 6.0 %collective-permute-start = (bf16[8,24,128]{2,1,0:T(8,128)(2,1)S(1)}, bf16[8,24,128]{2,1,0:T(8,128)(2,1)S(1)}, u32[]{:S(2)}, u32[]{:S(2)}) collective-permute-start(bf16[8,24,128]{2,1,0:T(8,128)(2,1)S(1)} %get-tuple-element.45), channel_id=1, source_target_pairs={{0,8},{8,0},{16,24},{24,16},{32,40},{40,32},{48,56},{56,48},{64,72... | collective-permute-start | bytes 147464 | tf_op jit(solution)/shard_map/ppermute | solution.py:218
  18.9 13.0 %copy-start = (bf16[27,64,16]{1,2,0:T(8,128)(2,1)S(1)}, bf16[27,64,16]{1,2,0:T(8,128)(2,1)}, u32[]{:S(2)}) copy-start(bf16[27,64,16]{1,2,0:T(8,128)(2,1)} %param.5) | copy-start | bytes 165892
  18.9 22.7 %all-to-all-start.1 = ((f32[16,48,128]{2,1,0:T(8,128)}), f32[16,48,128]{2,1,0:T(8,128)S(1)}, u32[]{:S(2)}, u32[]{:S(2)}) async-start(f32[16,48,128]{2,1,0:T(8,128)} %get-tuple-element.23), calls=%async_computation.1 | async-start | bytes 786432 | tf_op jit(solution)/shard_map/all_to_all | solution.py:262
  32.4 13.8 %collective-permute-start.2 = (bf16[9,2,8,8,128]{4,3,2,1,0:T(8,128)(2,1)S(1)}, bf16[9,2,8,8,128]{4,3,2,1,0:T(8,128)(2,1)S(1)}, u32[]{:S(2)}, u32[]{:S(2)}) collective-permute-start(bf16[9,2,8,8,128]{4,3,2,1,0:T(8,128)(2,1)S(1)} %get-tuple-element.25.sent_ref), channel_id=1, source_target_pairs={{0,4},{1,5},{2,6},{3,7},{4,0},{5,1},{6,2},{7,3},{8,12},{9,13},{10,... | collective-permute-start | bytes 884744 | tf_op jit(solution)/shard_map/ppermute | solution.py:274
  46.3 23.6 %collective-permute-start.3 = (bf16[6,2,8,8,128]{4,3,2,1,0:T(8,128)(2,1)S(1)}, bf16[6,2,8,8,128]{4,3,2,1,0:T(8,128)(2,1)S(1)}, u32[]{:S(2)}, u32[]{:S(2)}) collective-permute-start(bf16[6,2,8,8,128]{4,3,2,1,0:T(8,128)(2,1)S(1)} %get-tuple-element.29.sent_ref), channel_id=1, source_target_pairs={{0,2},{1,3},{2,0},{3,1},{4,6},{5,7},{6,4},{7,5},{8,10},{9,11},{10,... | collective-permute-start | bytes 589832 | tf_op jit(solution)/shard_map/ppermute | solution.py:278
  70.7 16.1 %all-to-all-start.2 = ((f32[16,3,16,128]{3,2,1,0:T(8,128)}), f32[16,3,16,128]{3,2,1,0:T(8,128)S(1)}, u32[]{:S(2)}, u32[]{:S(2)}) async-start(f32[16,3,16,128]{3,2,1,0:T(8,128)} %broadcast_in_dim.7), calls=%async_computation.2 | async-start | bytes 786432 | tf_op jit(solution)/shard_map/all_to_all | solution.py:283
  77.7 1.9 %copy-start.2 = (f32[16]{0:T(128)S(1)}, f32[16]{0:T(128)}, u32[]{:S(2)}) copy-start(f32[16]{0:T(128)} %param.6) | copy-start | bytes 196
  77.7 3.3 %collective-permute-start.4 = (bf16[6,2,8,8,128]{4,3,2,1,0:T(8,128)(2,1)S(1)}, bf16[6,2,8,8,128]{4,3,2,1,0:T(8,128)(2,1)S(1)}, u32[]{:S(2)}, u32[]{:S(2)}) collective-permute-start(bf16[6,2,8,8,128]{4,3,2,1,0:T(8,128)(2,1)S(1)} %get-tuple-element.34.sent_ref), channel_id=1, source_target_pairs={{0,1},{1,0},{2,3},{3,2},{4,5},{5,4},{6,7},{7,6},{8,9},{9,8},{10,11... | collective-permute-start | bytes 589832 | tf_op jit(solution)/shard_map/ppermute | solution.py:282

commit v6 on v4

--- a/solution.py
+++ b/solution.py
@@ -10,6 +10,7 @@
 F32 = jnp.float32
 BF16 = jnp.bfloat16
 WHOLE = pl.BlockSpec(memory_space=pltpu.VMEM)
+SCALAR = pl.BlockSpec(memory_space=pltpu.SMEM)
 PARAMS = pltpu.CompilerParams(vmem_limit_bytes=40 * 1024 * 1024)
 
 
@@ -30,27 +31,30 @@
     return jnp.where(lane == edge, 0.0, turned)
 
 
-def weight_sums(vol_ref, grad_ref, before_ref, after_ref, sums_ref, gpad):
+def weight_sums(odd_ref, vol_ref, grad_ref, outer_ref, inner_ref, sums_ref, gpad):
     peers, depth, rows, share, cols = vol_ref.shape
-    outs = grad_ref.shape[2]
+    outs = grad_ref.shape[0]
     chans = peers * share
+    odd = odd_ref[0] == 1
+    inner = inner_ref[0:outs].astype(F32)
+    outer = outer_ref[0:outs].astype(F32)
+    planes = [
+        jnp.where(odd, inner, outer),
+        *[grad_ref[:, d].astype(F32) for d in range(depth)],
+        jnp.where(odd, outer, inner),
+    ]
     blank = jnp.zeros((3 * outs, cols), BF16)
     bias_sum = jnp.zeros((outs, cols), F32)
     for p in range(depth + 2):
         gpad[p, 0] = blank
         gpad[p, rows + 1] = blank
+        plane = jnp.swapaxes(planes[p], 0, 1)
         for h in range(rows):
-            if p == 0:
-                line = before_ref[h, 0:outs]
-            elif p == depth + 1:
-                line = after_ref[h, 0:outs]
-            else:
-                line = grad_ref[p - 1, h]
-            wide = line.astype(F32)
+            wide = plane[h]
             if 0 < p < depth + 1:
                 bias_sum = bias_sum + wide
             gpad[p, h + 1, 0:outs] = slide(wide, 1).astype(BF16)
-            gpad[p, h + 1, outs : 2 * outs] = line
+            gpad[p, h + 1, outs : 2 * outs] = wide.astype(BF16)
             gpad[p, h + 1, 2 * outs : 3 * outs] = slide(wide, -1).astype(BF16)
     acc = jnp.zeros((27 * outs, chans), F32)
     for d in range(depth):
@@ -91,7 +95,7 @@
 
 
 def shares_first(
-    me_ref, moved_ref, taps_ref, before_ref, after_ref, keep_ref, send_ref, turned
+    odd_ref, me_ref, moved_ref, taps_ref, outer_ref, inner_ref, keep_ref, send_ref, turned
 ):
     _, depth, rows, share, cols = keep_ref.shape
     outs, chans = taps_ref.shape[1:]
@@ -100,7 +104,7 @@
     behind = jnp.concatenate(
         [
             turned[pl.ds(pl.multiple_of(share * jnp.bitwise_xor(me, r), share), share)]
-            for r in range(8)
+            for r in ORDER
         ],
         axis=0,
     ).astype(BF16)
@@ -116,9 +120,11 @@
                         high, low = split(value)
                         send_ref[2 * (r - 4), d, h + k] = high
                         send_ref[2 * (r - 4) + 1, d, h + k] = low
-    for h in range(rows):
-        send_ref[8, 0, h] = before_ref[h, outs : outs + share]
-        send_ref[8, 1, h] = after_ref[h, outs : outs + share]
+    odd = odd_ref[0] == 1
+    inner = inner_ref[outs : outs + share].astype(F32)
+    outer = outer_ref[outs : outs + share].astype(F32)
+    send_ref[8, 0] = jnp.swapaxes(jnp.where(odd, inner, outer), 0, 1).astype(BF16)
+    send_ref[8, 1] = jnp.swapaxes(jnp.where(odd, outer, inner), 0, 1).astype(BF16)
 
 
 def shares_next(keep_ref, sent_ref, got_ref, kept_ref, send_ref):
@@ -139,6 +145,12 @@
             place += 1
 
 
+def shares_last(keep_ref, sent_ref, got_ref, mine_ref, kept_ref, send_ref, spread_ref):
+    shares_next(keep_ref, sent_ref, got_ref, kept_ref, send_ref)
+    for k in range(spread_ref.shape[0]):
+        spread_ref[k] = mine_ref[...]
+
+
 def finish(
     me_ref, vol_ref, keep_ref, sent_ref, got_ref, taps_ref, bias_ref, out_ref, back_ref, halo, vpad
 ):
@@ -146,9 +158,10 @@
     taps = taps_ref[...]
     outs, chans = taps.shape[1:]
     me = me_ref[0]
-    for place, r in enumerate((0, 4, 2, 6)):
+    first, second, third = SWAPS
+    for place, r in enumerate((0, first, second, first ^ second)):
         halo[jnp.bitwise_xor(me, r)] = sent_ref[2 + place]
-        halo[jnp.bitwise_xor(me, r + 1)] = got_ref[2 + place]
+        halo[jnp.bitwise_xor(me, r ^ third)] = got_ref[2 + place]
     blank = jnp.zeros((chans, cols), BF16)
     for p in range(depth + 2):
         vpad[p, 0] = blank
@@ -207,34 +220,22 @@
     bias_ref[...] = flat[:, :outs]
 
 
+SWAPS = (2, 1, 4)
+ORDER = [sum(bit for k, bit in enumerate(SWAPS) if n & (4 >> k)) for n in range(8)]
 XY_GROUPS = [[16 * z + k for k in range(16)] for z in range(4)]
 Z_GROUPS = [[16 * z + k for z in range(4)] for k in range(16)]
 EVEN = [(i, i ^ 1) for i in range(64)]
 ODD = [(i, ((i + 1) ^ 1) - 1) for i in range(1, 63)]
 
 
-def swap_edges(head, tail):
-    odd = (lax.axis_index("space") % 2) == 1
+def swap_edges(odd, head, tail):
     inner = lax.ppermute(jnp.where(odd, head, tail), "space", EVEN)
     outer = lax.ppermute(jnp.where(odd, tail, head), "space", ODD)
-    return jnp.where(odd, inner, outer), jnp.where(odd, outer, inner)
+    return inner, outer
 
 
 def swap_pairs(bit):
     return [(f, f ^ bit) for f in range(8)]
-
-
-def shares_step(blocks, block):
-    return pl.pallas_call(
-        shares_next,
-        out_shape=(
-            jax.ShapeDtypeStruct((blocks,) + block, F32),
-            jax.ShapeDtypeStruct((6,) + block, BF16),
-        ),
-        in_specs=[WHOLE] * 3,
-        out_specs=(WHOLE,) * 2,
-        compiler_params=PARAMS,
-    )
 
 
 def local(volume, weight, bias, grad_out):
@@ -242,11 +243,14 @@
     outs = grad_out.shape[0]
     chans = weight.shape[1]
     taps = weight.transpose(0, 2, 1)
-    grad = grad_out.transpose(1, 2, 0, 3)
     own = volume.transpose(1, 2, 0, 3)
+    odd = jnp.bitwise_and(lax.axis_index("space").astype(jnp.int32), 1)
     me = lax.axis_index("filt").astype(jnp.int32).reshape(1)
-    both = jnp.concatenate([grad, own], axis=2)
-    before, after = swap_edges(both[0], both[depth - 1])
+    head, tail = (
+        jnp.concatenate([grad_out[:, d], volume[:, d]], axis=0) for d in (0, depth - 1)
+    )
+    inner, outer = swap_edges(odd == 1, head, tail)
+    odd = odd.reshape(1)
     vol = lax.all_to_all(jnp.broadcast_to(own[None], (8,) + own.shape), "filt", 0, 0)
     block = (depth, rows, share, cols)
     sums, moved = pl.pallas_call(
@@ -255,10 +259,10 @@
             jax.ShapeDtypeStruct((16, outs, cols), F32),
             jax.ShapeDtypeStruct((depth + 2, rows + 2, 3 * outs, cols), BF16),
         ),
-        in_specs=[WHOLE] * 4,
-        out_specs=(WHOLE,) * 2,
-        compiler_params=PARAMS,
-    )(vol, grad, before, after)
+        in_specs=[SCALAR] + [WHOLE] * 4,
+        out_specs=(WHOLE,) * 2,
+        compiler_params=PARAMS,
+    )(odd, vol, grad_out, outer, inner)
     parts = lax.all_to_all(sums, "space", 0, 0, axis_index_groups=XY_GROUPS)
     keep, send = pl.pallas_call(
         shares_first,
@@ -266,30 +270,47 @@
             jax.ShapeDtypeStruct((4,) + block, F32),
             jax.ShapeDtypeStruct((9,) + block, BF16),
         ),
-        in_specs=[pl.BlockSpec(memory_space=pltpu.SMEM)] + [WHOLE] * 4,
+        in_specs=[SCALAR] * 2 + [WHOLE] * 4,
         out_specs=(WHOLE,) * 2,
         scratch_shapes=[pltpu.VMEM((chans, 27 * outs), F32)],
         compiler_params=PARAMS,
-    )(me, moved, taps, before, after)
-    got = lax.ppermute(send, "filt", swap_pairs(4))
+    )(odd, me, moved, taps, outer, inner)
+    got = lax.ppermute(send, "filt", swap_pairs(SWAPS[0]))
     mine = jnp.sum(parts, axis=0)
     mine, got = lax.optimization_barrier((mine, got))
-    keep, send = shares_step(2, block)(keep, send, got)
-    got = lax.ppermute(send, "filt", swap_pairs(2))
+    keep, send = pl.pallas_call(
+        shares_next,
+        out_shape=(
+            jax.ShapeDtypeStruct((2,) + block, F32),
+            jax.ShapeDtypeStruct((6,) + block, BF16),
+        ),
+        in_specs=[WHOLE] * 3,
+        out_specs=(WHOLE,) * 2,
+        compiler_params=PARAMS,
+    )(keep, send, got)
+    got = lax.ppermute(send, "filt", swap_pairs(SWAPS[1]))
     mine = lax.psum(mine, "space", axis_index_groups=Z_GROUPS)
     mine, got = lax.optimization_barrier((mine, got))
-    keep, send = shares_step(1, block)(keep, send, got)
-    got = lax.ppermute(send, "filt", swap_pairs(1))
-    every = lax.all_to_all(
-        jnp.broadcast_to(mine[None], (16,) + mine.shape), "space", 0, 0, axis_index_groups=XY_GROUPS
-    )
+    keep, send, spread = pl.pallas_call(
+        shares_last,
+        out_shape=(
+            jax.ShapeDtypeStruct((1,) + block, F32),
+            jax.ShapeDtypeStruct((6,) + block, BF16),
+            jax.ShapeDtypeStruct((16, outs, cols), F32),
+        ),
+        in_specs=[WHOLE] * 4,
+        out_specs=(WHOLE,) * 3,
+        compiler_params=PARAMS,
+    )(keep, send, got, mine)
+    got = lax.ppermute(send, "filt", swap_pairs(SWAPS[2]))
+    every = lax.all_to_all(spread, "space", 0, 0, axis_index_groups=XY_GROUPS)
     output, grad_volume = pl.pallas_call(
         finish,
         out_shape=(
             jax.ShapeDtypeStruct((outs, depth, rows, cols), BF16),
             jax.ShapeDtypeStruct((share, depth, rows, cols), BF16),
         ),
-        in_specs=[pl.BlockSpec(memory_space=pltpu.SMEM)] + [WHOLE] * 6,
+        in_specs=[SCALAR] + [WHOLE] * 6,
         out_specs=(WHOLE,) * 2,
         scratch_shapes=[
             pltpu.VMEM((8,) + block, BF16),

time: 81.6 us -> 81.8 us (level)
  the two profiles are of different devices: /device:TPU:1 before, /device:TPU:32 now
where the time goes in v6:
time: 81.8 us; the launch traced here: 81.2 us
  blocking collectives  37.4 us (46%)
  starting transfers between devices  27 us (33%)
  waiting for transfers between devices  8.64 us (11%)
  Pallas kernels  4.18 us (5%)
  local copies, waits for them, and re-layouts  3.23 us (4%)
    all_to_all x1, blocking collectives, local(): parts = lax.all_to_all(sums, 'space', 0, 0, axis_index_groups=XY_GROUPS)  19 us
    psum x1, blocking collectives, local(): mine = lax.psum(mine, 'space', axis_index_groups=Z_GROUPS)  18.4 us
    all_to_all x1, starting transfers between devices, local(): lax.all_to_all(jnp.broadcast_to(own[None], (8,) + own.shape), 'filt', 0, 0)  8.93 us
    ppermute x1, starting transfers between devices, local(): got = lax.ppermute(send, 'filt', swap_pairs(SWAPS[2]))  4.57 us
    ppermute x1, starting transfers between devices, local(): got = lax.ppermute(send, 'filt', swap_pairs(SWAPS[0]))  3.76 us
    all_to_all x1, starting transfers between devices, local(): every = lax.all_to_all(spread, 'space', 0, 0, axis_index_groups=XY_GROUPS)  3.61 us
    ppermute x1, starting transfers between devices, swap_edges(): inner = lax.ppermute(jnp.where(odd, head, tail), 'space', EVEN)  3.51 us
    all_to_all x1, waiting for transfers between devices, local(): every = lax.all_to_all(spread, 'space', 0, 0, axis_index_groups=XY_GROUPS)  3.38 us
  transfers between devices with their start and end apart: 7, of which 4 were waited for; matrix products, arithmetic and copies ran while one was open for 0% of the time, Pallas kernels for 2%

profile of v6, /device:TPU:32, one launch (start us, length us, event | category | flops | bytes accessed | tf_op | source)
XLA Modules:
  0.0 81.2 jit_solution(17458647691514945888)
XLA Ops:
  0.6 0.8 copy.8
  1.4 0.7 broadcast_in_dim.4
  2.1 0.0 copy-start.2
  2.2 8.9 %all-to-all-start = ((bf16[8,2,8,8,128]{4,3,2,1,0:T(8,128)(2,1)}), bf16[8,2,8,8,128]{4,3,2,1,0:T(8,128)(2,1)S(1)}, u32[]{:S(2)}, u32[]{:S(2)}) async-start(bf16[8,2,8,8,128]{4,3,2,1,0:T(8,128)(2,1)} %broadcast_in_dim.4), calls=%async_computation | async-start | bytes 524288 | tf_op jit(solution)/shard_map/all_to_all | solution.py:254
  11.1 0.0 copy-start.1
  11.1 0.0 copy-done.2
  11.1 0.8 %copy-done.1 = bf16[16,2,8,128]{3,2,1,0:T(8,128)(2,1)S(1)} copy-done((bf16[16,2,8,128]{3,2,1,0:T(8,128)(2,1)S(1)}, bf16[16,2,8,128]{3,2,1,0:T(8,128)(2,1)}, u32[]{:S(2)}) %copy-start.1) | copy-done | bytes 65560
  11.9 0.7 collective-permute-start
  12.6 3.5 %collective-permute-start.1 = (bf16[24,8,128]{2,1,0:T(8,128)(2,1)S(1)}, bf16[24,8,128]{2,1,0:T(8,128)(2,1)S(1)}, u32[]{:S(2)}, u32[]{:S(2)}) collective-permute-start(bf16[24,8,128]{2,1,0:T(8,128)(2,1)S(1)} %get-tuple-element.44), channel_id=1, source_target_pairs={{0,8},{8,0},{16,24},{24,16},{32,40},{40,32},{48,56},{56,48},{64,72... | collective-permute-start | bytes 147464 | tf_op jit(solution)/shard_map/ppermute | solution.py:232
  16.1 0.0 collective-permute-done.outer_ref
  16.1 2.5 %collective-permute-done.1.inner_ref = bf16[24,8,128]{2,1,0:T(8,128)(2,1)S(1)} collective-permute-done((bf16[24,8,128]{2,1,0:T(8,128)(2,1)S(1)}, bf16[24,8,128]{2,1,0:T(8,128)(2,1)S(1)}, u32[]{:S(2)}, u32[]{:S(2)}) %collective-permute-start.1) | collective-permute-done | bytes 49184 | tf_op jit(solution)/shard_map/ppermute | solution.py:232
  18.6 0.4 all-to-all-done.vol_ref
  19.0 0.0 copy-start
  19.0 0.8 shard_map.75
  19.7 0.1 copy-done
  19.9 0.5 shard_map.76
  20.4 3.8 %collective-permute-start.2 = (bf16[9,2,8,8,128]{4,3,2,1,0:T(8,128)(2,1)S(1)}, bf16[9,2,8,8,128]{4,3,2,1,0:T(8,128)(2,1)S(1)}, u32[]{:S(2)}, u32[]{:S(2)}) collective-permute-start(bf16[9,2,8,8,128]{4,3,2,1,0:T(8,128)(2,1)S(1)} %get-tuple-element.26.sent_ref), channel_id=1, source_target_pairs={{0,2},{1,3},{2,0},{3,1},{4,6},{5,7},{6,4},{7,5},{8,10},{9,11},{10,... | collective-permute-start | bytes 884744 | tf_op jit(solution)/shard_map/ppermute | solution.py:278
  24.2 19.0 %all_to_all.15 = f32[16,16,128]{2,1,0:T(8,128)S(1)} all-to-all(f32[16,16,128]{2,1,0:T(8,128)S(1)} %get-tuple-element.27), channel_id=1, replica_groups={{0,8,16,24,32,40,48,56,64,72,80,88,96,104,112,120},{128,136,144,152,160..., dimensions={0} | all-to-all | bytes 262144 | tf_op jit(solution)/shard_map/all_to_all | solution.py:266
  43.2 0.0 collective-permute-done.2.got_ref
  43.2 0.1 shard_map.77
  43.3 1.9 %collective-permute-start.3 = (bf16[6,2,8,8,128]{4,3,2,1,0:T(8,128)(2,1)S(1)}, bf16[6,2,8,8,128]{4,3,2,1,0:T(8,128)(2,1)S(1)}, u32[]{:S(2)}, u32[]{:S(2)}) collective-permute-start(bf16[6,2,8,8,128]{4,3,2,1,0:T(8,128)(2,1)S(1)} %get-tuple-element.30.sent_ref), channel_id=1, source_target_pairs={{0,1},{1,0},{2,3},{3,2},{4,5},{5,4},{6,7},{7,6},{8,9},{9,8},{10,11... | collective-permute-start | bytes 589832 | tf_op jit(solution)/shard_map/ppermute | solution.py:291
  45.2 18.4 %psum.7.mine_ref = f32[16,128]{1,0:T(8,128)S(1)} all-reduce(f32[16,128]{1,0:T(8,128)S(1)} %reduce_sum.9), channel_id=1, replica_groups={{0,128,256,384},{8,136,264,392},{16,144,272,400},{24,152,280,408},{32,1..., use_global_device_ids=true, to_apply=%region_1.2 | all-reduce | flops 2048 | bytes 16384 | tf_op jit(solution)/shard_map/psum | solution.py:292
  63.6 0.0 collective-permute-done.3.got_ref
  63.6 0.7 shard_map.78
  64.3 4.6 %collective-permute-start.4 = (bf16[6,2,8,8,128]{4,3,2,1,0:T(8,128)(2,1)S(1)}, bf16[6,2,8,8,128]{4,3,2,1,0:T(8,128)(2,1)S(1)}, u32[]{:S(2)}, u32[]{:S(2)}) collective-permute-start(bf16[6,2,8,8,128]{4,3,2,1,0:T(8,128)(2,1)S(1)} %get-tuple-element.36.sent_ref), channel_id=1, source_target_pairs={{0,4},{1,5},{2,6},{3,7},{4,0},{5,1},{6,2},{7,3},{8,12},{9,13},{10,... | collective-permute-start | bytes 589832 | tf_op jit(solution)/shard_map/ppermute | solution.py:305
  68.9 3.6 %all-to-all-start.2 = ((f32[16,16,128]{2,1,0:T(8,128)}), f32[16,16,128]{2,1,0:T(8,128)S(1)}, u32[]{:S(2)}, u32[]{:S(2)}) async-start(f32[16,16,128]{2,1,0:T(8,128)} %get-tuple-element.34), calls=%async_computation.2 | async-start | bytes 262144 | tf_op jit(solution)/shard_map/all_to_all | solution.py:306
  72.5 0.0 copy-start.3
  72.5 0.6 copy-done.3
  73.1 0.1 copy.13.bias_ref
  73.2 2.4 %collective-permute-done.4.got_ref = bf16[6,2,8,8,128]{4,3,2,1,0:T(8,128)(2,1)S(1)} collective-permute-done((bf16[6,2,8,8,128]{4,3,2,1,0:T(8,128)(2,1)S(1)}, bf16[6,2,8,8,128]{4,3,2,1,0:T(8,128)(2,1)S(1)}, u32[]{:S(2)}, u32[]{:S(2)}) %collective-permute-start.4) | collective-permute-done | bytes 196640 | tf_op jit(solution)/shard_map/ppermute | solution.py:305
  75.6 1.3 %shard_map.79 = (bf16[16,2,8,128]{3,2,1,0:T(8,128)(2,1)}, bf16[8,2,8,128]{3,2,1,0:T(8,128)(2,1)}) custom-call(s32[1]{0:T(128)} %bitcast.1.me_ref, bf16[8,2,8,8,128]{4,3,2,1,0:T(8,128)(2,1)S(1)} %all-to-all-done.vol_ref, f32[1,2,8,8,128]{4,3,2,1,0:T(8,128)S(1)} %get-tuple-element.35.keep_ref, bf16[6,2,8,8,128]{4,3,2,1,0:T(8,128)(2,1)S(1)} %get-tuple-element.36.sent_ref, ...), custom_call_target="tpu_custom_call" | custom-call | tf_op jit(solution)/shard_map/pallas_call | solution.py:307
  76.9 3.4 %all-to-all-done.2.refs_0_ = f32[16,16,128]{2,1,0:T(8,128)S(1)} async-done(((f32[16,16,128]{2,1,0:T(8,128)}), f32[16,16,128]{2,1,0:T(8,128)S(1)}, u32[]{:S(2)}, u32[]{:S(2)}) %all-to-all-start.2) | async-done | bytes 131104 | tf_op jit(solution)/shard_map/all_to_all | solution.py:306
  80.3 0.8 %shard_map.80 = (f32[27,16,64]{2,1,0:T(8,128)}, f32[1,16]{1,0:T(1,128)}) custom-call(f32[16,16,128]{2,1,0:T(8,128)S(1)} %all-to-all-done.2.refs_0_), custom_call_target="tpu_custom_call" | custom-call | tf_op jit(solution)/shard_map/pallas_call | solution.py:323
  (4 shorter events, 0.0 us)
Async XLA Ops:
  2.1 8.9 %copy-start.2 = (bf16[8,2,8,128]{3,2,1,0:T(8,128)(2,1)S(1)}, bf16[8,2,8,128]{3,2,1,0:T(8,128)(2,1)}, u32[]{:S(2)}) copy-start(bf16[8,2,8,128]{3,2,1,0:T(8,128)(2,1)} %param.4) | copy-start | bytes 98308
  2.2 16.8 %all-to-all-start = ((bf16[8,2,8,8,128]{4,3,2,1,0:T(8,128)(2,1)}), bf16[8,2,8,8,128]{4,3,2,1,0:T(8,128)(2,1)S(1)}, u32[]{:S(2)}, u32[]{:S(2)}) async-start(bf16[8,2,8,8,128]{4,3,2,1,0:T(8,128)(2,1)} %broadcast_in_dim.4), calls=%async_computation | async-start | bytes 524288 | tf_op jit(solution)/shard_map/all_to_all | solution.py:254
  11.1 0.8 %copy-start.1 = (bf16[16,2,8,128]{3,2,1,0:T(8,128)(2,1)S(1)}, bf16[16,2,8,128]{3,2,1,0:T(8,128)(2,1)}, u32[]{:S(2)}) copy-start(bf16[16,2,8,128]{3,2,1,0:T(8,128)(2,1)} %grad_ref.1) | copy-start | bytes 196612
  11.9 4.2 %collective-permute-start = (bf16[24,8,128]{2,1,0:T(8,128)(2,1)S(1)}, bf16[24,8,128]{2,1,0:T(8,128)(2,1)S(1)}, u32[]{:S(2)}, u32[]{:S(2)}) collective-permute-start(bf16[24,8,128]{2,1,0:T(8,128)(2,1)S(1)} %get-tuple-element.45), channel_id=1, source_target_pairs={{8,16},{16,8},{24,32},{32,24},{40,48},{48,40},{56,64},{64,56},{72,... | collective-permute-start | bytes 147464 | tf_op jit(solution)/shard_map/ppermute | solution.py:233
  12.6 6.0 %collective-permute-start.1 = (bf16[24,8,128]{2,1,0:T(8,128)(2,1)S(1)}, bf16[24,8,128]{2,1,0:T(8,128)(2,1)S(1)}, u32[]{:S(2)}, u32[]{:S(2)}) collective-permute-start(bf16[24,8,128]{2,1,0:T(8,128)(2,1)S(1)} %get-tuple-element.44), channel_id=1, source_target_pairs={{0,8},{8,0},{16,24},{24,16},{32,40},{40,32},{48,56},{56,48},{64,72... | collective-permute-start | bytes 147464 | tf_op jit(solution)/shard_map/ppermute | solution.py:232
  19.0 0.9 %copy-start = (bf16[27,64,16]{1,2,0:T(8,128)(2,1)S(1)}, bf16[27,64,16]{1,2,0:T(8,128)(2,1)}, u32[]{:S(2)}) copy-start(bf16[27,64,16]{1,2,0:T(8,128)(2,1)} %param.5) | copy-start | bytes 165892
  20.4 22.8 %collective-permute-start.2 = (bf16[9,2,8,8,128]{4,3,2,1,0:T(8,128)(2,1)S(1)}, bf16[9,2,8,8,128]{4,3,2,1,0:T(8,128)(2,1)S(1)}, u32[]{:S(2)}, u32[]{:S(2)}) collective-permute-start(bf16[9,2,8,8,128]{4,3,2,1,0:T(8,128)(2,1)S(1)} %get-tuple-element.26.sent_ref), channel_id=1, source_target_pairs={{0,2},{1,3},{2,0},{3,1},{4,6},{5,7},{6,4},{7,5},{8,10},{9,11},{10,... | collective-permute-start | bytes 884744 | tf_op jit(solution)/shard_map/ppermute | solution.py:278
  43.3 20.3 %collective-permute-start.3 = (bf16[6,2,8,8,128]{4,3,2,1,0:T(8,128)(2,1)S(1)}, bf16[6,2,8,8,128]{4,3,2,1,0:T(8,128)(2,1)S(1)}, u32[]{:S(2)}, u32[]{:S(2)}) collective-permute-start(bf16[6,2,8,8,128]{4,3,2,1,0:T(8,128)(2,1)S(1)} %get-tuple-element.30.sent_ref), channel_id=1, source_target_pairs={{0,1},{1,0},{2,3},{3,2},{4,5},{5,4},{6,7},{7,6},{8,9},{9,8},{10,11... | collective-permute-start | bytes 589832 | tf_op jit(solution)/shard_map/ppermute | solution.py:291
  64.3 11.3 %collective-permute-start.4 = (bf16[6,2,8,8,128]{4,3,2,1,0:T(8,128)(2,1)S(1)}, bf16[6,2,8,8,128]{4,3,2,1,0:T(8,128)(2,1)S(1)}, u32[]{:S(2)}, u32[]{:S(2)}) collective-permute-start(bf16[6,2,8,8,128]{4,3,2,1,0:T(8,128)(2,1)S(1)} %get-tuple-element.36.sent_ref), channel_id=1, source_target_pairs={{0,4},{1,5},{2,6},{3,7},{4,0},{5,1},{6,2},{7,3},{8,12},{9,13},{10,... | collective-permute-start | bytes 589832 | tf_op jit(solution)/shard_map/ppermute | solution.py:305
  68.9 11.5 %all-to-all-start.2 = ((f32[16,16,128]{2,1,0:T(8,128)}), f32[16,16,128]{2,1,0:T(8,128)S(1)}, u32[]{:S(2)}, u32[]{:S(2)}) async-start(f32[16,16,128]{2,1,0:T(8,128)} %get-tuple-element.34), calls=%async_computation.2 | async-start | bytes 262144 | tf_op jit(solution)/shard_map/all_to_all | solution.py:306
  72.5 0.7 copy-start.3

commit v7 on v6

--- a/solution.py
+++ b/solution.py
@@ -31,31 +31,41 @@
     return jnp.where(lane == edge, 0.0, turned)
 
 
-def weight_sums(odd_ref, vol_ref, grad_ref, outer_ref, inner_ref, sums_ref, gpad):
+def shifted(plane, target):
+    outs, rows, cols = plane.shape
+    blank = jnp.zeros((3 * outs, cols), BF16)
+    target[0] = blank
+    target[rows + 1] = blank
+    turned = jnp.swapaxes(plane, 0, 1)
+    for h in range(rows):
+        wide = turned[h]
+        target[h + 1, 0:outs] = slide(wide, 1).astype(BF16)
+        target[h + 1, outs : 2 * outs] = wide.astype(BF16)
+        target[h + 1, 2 * outs : 3 * outs] = slide(wide, -1).astype(BF16)
+
+
+def ready_planes(grad_ref, outer_ref, planes_ref, bias_ref):
+    outs, depth, rows, cols = grad_ref.shape
+    total = None
+    for d in range(depth):
+        plane = grad_ref[:, d].astype(F32)
+        shifted(plane, planes_ref.at[d])
+        part = jnp.sum(plane, axis=1)
+        total = part if total is None else total + part
+    shifted(outer_ref[0:outs].astype(F32), planes_ref.at[depth])
+    half = cols // 2
+    bias_ref[...] = total[:, :half] + total[:, half:]
+
+
+def weight_sums(odd_ref, vol_ref, planes_ref, bias_ref, inner_ref, sums_ref, gpad):
     peers, depth, rows, share, cols = vol_ref.shape
-    outs = grad_ref.shape[0]
+    outs = bias_ref.shape[0]
     chans = peers * share
-    odd = odd_ref[0] == 1
-    inner = inner_ref[0:outs].astype(F32)
-    outer = outer_ref[0:outs].astype(F32)
-    planes = [
-        jnp.where(odd, inner, outer),
-        *[grad_ref[:, d].astype(F32) for d in range(depth)],
-        jnp.where(odd, outer, inner),
-    ]
-    blank = jnp.zeros((3 * outs, cols), BF16)
-    bias_sum = jnp.zeros((outs, cols), F32)
-    for p in range(depth + 2):
-        gpad[p, 0] = blank
-        gpad[p, rows + 1] = blank
-        plane = jnp.swapaxes(planes[p], 0, 1)
-        for h in range(rows):
-            wide = plane[h]
-            if 0 < p < depth + 1:
-                bias_sum = bias_sum + wide
-            gpad[p, h + 1, 0:outs] = slide(wide, 1).astype(BF16)
-            gpad[p, h + 1, outs : 2 * outs] = wide.astype(BF16)
-            gpad[p, h + 1, 2 * outs : 3 * outs] = slide(wide, -1).astype(BF16)
+    odd = odd_ref[0]
+    for d in range(depth):
+        gpad[d + 1] = planes_ref[d]
+    gpad[(depth + 1) * odd] = planes_ref[depth]
+    shifted(inner_ref[0:outs].astype(F32), gpad.at[(depth + 1) * (1 - odd)])
     acc = jnp.zeros((27 * outs, chans), F32)
     for d in range(depth):
         for h in range(0, rows, 2):
@@ -67,11 +77,9 @@
                 axis=1,
             )
             acc = acc + dot_lanes(moved_rows(gpad, d, h), cells)
-    half = cols // 2
-    bias_half = bias_sum[:, :half] + bias_sum[:, half:]
     for r in range(14):
         first = acc[2 * r * outs : (2 * r + 1) * outs]
-        second = bias_half if r == 13 else acc[(2 * r + 1) * outs : (2 * r + 2) * outs]
+        second = bias_ref[...] if r == 13 else acc[(2 * r + 1) * outs : (2 * r + 2) * outs]
         sums_ref[r] = jnp.concatenate([first, second], axis=1)
     for r in range(14, 16):
         sums_ref[r] = jnp.zeros((outs, cols), F32)
@@ -253,6 +261,17 @@
     odd = odd.reshape(1)
     vol = lax.all_to_all(jnp.broadcast_to(own[None], (8,) + own.shape), "filt", 0, 0)
     block = (depth, rows, share, cols)
+    planes, bias_sums = pl.pallas_call(
+        ready_planes,
+        out_shape=(
+            jax.ShapeDtypeStruct((depth + 1, rows + 2, 3 * outs, cols), BF16),
+            jax.ShapeDtypeStruct((outs, cols // 2), F32),
+        ),
+        in_specs=[WHOLE] * 2,
+        out_specs=(WHOLE,) * 2,
+        compiler_params=PARAMS,
+        cost_estimate=pl.CostEstimate(flops=9_500_000_000, bytes_accessed=0, transcendentals=0),
+    )(grad_out, outer)
     sums, moved = pl.pallas_call(
         weight_sums,
         out_shape=(
@@ -262,7 +281,7 @@
         in_specs=[SCALAR] + [WHOLE] * 4,
         out_specs=(WHOLE,) * 2,
         compiler_params=PARAMS,
-    )(odd, vol, grad_out, outer, inner)
+    )(odd, vol, planes, bias_sums, inner)
     parts = lax.all_to_all(sums, "space", 0, 0, axis_index_groups=XY_GROUPS)
     keep, send = pl.pallas_call(
         shares_first,

time: 81.8 us -> 79.1 us (0.967)
  the two profiles are of different devices: /device:TPU:32 before, /device:TPU:2 now
where the time goes in v7:
time: 79.1 us; the launch traced here: 78.5 us
  blocking collectives  33.6 us (42%)
  starting transfers between devices  25.6 us (32%)
  waiting for transfers between devices  11.8 us (15%)
  Pallas kernels  4.33 us (5%)
  local copies, waits for them, and re-layouts  2.43 us (3%)
    all_to_all x1, blocking collectives, local(): parts = lax.all_to_all(sums, 'space', 0, 0, axis_index_groups=XY_GROUPS)  17 us
    psum x1, blocking collectives, local(): mine = lax.psum(mine, 'space', axis_index_groups=Z_GROUPS)  16.6 us
    all_to_all x1, starting transfers between devices, local(): lax.all_to_all(jnp.broadcast_to(own[None], (8,) + own.shape), 'filt', 0, 0)  6.03 us
    all_to_all x1, starting transfers between devices, local(): every = lax.all_to_all(spread, 'space', 0, 0, axis_index_groups=XY_GROUPS)  5.07 us
    ppermute x1, starting transfers between devices, swap_edges(): outer = lax.ppermute(jnp.where(odd, tail, head), 'space', ODD)  4.89 us
    ppermute x1, waiting for transfers between devices, swap_edges(): inner = lax.ppermute(jnp.where(odd, head, tail), 'space', EVEN)  3.78 us
    all_to_all x1, waiting for transfers between devices, local(): lax.all_to_all(jnp.broadcast_to(own[None], (8,) + own.shape), 'filt', 0, 0)  3.71 us
    ppermute x1, starting transfers between devices, local(): got = lax.ppermute(send, 'filt', swap_pairs(SWAPS[2]))  3.5 us
  transfers between devices with their start and end apart: 7, of which 4 were waited for; matrix products, arithmetic and copies ran while one was open for 1% of the time, Pallas kernels for 2%

profile of v7, /device:TPU:2, one launch (start us, length us, event | category | flops | bytes accessed | tf_op | source)
XLA Modules:
  0.0 78.5 jit_solution(1642411884695364388)
XLA Ops:
  0.6 0.0 copy-start.2
  0.6 0.8 %slice_bitcast_fusion.1 = (bf16[16,8,128]{2,1,0:T(8,128)(2,1)S(1)}, bf16[16,8,128]{2,1,0:T(8,128)(2,1)S(1)}) fusion(bf16[16,2,8,128]{3,2,1,0:T(8,128)(2,1)} %grad_ref.1), kind=kLoop, calls=%fused_computation.5 | loop fusion | bytes 131072 | tf_op jit(solution)/shard_map/squeeze | solution.py:258
  1.4 0.0 copy-done.2
  1.5 4.9 %collective-permute-start = (bf16[24,8,128]{2,1,0:T(8,128)(2,1)S(1)}, bf16[24,8,128]{2,1,0:T(8,128)(2,1)S(1)}, u32[]{:S(2)}, u32[]{:S(2)}) collective-permute-start(bf16[24,8,128]{2,1,0:T(8,128)(2,1)S(1)} %get-tuple-element.49), channel_id=1, source_target_pairs={{8,16},{16,8},{24,32},{32,24},{40,48},{48,40},{56,64},{64,56},{72,... | collective-permute-start | bytes 147464 | tf_op jit(solution)/shard_map/ppermute | solution.py:241
  6.4 0.7 broadcast_in_dim.4
  7.1 0.0 copy-start.1
  7.1 6.0 %all-to-all-start = ((bf16[8,2,8,8,128]{4,3,2,1,0:T(8,128)(2,1)}), bf16[8,2,8,8,128]{4,3,2,1,0:T(8,128)(2,1)S(1)}, u32[]{:S(2)}, u32[]{:S(2)}) async-start(bf16[8,2,8,8,128]{4,3,2,1,0:T(8,128)(2,1)} %broadcast_in_dim.4), calls=%async_computation | async-start | bytes 524288 | tf_op jit(solution)/shard_map/all_to_all | solution.py:262
  13.2 2.1 %collective-permute-start.1 = (bf16[24,8,128]{2,1,0:T(8,128)(2,1)S(1)}, bf16[24,8,128]{2,1,0:T(8,128)(2,1)S(1)}, u32[]{:S(2)}, u32[]{:S(2)}) collective-permute-start(bf16[24,8,128]{2,1,0:T(8,128)(2,1)S(1)} %get-tuple-element.48), channel_id=1, source_target_pairs={{0,8},{8,0},{16,24},{24,16},{32,40},{40,32},{48,56},{56,48},{64,72... | collective-permute-start | bytes 147464 | tf_op jit(solution)/shard_map/ppermute | solution.py:240
  15.2 0.0 collective-permute-done.outer_ref
  15.2 0.0 copy-done.1
  15.3 0.2 shard_map.75
  15.4 3.8 %collective-permute-done.1.inner_ref = bf16[24,8,128]{2,1,0:T(8,128)(2,1)S(1)} collective-permute-done((bf16[24,8,128]{2,1,0:T(8,128)(2,1)S(1)}, bf16[24,8,128]{2,1,0:T(8,128)(2,1)S(1)}, u32[]{:S(2)}, u32[]{:S(2)}) %collective-permute-start.1) | collective-permute-done | bytes 49184 | tf_op jit(solution)/shard_map/ppermute | solution.py:240
  19.2 3.7 %all-to-all-done.vol_ref = bf16[8,2,8,8,128]{4,3,2,1,0:T(8,128)(2,1)S(1)} async-done(((bf16[8,2,8,8,128]{4,3,2,1,0:T(8,128)(2,1)}), bf16[8,2,8,8,128]{4,3,2,1,0:T(8,128)(2,1)S(1)}, u32[]{:S(2)}, u32[]{:S(2)}) %all-to-all-start) | async-done | bytes 262176 | tf_op jit(solution)/shard_map/all_to_all | solution.py:262
  22.9 0.0 copy-start
  22.9 0.7 shard_map.76
  23.7 0.1 copy-done
  23.8 0.5 shard_map.77
  24.3 2.1 %collective-permute-start.2 = (bf16[9,2,8,8,128]{4,3,2,1,0:T(8,128)(2,1)S(1)}, bf16[9,2,8,8,128]{4,3,2,1,0:T(8,128)(2,1)S(1)}, u32[]{:S(2)}, u32[]{:S(2)}) collective-permute-start(bf16[9,2,8,8,128]{4,3,2,1,0:T(8,128)(2,1)S(1)} %get-tuple-element.30.sent_ref), channel_id=1, source_target_pairs={{0,2},{1,3},{2,0},{3,1},{4,6},{5,7},{6,4},{7,5},{8,10},{9,11},{10,... | collective-permute-start | bytes 884744 | tf_op jit(solution)/shard_map/ppermute | solution.py:297
  26.4 17.0 %all_to_all.15 = f32[16,16,128]{2,1,0:T(8,128)S(1)} all-to-all(f32[16,16,128]{2,1,0:T(8,128)S(1)} %get-tuple-element.31), channel_id=1, replica_groups={{0,8,16,24,32,40,48,56,64,72,80,88,96,104,112,120},{128,136,144,152,160..., dimensions={0} | all-to-all | bytes 262144 | tf_op jit(solution)/shard_map/all_to_all | solution.py:285
  43.4 0.0 collective-permute-done.2.got_ref
  43.5 0.1 shard_map.78
  43.5 1.9 %collective-permute-start.3 = (bf16[6,2,8,8,128]{4,3,2,1,0:T(8,128)(2,1)S(1)}, bf16[6,2,8,8,128]{4,3,2,1,0:T(8,128)(2,1)S(1)}, u32[]{:S(2)}, u32[]{:S(2)}) collective-permute-start(bf16[6,2,8,8,128]{4,3,2,1,0:T(8,128)(2,1)S(1)} %get-tuple-element.34.sent_ref), channel_id=1, source_target_pairs={{0,1},{1,0},{2,3},{3,2},{4,5},{5,4},{6,7},{7,6},{8,9},{9,8},{10,11... | collective-permute-start | bytes 589832 | tf_op jit(solution)/shard_map/ppermute | solution.py:310
  45.4 16.6 %psum.7.mine_ref = f32[16,128]{1,0:T(8,128)S(1)} all-reduce(f32[16,128]{1,0:T(8,128)S(1)} %reduce_sum.9), channel_id=1, replica_groups={{0,128,256,384},{8,136,264,392},{16,144,272,400},{24,152,280,408},{32,1..., use_global_device_ids=true, to_apply=%region_1.2 | all-reduce | flops 2048 | bytes 16384 | tf_op jit(solution)/shard_map/psum | solution.py:311
  62.0 0.0 collective-permute-done.3.got_ref
  62.0 0.7 shard_map.79
  62.7 3.5 %collective-permute-start.4 = (bf16[6,2,8,8,128]{4,3,2,1,0:T(8,128)(2,1)S(1)}, bf16[6,2,8,8,128]{4,3,2,1,0:T(8,128)(2,1)S(1)}, u32[]{:S(2)}, u32[]{:S(2)}) collective-permute-start(bf16[6,2,8,8,128]{4,3,2,1,0:T(8,128)(2,1)S(1)} %get-tuple-element.40.sent_ref), channel_id=1, source_target_pairs={{0,4},{1,5},{2,6},{3,7},{4,0},{5,1},{6,2},{7,3},{8,12},{9,13},{10,... | collective-permute-start | bytes 589832 | tf_op jit(solution)/shard_map/ppermute | solution.py:324
  66.2 5.1 %all-to-all-start.2 = ((f32[16,16,128]{2,1,0:T(8,128)}), f32[16,16,128]{2,1,0:T(8,128)S(1)}, u32[]{:S(2)}, u32[]{:S(2)}) async-start(f32[16,16,128]{2,1,0:T(8,128)} %get-tuple-element.38), calls=%async_computation.2 | async-start | bytes 262144 | tf_op jit(solution)/shard_map/all_to_all | solution.py:325
  71.3 0.0 copy-start.3
  71.3 0.6 copy-done.3
  72.0 0.1 copy.13.bias_ref
  72.0 2.8 %collective-permute-done.4.got_ref = bf16[6,2,8,8,128]{4,3,2,1,0:T(8,128)(2,1)S(1)} collective-permute-done((bf16[6,2,8,8,128]{4,3,2,1,0:T(8,128)(2,1)S(1)}, bf16[6,2,8,8,128]{4,3,2,1,0:T(8,128)(2,1)S(1)}, u32[]{:S(2)}, u32[]{:S(2)}) %collective-permute-start.4) | collective-permute-done | bytes 196640 | tf_op jit(solution)/shard_map/ppermute | solution.py:324
  74.9 1.3 %shard_map.80 = (bf16[16,2,8,128]{3,2,1,0:T(8,128)(2,1)}, bf16[8,2,8,128]{3,2,1,0:T(8,128)(2,1)}) custom-call(s32[1]{0:T(128)} %bitcast.1.me_ref, bf16[8,2,8,8,128]{4,3,2,1,0:T(8,128)(2,1)S(1)} %all-to-all-done.vol_ref, f32[1,2,8,8,128]{4,3,2,1,0:T(8,128)S(1)} %get-tuple-element.39.keep_ref, bf16[6,2,8,8,128]{4,3,2,1,0:T(8,128)(2,1)S(1)} %get-tuple-element.40.sent_ref, ...), custom_call_target="tpu_custom_call" | custom-call | tf_op jit(solution)/shard_map/pallas_call | solution.py:326
  76.2 1.5 %all-to-all-done.2.refs_0_ = f32[16,16,128]{2,1,0:T(8,128)S(1)} async-done(((f32[16,16,128]{2,1,0:T(8,128)}), f32[16,16,128]{2,1,0:T(8,128)S(1)}, u32[]{:S(2)}, u32[]{:S(2)}) %all-to-all-start.2) | async-done | bytes 131104 | tf_op jit(solution)/shard_map/all_to_all | solution.py:325
  77.7 0.8 %shard_map.81 = (f32[27,16,64]{2,1,0:T(8,128)}, f32[1,16]{1,0:T(1,128)}) custom-call(f32[16,16,128]{2,1,0:T(8,128)S(1)} %all-to-all-done.2.refs_0_), custom_call_target="tpu_custom_call" | custom-call | tf_op jit(solution)/shard_map/pallas_call | solution.py:342
  (4 shorter events, 0.0 us)
Async XLA Ops:
  0.6 0.8 %copy-start.2 = (bf16[8,2,8,128]{3,2,1,0:T(8,128)(2,1)S(1)}, bf16[8,2,8,128]{3,2,1,0:T(8,128)(2,1)}, u32[]{:S(2)}) copy-start(bf16[8,2,8,128]{3,2,1,0:T(8,128)(2,1)} %param.4) | copy-start | bytes 98308
  1.5 13.8 %collective-permute-start = (bf16[24,8,128]{2,1,0:T(8,128)(2,1)S(1)}, bf16[24,8,128]{2,1,0:T(8,128)(2,1)S(1)}, u32[]{:S(2)}, u32[]{:S(2)}) collective-permute-start(bf16[24,8,128]{2,1,0:T(8,128)(2,1)S(1)} %get-tuple-element.49), channel_id=1, source_target_pairs={{8,16},{16,8},{24,32},{32,24},{40,48},{48,40},{56,64},{64,56},{72,... | collective-permute-start | bytes 147464 | tf_op jit(solution)/shard_map/ppermute | solution.py:241
  7.1 8.1 %copy-start.1 = (bf16[16,2,8,128]{3,2,1,0:T(8,128)(2,1)S(1)}, bf16[16,2,8,128]{3,2,1,0:T(8,128)(2,1)}, u32[]{:S(2)}) copy-start(bf16[16,2,8,128]{3,2,1,0:T(8,128)(2,1)} %grad_ref.1) | copy-start | bytes 196612
  7.1 15.8 %all-to-all-start = ((bf16[8,2,8,8,128]{4,3,2,1,0:T(8,128)(2,1)}), bf16[8,2,8,8,128]{4,3,2,1,0:T(8,128)(2,1)S(1)}, u32[]{:S(2)}, u32[]{:S(2)}) async-start(bf16[8,2,8,8,128]{4,3,2,1,0:T(8,128)(2,1)} %broadcast_in_dim.4), calls=%async_computation | async-start | bytes 524288 | tf_op jit(solution)/shard_map/all_to_all | solution.py:262
  13.2 6.0 %collective-permute-start.1 = (bf16[24,8,128]{2,1,0:T(8,128)(2,1)S(1)}, bf16[24,8,128]{2,1,0:T(8,128)(2,1)S(1)}, u32[]{:S(2)}, u32[]{:S(2)}) collective-permute-start(bf16[24,8,128]{2,1,0:T(8,128)(2,1)S(1)} %get-tuple-element.48), channel_id=1, source_target_pairs={{0,8},{8,0},{16,24},{24,16},{32,40},{40,32},{48,56},{56,48},{64,72... | collective-permute-start | bytes 147464 | tf_op jit(solution)/shard_map/ppermute | solution.py:240
  22.9 0.9 %copy-start = (bf16[27,64,16]{1,2,0:T(8,128)(2,1)S(1)}, bf16[27,64,16]{1,2,0:T(8,128)(2,1)}, u32[]{:S(2)}) copy-start(bf16[27,64,16]{1,2,0:T(8,128)(2,1)} %param.5) | copy-start | bytes 165892
  24.3 19.1 %collective-permute-start.2 = (bf16[9,2,8,8,128]{4,3,2,1,0:T(8,128)(2,1)S(1)}, bf16[9,2,8,8,128]{4,3,2,1,0:T(8,128)(2,1)S(1)}, u32[]{:S(2)}, u32[]{:S(2)}) collective-permute-start(bf16[9,2,8,8,128]{4,3,2,1,0:T(8,128)(2,1)S(1)} %get-tuple-element.30.sent_ref), channel_id=1, source_target_pairs={{0,2},{1,3},{2,0},{3,1},{4,6},{5,7},{6,4},{7,5},{8,10},{9,11},{10,... | collective-permute-start | bytes 884744 | tf_op jit(solution)/shard_map/ppermute | solution.py:297
  43.5 18.5 %collective-permute-start.3 = (bf16[6,2,8,8,128]{4,3,2,1,0:T(8,128)(2,1)S(1)}, bf16[6,2,8,8,128]{4,3,2,1,0:T(8,128)(2,1)S(1)}, u32[]{:S(2)}, u32[]{:S(2)}) collective-permute-start(bf16[6,2,8,8,128]{4,3,2,1,0:T(8,128)(2,1)S(1)} %get-tuple-element.34.sent_ref), channel_id=1, source_target_pairs={{0,1},{1,0},{2,3},{3,2},{4,5},{5,4},{6,7},{7,6},{8,9},{9,8},{10,11... | collective-permute-start | bytes 589832 | tf_op jit(solution)/shard_map/ppermute | solution.py:310
  62.7 12.2 %collective-permute-start.4 = (bf16[6,2,8,8,128]{4,3,2,1,0:T(8,128)(2,1)S(1)}, bf16[6,2,8,8,128]{4,3,2,1,0:T(8,128)(2,1)S(1)}, u32[]{:S(2)}, u32[]{:S(2)}) collective-permute-start(bf16[6,2,8,8,128]{4,3,2,1,0:T(8,128)(2,1)S(1)} %get-tuple-element.40.sent_ref), channel_id=1, source_target_pairs={{0,4},{1,5},{2,6},{3,7},{4,0},{5,1},{6,2},{7,3},{8,12},{9,13},{10,... | collective-permute-start | bytes 589832 | tf_op jit(solution)/shard_map/ppermute | solution.py:324
  66.2 11.5 %all-to-all-start.2 = ((f32[16,16,128]{2,1,0:T(8,128)}), f32[16,16,128]{2,1,0:T(8,128)S(1)}, u32[]{:S(2)}, u32[]{:S(2)}) async-start(f32[16,16,128]{2,1,0:T(8,128)} %get-tuple-element.38), calls=%async_computation.2 | async-start | bytes 262144 | tf_op jit(solution)/shard_map/all_to_all | solution.py:325
  71.3 0.7 copy-start.3

commit v8 on v7

--- a/solution.py
+++ b/solution.py
@@ -57,15 +57,10 @@
     bias_ref[...] = total[:, :half] + total[:, half:]
 
 
-def weight_sums(odd_ref, vol_ref, planes_ref, bias_ref, inner_ref, sums_ref, gpad):
+def weight_sums(vol_ref, gpad, bias_ref, sums_ref):
     peers, depth, rows, share, cols = vol_ref.shape
     outs = bias_ref.shape[0]
     chans = peers * share
-    odd = odd_ref[0]
-    for d in range(depth):
-        gpad[d + 1] = planes_ref[d]
-    gpad[(depth + 1) * odd] = planes_ref[depth]
-    shifted(inner_ref[0:outs].astype(F32), gpad.at[(depth + 1) * (1 - odd)])
     acc = jnp.zeros((27 * outs, chans), F32)
     for d in range(depth):
         for h in range(0, rows, 2):
@@ -103,10 +98,14 @@
 
 
 def shares_first(
-    odd_ref, me_ref, moved_ref, taps_ref, outer_ref, inner_ref, keep_ref, send_ref, turned
+    odd_ref, me_ref, planes_ref, taps_ref, outer_ref, inner_ref, gpad, keep_ref, send_ref, turned
 ):
     _, depth, rows, share, cols = keep_ref.shape
     outs, chans = taps_ref.shape[1:]
+    for d in range(depth):
+        gpad[d + 1] = planes_ref[d]
+    gpad[(depth + 1) * odd_ref[0]] = planes_ref[depth]
+    shifted(inner_ref[0:outs].astype(F32), gpad.at[(depth + 1) * (1 - odd_ref[0])])
     turned[...] = taps_ref[...].reshape(27 * outs, chans).astype(F32).T
     me = me_ref[0]
     behind = jnp.concatenate(
@@ -118,7 +117,7 @@
     ).astype(BF16)
     for d in range(depth):
         for h in range(0, rows, 2):
-            back = dot(behind, moved_rows(moved_ref, d, h))
+            back = dot(behind, moved_rows(gpad, d, h))
             for k in range(2):
                 for r in range(8):
                     value = back[share * r : share * (r + 1), k * cols : (k + 1) * cols]
@@ -133,6 +132,10 @@
     outer = outer_ref[outs : outs + share].astype(F32)
     send_ref[8, 0] = jnp.swapaxes(jnp.where(odd, inner, outer), 0, 1).astype(BF16)
     send_ref[8, 1] = jnp.swapaxes(jnp.where(odd, outer, inner), 0, 1).astype(BF16)
+
+
+def add_parts(parts_ref, mine_ref):
+    mine_ref[...] = jnp.sum(parts_ref[...], axis=0)
 
 
 def shares_next(keep_ref, sent_ref, got_ref, kept_ref, send_ref):
@@ -228,7 +231,7 @@
     bias_ref[...] = flat[:, :outs]
 
 
-SWAPS = (2, 1, 4)
+SWAPS = (2, 4, 1)
 ORDER = [sum(bit for k, bit in enumerate(SWAPS) if n & (4 >> k)) for n in range(8)]
 XY_GROUPS = [[16 * z + k for k in range(16)] for z in range(4)]
 Z_GROUPS = [[16 * z + k for z in range(4)] for k in range(16)]
@@ -272,32 +275,29 @@
         compiler_params=PARAMS,
         cost_estimate=pl.CostEstimate(flops=9_500_000_000, bytes_accessed=0, transcendentals=0),
     )(grad_out, outer)
-    sums, moved = pl.pallas_call(
+    moved, keep, send = pl.pallas_call(
+        shares_first,
+        out_shape=(
+            jax.ShapeDtypeStruct((depth + 2, rows + 2, 3 * outs, cols), BF16),
+            jax.ShapeDtypeStruct((4,) + block, F32),
+            jax.ShapeDtypeStruct((9,) + block, BF16),
+        ),
+        in_specs=[SCALAR] * 2 + [WHOLE] * 4,
+        out_specs=(WHOLE,) * 3,
+        scratch_shapes=[pltpu.VMEM((chans, 27 * outs), F32)],
+        compiler_params=PARAMS,
+    )(odd, me, planes, taps, outer, inner)
+    got = lax.ppermute(send, "filt", swap_pairs(SWAPS[0]))
+    sums = pl.pallas_call(
         weight_sums,
-        out_shape=(
-            jax.ShapeDtypeStruct((16, outs, cols), F32),
-            jax.ShapeDtypeStruct((depth + 2, rows + 2, 3 * outs, cols), BF16),
-        ),
-        in_specs=[SCALAR] + [WHOLE] * 4,
-        out_specs=(WHOLE,) * 2,
-        compiler_params=PARAMS,
-    )(odd, vol, planes, bias_sums, inner)
+        out_shape=jax.ShapeDtypeStruct((16, outs, cols), F32),
+        in_specs=[WHOLE] * 3,
+        out_specs=WHOLE,
+        compiler_params=PARAMS,
+        cost_estimate=pl.CostEstimate(flops=6_000_000_000, bytes_accessed=0, transcendentals=0),
+    )(vol, moved, bias_sums)
     parts = lax.all_to_all(sums, "space", 0, 0, axis_index_groups=XY_GROUPS)
     keep, send = pl.pallas_call(
-        shares_first,
-        out_shape=(
-            jax.ShapeDtypeStruct((4,) + block, F32),
-            jax.ShapeDtypeStruct((9,) + block, BF16),
-        ),
-        in_specs=[SCALAR] * 2 + [WHOLE] * 4,
-        out_specs=(WHOLE,) * 2,
-        scratch_shapes=[pltpu.VMEM((chans, 27 * outs), F32)],
-        compiler_params=PARAMS,
-    )(odd, me, moved, taps, outer, inner)
-    got = lax.ppermute(send, "filt", swap_pairs(SWAPS[0]))
-    mine = jnp.sum(parts, axis=0)
-    mine, got = lax.optimization_barrier((mine, got))
-    keep, send = pl.pallas_call(
         shares_next,
         out_shape=(
             jax.ShapeDtypeStruct((2,) + block, F32),
@@ -306,8 +306,17 @@
         in_specs=[WHOLE] * 3,
         out_specs=(WHOLE,) * 2,
         compiler_params=PARAMS,
+        cost_estimate=pl.CostEstimate(flops=1000, bytes_accessed=0, transcendentals=0),
     )(keep, send, got)
     got = lax.ppermute(send, "filt", swap_pairs(SWAPS[1]))
+    mine = pl.pallas_call(
+        add_parts,
+        out_shape=jax.ShapeDtypeStruct((outs, cols), F32),
+        in_specs=[WHOLE],
+        out_specs=WHOLE,
+        compiler_params=PARAMS,
+        cost_estimate=pl.CostEstimate(flops=10_000_000_000, bytes_accessed=0, transcendentals=0),
+    )(parts)
     mine = lax.psum(mine, "space", axis_index_groups=Z_GROUPS)
     mine, got = lax.optimization_barrier((mine, got))
     keep, send, spread = pl.pallas_call(

time: 79.1 us -> 76.2 us (0.963)
  the two profiles are of different devices: /device:TPU:2 before, /device:TPU:1 now
where the time goes in v8:
time: 76.2 us; the launch traced here: 75.6 us
  starting transfers between devices  41.4 us (54%)
  blocking collectives  15.4 us (20%)
  waiting for transfers between devices  10.7 us (14%)
  Pallas kernels  4.98 us (7%)
  local copies, waits for them, and re-layouts  2.29 us (3%)
  between operations  0.8 us (1%)
    psum x1, blocking collectives, local(): mine = lax.psum(mine, 'space', axis_index_groups=Z_GROUPS)  15.4 us
    all_to_all x1, starting transfers between devices, local(): lax.all_to_all(jnp.broadcast_to(own[None], (8,) + own.shape), 'filt', 0, 0)  10.3 us
    all_to_all x1, starting transfers between devices, local(): parts = lax.all_to_all(sums, 'space', 0, 0, axis_index_groups=XY_GROUPS)  10 us
    ppermute x1, starting transfers between devices, local(): got = lax.ppermute(send, 'filt', swap_pairs(SWAPS[2]))  6.57 us
    all_to_all x1, waiting for transfers between devices, local(): every = lax.all_to_all(spread, 'space', 0, 0, axis_index_groups=XY_GROUPS)  4.63 us
    ppermute x1, starting transfers between devices, local(): got = lax.ppermute(send, 'filt', swap_pairs(SWAPS[1]))  3.76 us
    all_to_all x1, starting transfers between devices, local(): every = lax.all_to_all(spread, 'space', 0, 0, axis_index_groups=XY_GROUPS)  3.52 us
    ppermute x1, starting transfers between devices, local(): got = lax.ppermute(send, 'filt', swap_pairs(SWAPS[0]))  3.3 us
  transfers between devices with their start and end apart: 8, of which 4 were waited for; matrix products, arithmetic and copies ran while one was open for 1% of the time, Pallas kernels for 5%

profile of v8, /device:TPU:1, one launch (start us, length us, event | category | flops | bytes accessed | tf_op | source)
XLA Modules:
  0.0 75.6 jit_solution(2157798100467681347)
XLA Ops:
  0.6 0.0 copy-start.2
  0.6 0.8 %slice_bitcast_fusion.1 = (bf16[16,8,128]{2,1,0:T(8,128)(2,1)S(1)}, bf16[16,8,128]{2,1,0:T(8,128)(2,1)S(1)}) fusion(bf16[16,2,8,128]{3,2,1,0:T(8,128)(2,1)} %grad_ref.1), kind=kLoop, calls=%fused_computation.5 | loop fusion | bytes 131072 | tf_op jit(solution)/shard_map/squeeze | solution.py:261
  1.4 0.0 copy-done.2
  1.5 0.7 collective-permute-start
  2.2 0.7 broadcast_in_dim.4
  2.9 0.0 copy-start.1
  2.9 10.3 %all-to-all-start = ((bf16[8,2,8,8,128]{4,3,2,1,0:T(8,128)(2,1)}), bf16[8,2,8,8,128]{4,3,2,1,0:T(8,128)(2,1)S(1)}, u32[]{:S(2)}, u32[]{:S(2)}) async-start(bf16[8,2,8,8,128]{4,3,2,1,0:T(8,128)(2,1)} %broadcast_in_dim.4), calls=%async_computation | async-start | bytes 524288 | tf_op jit(solution)/shard_map/all_to_all | solution.py:265
  13.2 3.2 %collective-permute-start.1 = (bf16[24,8,128]{2,1,0:T(8,128)(2,1)S(1)}, bf16[24,8,128]{2,1,0:T(8,128)(2,1)S(1)}, u32[]{:S(2)}, u32[]{:S(2)}) collective-permute-start(bf16[24,8,128]{2,1,0:T(8,128)(2,1)S(1)} %get-tuple-element.42), channel_id=1, source_target_pairs={{0,8},{8,0},{16,24},{24,16},{32,40},{40,32},{48,56},{56,48},{64,72... | collective-permute-start | bytes 147464 | tf_op jit(solution)/shard_map/ppermute | solution.py:243
  16.5 0.0 copy-start
  16.5 0.0 collective-permute-done.outer_ref
  16.5 0.0 copy-done.1
  16.5 0.2 shard_map.75
  16.7 1.7 %collective-permute-done.1.inner_ref = bf16[24,8,128]{2,1,0:T(8,128)(2,1)S(1)} collective-permute-done((bf16[24,8,128]{2,1,0:T(8,128)(2,1)S(1)}, bf16[24,8,128]{2,1,0:T(8,128)(2,1)S(1)}, u32[]{:S(2)}, u32[]{:S(2)}) %collective-permute-start.1) | collective-permute-done | bytes 49184 | tf_op jit(solution)/shard_map/ppermute | solution.py:243
  18.3 0.0 copy-done
  18.3 0.6 shard_map.76
  18.9 3.3 %collective-permute-start.2 = (bf16[9,2,8,8,128]{4,3,2,1,0:T(8,128)(2,1)S(1)}, bf16[9,2,8,8,128]{4,3,2,1,0:T(8,128)(2,1)S(1)}, u32[]{:S(2)}, u32[]{:S(2)}) collective-permute-start(bf16[9,2,8,8,128]{4,3,2,1,0:T(8,128)(2,1)S(1)} %get-tuple-element.25.sent_ref), channel_id=1, source_target_pairs={{0,2},{1,3},{2,0},{3,1},{4,6},{5,7},{6,4},{7,5},{8,10},{9,11},{10,... | collective-permute-start | bytes 884744 | tf_op jit(solution)/shard_map/ppermute | solution.py:290
  22.2 1.5 %all-to-all-done.vol_ref = bf16[8,2,8,8,128]{4,3,2,1,0:T(8,128)(2,1)S(1)} async-done(((bf16[8,2,8,8,128]{4,3,2,1,0:T(8,128)(2,1)}), bf16[8,2,8,8,128]{4,3,2,1,0:T(8,128)(2,1)S(1)}, u32[]{:S(2)}, u32[]{:S(2)}) %all-to-all-start) | async-done | bytes 262176 | tf_op jit(solution)/shard_map/all_to_all | solution.py:265
  23.7 1.3 %shard_map.78 = f32[16,16,128]{2,1,0:T(8,128)} custom-call(bf16[8,2,8,8,128]{4,3,2,1,0:T(8,128)(2,1)S(1)} %all-to-all-done.vol_ref, bf16[4,10,48,128]{3,2,1,0:T(8,128)(2,1)S(1)} %get-tuple-element.28.gpad, f32[16,64]{1,0:T(8,128)S(1)} %get-tuple-element.29.bias_ref), custom_call_target="tpu_custom_call" | custom-call | flops 6000000000 | tf_op jit(solution)/shard_map/pallas_call | solution.py:291
  25.1 10.0 %all-to-all-start.1 = ((f32[16,16,128]{2,1,0:T(8,128)}), f32[16,16,128]{2,1,0:T(8,128)S(1)}, u32[]{:S(2)}, u32[]{:S(2)}) async-start(f32[16,16,128]{2,1,0:T(8,128)} %shard_map.78), calls=%async_computation.1 | async-start | bytes 262144 | tf_op jit(solution)/shard_map/all_to_all | solution.py:299
  35.1 0.0 collective-permute-done.2.got_ref
  35.1 0.1 shard_map.77
  35.2 3.8 %collective-permute-start.3 = (bf16[6,2,8,8,128]{4,3,2,1,0:T(8,128)(2,1)S(1)}, bf16[6,2,8,8,128]{4,3,2,1,0:T(8,128)(2,1)S(1)}, u32[]{:S(2)}, u32[]{:S(2)}) collective-permute-start(bf16[6,2,8,8,128]{4,3,2,1,0:T(8,128)(2,1)S(1)} %get-tuple-element.27.sent_ref), channel_id=1, source_target_pairs={{0,4},{1,5},{2,6},{3,7},{4,0},{5,1},{6,2},{7,3},{8,12},{9,13},{10,... | collective-permute-start | bytes 589832 | tf_op jit(solution)/shard_map/ppermute | solution.py:311
  39.0 2.9 %all-to-all-done.1.parts_ref = f32[16,16,128]{2,1,0:T(8,128)S(1)} async-done(((f32[16,16,128]{2,1,0:T(8,128)}), f32[16,16,128]{2,1,0:T(8,128)S(1)}, u32[]{:S(2)}, u32[]{:S(2)}) %all-to-all-start.1) | async-done | bytes 131104 | tf_op jit(solution)/shard_map/all_to_all | solution.py:299
  41.9 15.4 %psum.7.mine_ref = f32[16,128]{1,0:T(8,128)S(1)} all-reduce(f32[16,128]{1,0:T(8,128)S(1)} %shard_map.79), channel_id=1, replica_groups={{0,128,256,384},{8,136,264,392},{16,144,272,400},{24,152,280,408},{32,1..., use_global_device_ids=true, to_apply=%region_0.1 | all-reduce | flops 2048 | bytes 16384 | tf_op jit(solution)/shard_map/psum | solution.py:320
  57.3 0.0 collective-permute-done.3.got_ref
  57.3 0.7 shard_map.80
  58.0 6.6 %collective-permute-start.4 = (bf16[6,2,8,8,128]{4,3,2,1,0:T(8,128)(2,1)S(1)}, bf16[6,2,8,8,128]{4,3,2,1,0:T(8,128)(2,1)S(1)}, u32[]{:S(2)}, u32[]{:S(2)}) collective-permute-start(bf16[6,2,8,8,128]{4,3,2,1,0:T(8,128)(2,1)S(1)} %get-tuple-element.34.sent_ref), channel_id=1, source_target_pairs={{0,1},{1,0},{2,3},{3,2},{4,5},{5,4},{6,7},{7,6},{8,9},{9,8},{10,11... | collective-permute-start | bytes 589832 | tf_op jit(solution)/shard_map/ppermute | solution.py:333
  64.5 3.5 %all-to-all-start.2 = ((f32[16,16,128]{2,1,0:T(8,128)}), f32[16,16,128]{2,1,0:T(8,128)S(1)}, u32[]{:S(2)}, u32[]{:S(2)}) async-start(f32[16,16,128]{2,1,0:T(8,128)} %get-tuple-element.32), calls=%async_computation.2 | async-start | bytes 262144 | tf_op jit(solution)/shard_map/all_to_all | solution.py:334
  68.1 0.0 copy-start.3
  68.1 0.6 copy-done.3
  68.7 0.1 copy.13.bias_ref
  68.8 0.0 collective-permute-done.4.got_ref
  68.8 1.3 %shard_map.81 = (bf16[16,2,8,128]{3,2,1,0:T(8,128)(2,1)}, bf16[8,2,8,128]{3,2,1,0:T(8,128)(2,1)}) custom-call(s32[1]{0:T(128)} %bitcast.1.me_ref, bf16[8,2,8,8,128]{4,3,2,1,0:T(8,128)(2,1)S(1)} %all-to-all-done.vol_ref, f32[1,2,8,8,128]{4,3,2,1,0:T(8,128)S(1)} %get-tuple-element.33.keep_ref, bf16[6,2,8,8,128]{4,3,2,1,0:T(8,128)(2,1)S(1)} %get-tuple-element.34.sent_ref, ...), custom_call_target="tpu_custom_call" | custom-call | tf_op jit(solution)/shard_map/pallas_call | solution.py:335
  70.1 4.6 %all-to-all-done.2.refs_0_ = f32[16,16,128]{2,1,0:T(8,128)S(1)} async-done(((f32[16,16,128]{2,1,0:T(8,128)}), f32[16,16,128]{2,1,0:T(8,128)S(1)}, u32[]{:S(2)}, u32[]{:S(2)}) %all-to-all-start.2) | async-done | bytes 131104 | tf_op jit(solution)/shard_map/all_to_all | solution.py:334
  74.8 0.8 %shard_map.82 = (f32[27,16,64]{2,1,0:T(8,128)}, f32[1,16]{1,0:T(1,128)}) custom-call(f32[16,16,128]{2,1,0:T(8,128)S(1)} %all-to-all-done.2.refs_0_), custom_call_target="tpu_custom_call" | custom-call | tf_op jit(solution)/shard_map/pallas_call | solution.py:351
  (4 shorter events, 0.0 us)
Async XLA Ops:
  0.6 0.8 %copy-start.2 = (bf16[8,2,8,128]{3,2,1,0:T(8,128)(2,1)S(1)}, bf16[8,2,8,128]{3,2,1,0:T(8,128)(2,1)}, u32[]{:S(2)}) copy-start(bf16[8,2,8,128]{3,2,1,0:T(8,128)(2,1)} %param.4) | copy-start | bytes 98308
  1.5 15.0 %collective-permute-start = (bf16[24,8,128]{2,1,0:T(8,128)(2,1)S(1)}, bf16[24,8,128]{2,1,0:T(8,128)(2,1)S(1)}, u32[]{:S(2)}, u32[]{:S(2)}) collective-permute-start(bf16[24,8,128]{2,1,0:T(8,128)(2,1)S(1)} %get-tuple-element.43), channel_id=1, source_target_pairs={{8,16},{16,8},{24,32},{32,24},{40,48},{48,40},{56,64},{64,56},{72,... | collective-permute-start | bytes 147464 | tf_op jit(solution)/shard_map/ppermute | solution.py:244
  2.9 13.6 %copy-start.1 = (bf16[16,2,8,128]{3,2,1,0:T(8,128)(2,1)S(1)}, bf16[16,2,8,128]{3,2,1,0:T(8,128)(2,1)}, u32[]{:S(2)}) copy-start(bf16[16,2,8,128]{3,2,1,0:T(8,128)(2,1)} %grad_ref.1) | copy-start | bytes 196612
  2.9 20.8 %all-to-all-start = ((bf16[8,2,8,8,128]{4,3,2,1,0:T(8,128)(2,1)}), bf16[8,2,8,8,128]{4,3,2,1,0:T(8,128)(2,1)S(1)}, u32[]{:S(2)}, u32[]{:S(2)}) async-start(bf16[8,2,8,8,128]{4,3,2,1,0:T(8,128)(2,1)} %broadcast_in_dim.4), calls=%async_computation | async-start | bytes 524288 | tf_op jit(solution)/shard_map/all_to_all | solution.py:265
  13.2 5.1 %collective-permute-start.1 = (bf16[24,8,128]{2,1,0:T(8,128)(2,1)S(1)}, bf16[24,8,128]{2,1,0:T(8,128)(2,1)S(1)}, u32[]{:S(2)}, u32[]{:S(2)}) collective-permute-start(bf16[24,8,128]{2,1,0:T(8,128)(2,1)S(1)} %get-tuple-element.42), channel_id=1, source_target_pairs={{0,8},{8,0},{16,24},{24,16},{32,40},{40,32},{48,56},{56,48},{64,72... | collective-permute-start | bytes 147464 | tf_op jit(solution)/shard_map/ppermute | solution.py:243
  16.5 1.9 %copy-start = (bf16[27,64,16]{1,2,0:T(8,128)(2,1)S(1)}, bf16[27,64,16]{1,2,0:T(8,128)(2,1)}, u32[]{:S(2)}) copy-start(bf16[27,64,16]{1,2,0:T(8,128)(2,1)} %param.5) | copy-start | bytes 165892
  18.9 16.2 %collective-permute-start.2 = (bf16[9,2,8,8,128]{4,3,2,1,0:T(8,128)(2,1)S(1)}, bf16[9,2,8,8,128]{4,3,2,1,0:T(8,128)(2,1)S(1)}, u32[]{:S(2)}, u32[]{:S(2)}) collective-permute-start(bf16[9,2,8,8,128]{4,3,2,1,0:T(8,128)(2,1)S(1)} %get-tuple-element.25.sent_ref), channel_id=1, source_target_pairs={{0,2},{1,3},{2,0},{3,1},{4,6},{5,7},{6,4},{7,5},{8,10},{9,11},{10,... | collective-permute-start | bytes 884744 | tf_op jit(solution)/shard_map/ppermute | solution.py:290
  25.1 16.8 %all-to-all-start.1 = ((f32[16,16,128]{2,1,0:T(8,128)}), f32[16,16,128]{2,1,0:T(8,128)S(1)}, u32[]{:S(2)}, u32[]{:S(2)}) async-start(f32[16,16,128]{2,1,0:T(8,128)} %shard_map.78), calls=%async_computation.1 | async-start | bytes 262144 | tf_op jit(solution)/shard_map/all_to_all | solution.py:299
  35.2 22.1 %collective-permute-start.3 = (bf16[6,2,8,8,128]{4,3,2,1,0:T(8,128)(2,1)S(1)}, bf16[6,2,8,8,128]{4,3,2,1,0:T(8,128)(2,1)S(1)}, u32[]{:S(2)}, u32[]{:S(2)}) collective-permute-start(bf16[6,2,8,8,128]{4,3,2,1,0:T(8,128)(2,1)S(1)} %get-tuple-element.27.sent_ref), channel_id=1, source_target_pairs={{0,4},{1,5},{2,6},{3,7},{4,0},{5,1},{6,2},{7,3},{8,12},{9,13},{10,... | collective-permute-start | bytes 589832 | tf_op jit(solution)/shard_map/ppermute | solution.py:311
  58.0 10.9 %collective-permute-start.4 = (bf16[6,2,8,8,128]{4,3,2,1,0:T(8,128)(2,1)S(1)}, bf16[6,2,8,8,128]{4,3,2,1,0:T(8,128)(2,1)S(1)}, u32[]{:S(2)}, u32[]{:S(2)}) collective-permute-start(bf16[6,2,8,8,128]{4,3,2,1,0:T(8,128)(2,1)S(1)} %get-tuple-element.34.sent_ref), channel_id=1, source_target_pairs={{0,1},{1,0},{2,3},{3,2},{4,5},{5,4},{6,7},{7,6},{8,9},{9,8},{10,11... | collective-permute-start | bytes 589832 | tf_op jit(solution)/shard_map/ppermute | solution.py:333
  64.5 10.2 %all-to-all-start.2 = ((f32[16,16,128]{2,1,0:T(8,128)}), f32[16,16,128]{2,1,0:T(8,128)S(1)}, u32[]{:S(2)}, u32[]{:S(2)}) async-start(f32[16,16,128]{2,1,0:T(8,128)} %get-tuple-element.32), calls=%async_computation.2 | async-start | bytes 262144 | tf_op jit(solution)/shard_map/all_to_all | solution.py:334
  68.1 0.7 copy-start.3

commit v9 on v8

--- a/solution.py
+++ b/solution.py
@@ -98,16 +98,17 @@
 
 
 def shares_first(
-    odd_ref, me_ref, planes_ref, taps_ref, outer_ref, inner_ref, gpad, keep_ref, send_ref, turned
+    planes_ref, taps_ref, outer_ref, inner_ref, gpad, keep_ref, send_ref, turned
 ):
     _, depth, rows, share, cols = keep_ref.shape
     outs, chans = taps_ref.shape[1:]
     for d in range(depth):
         gpad[d + 1] = planes_ref[d]
-    gpad[(depth + 1) * odd_ref[0]] = planes_ref[depth]
-    shifted(inner_ref[0:outs].astype(F32), gpad.at[(depth + 1) * (1 - odd_ref[0])])
+    parity = jnp.bitwise_and(lax.axis_index("space"), 1)
+    gpad[(depth + 1) * parity] = planes_ref[depth]
+    shifted(inner_ref[0:outs].astype(F32), gpad.at[(depth + 1) * (1 - parity)])
     turned[...] = taps_ref[...].reshape(27 * outs, chans).astype(F32).T
-    me = me_ref[0]
+    me = lax.axis_index("filt")
     behind = jnp.concatenate(
         [
             turned[pl.ds(pl.multiple_of(share * jnp.bitwise_xor(me, r), share), share)]
@@ -127,7 +128,7 @@
                         high, low = split(value)
                         send_ref[2 * (r - 4), d, h + k] = high
                         send_ref[2 * (r - 4) + 1, d, h + k] = low
-    odd = odd_ref[0] == 1
+    odd = parity == 1
     inner = inner_ref[outs : outs + share].astype(F32)
     outer = outer_ref[outs : outs + share].astype(F32)
     send_ref[8, 0] = jnp.swapaxes(jnp.where(odd, inner, outer), 0, 1).astype(BF16)
@@ -156,61 +157,81 @@
             place += 1
 
 
-def shares_last(keep_ref, sent_ref, got_ref, mine_ref, kept_ref, send_ref, spread_ref):
-    shares_next(keep_ref, sent_ref, got_ref, kept_ref, send_ref)
+def spread_sums(mine_ref, spread_ref):
     for k in range(spread_ref.shape[0]):
         spread_ref[k] = mine_ref[...]
 
 
-def finish(
-    me_ref, vol_ref, keep_ref, sent_ref, got_ref, taps_ref, bias_ref, out_ref, back_ref, halo, vpad
-):
-    peers, depth, rows, share, cols = vol_ref.shape
+def padded_plane(target, lines):
+    rows = len(lines)
+    blank = jnp.zeros(target.shape[1:], BF16)
+    target[0] = blank
+    target[rows + 1] = blank
+    for h in range(rows):
+        target[h + 1] = jnp.concatenate(lines[h], axis=0)
+
+
+def weights_ahead(taps, depths):
+    return jnp.concatenate(
+        [
+            jnp.concatenate([taps[9 * a + 3 * b + c] for a in depths for b in range(3)], axis=1)
+            for c in range(3)
+        ],
+        axis=0,
+    )
+
+
+def own_output(bias_ref, vol_ref, taps_ref, part_ref, vpad):
+    peers, depth, rows, _, cols = vol_ref.shape
     taps = taps_ref[...]
     outs, chans = taps.shape[1:]
-    me = me_ref[0]
+    row = lax.broadcasted_iota(jnp.int32, (3 * outs, 2 * cols), 0)
+    bias = jnp.zeros(row.shape, F32)
+    for o in range(outs):
+        bias = jnp.where(row == outs + o, bias_ref[o], bias)
+    for d in range(depth):
+        padded_plane(vpad.at[d], [[vol_ref[s, d, h] for s in range(peers)] for h in range(rows)])
+    for d in range(depth):
+        ahead = weights_ahead(taps, [e - d + 1 for e in range(depth)])
+        for h in range(0, rows, 2):
+            stack = jnp.concatenate(
+                [
+                    vpad[0:depth, h + k : h + k + 3].reshape(3 * depth * chans, cols)
+                    for k in range(2)
+                ],
+                axis=1,
+            )
+            part = dot(ahead, stack) + bias
+            for k in range(2):
+                part_ref[d, h + k] = part[:, k * cols : (k + 1) * cols]
+
+
+def finish(
+    part_ref, keep_ref, sent_ref, got_ref, taps_ref, out_ref, back_ref, halo, vpad
+):
+    depth, rows, _, cols = part_ref.shape
+    taps = taps_ref[...]
+    outs, chans = taps.shape[1:]
+    me = lax.axis_index("filt")
     first, second, third = SWAPS
     for place, r in enumerate((0, first, second, first ^ second)):
         halo[jnp.bitwise_xor(me, r)] = sent_ref[2 + place]
         halo[jnp.bitwise_xor(me, r ^ third)] = got_ref[2 + place]
-    blank = jnp.zeros((chans, cols), BF16)
-    for p in range(depth + 2):
-        vpad[p, 0] = blank
-        vpad[p, rows + 1] = blank
-        for h in range(rows):
-            if p == 0:
-                lines = [halo[s, 0, h] for s in range(peers)]
-            elif p == depth + 1:
-                lines = [halo[s, 1, h] for s in range(peers)]
-            else:
-                lines = [vol_ref[s, p - 1, h] for s in range(peers)]
-            vpad[p, h + 1] = jnp.concatenate(lines, axis=0)
-    ahead = jnp.concatenate(
-        [
-            jnp.concatenate([taps[9 * a + 3 * b + c] for a in range(3) for b in range(3)], axis=1)
-            for c in range(3)
-        ],
-        axis=0,
-    )
-    bias = jnp.broadcast_to(bias_ref[...], (outs, cols))
-    for d in range(depth):
+    for d in range(depth):
+        padded_plane(vpad.at[d], [[halo[s, d, h] for s in range(8)] for h in range(rows)])
+        ahead = weights_ahead(taps, [2 * d])
         lines = []
         for h in range(0, rows, 2):
             stack = jnp.concatenate(
-                [
-                    vpad[d : d + 3, h + k : h + k + 3].reshape(9 * chans, cols)
-                    for k in range(2)
-                ],
-                axis=1,
+                [vpad[d, h + k : h + k + 3].reshape(3 * chans, cols) for k in range(2)], axis=1
             )
             part = dot(ahead, stack)
             for k in range(2):
-                total = part[:, k * cols : (k + 1) * cols]
+                total = part[:, k * cols : (k + 1) * cols] + part_ref[d, h + k]
                 lines.append(
                     total[outs : 2 * outs]
                     + slide(total[0:outs], -1)
                     + slide(total[2 * outs : 3 * outs], 1)
-                    + bias
                 )
         out_ref[:, d] = jnp.swapaxes(jnp.stack(lines), 0, 1).astype(BF16)
         total = keep_ref[0, d] + got_ref[0, d].astype(F32) + got_ref[1, d].astype(F32)
@@ -256,12 +277,10 @@
     taps = weight.transpose(0, 2, 1)
     own = volume.transpose(1, 2, 0, 3)
     odd = jnp.bitwise_and(lax.axis_index("space").astype(jnp.int32), 1)
-    me = lax.axis_index("filt").astype(jnp.int32).reshape(1)
     head, tail = (
         jnp.concatenate([grad_out[:, d], volume[:, d]], axis=0) for d in (0, depth - 1)
     )
     inner, outer = swap_edges(odd == 1, head, tail)
-    odd = odd.reshape(1)
     vol = lax.all_to_all(jnp.broadcast_to(own[None], (8,) + own.shape), "filt", 0, 0)
     block = (depth, rows, share, cols)
     planes, bias_sums = pl.pallas_call(
@@ -282,11 +301,11 @@
             jax.ShapeDtypeStruct((4,) + block, F32),
             jax.ShapeDtypeStruct((9,) + block, BF16),
         ),
-        in_specs=[SCALAR] * 2 + [WHOLE] * 4,
+        in_specs=[WHOLE] * 4,
         out_specs=(WHOLE,) * 3,
         scratch_shapes=[pltpu.VMEM((chans, 27 * outs), F32)],
         compiler_params=PARAMS,
-    )(odd, me, planes, taps, outer, inner)
+    )(planes, taps, outer, inner)
     got = lax.ppermute(send, "filt", swap_pairs(SWAPS[0]))
     sums = pl.pallas_call(
         weight_sums,
@@ -318,35 +337,49 @@
         cost_estimate=pl.CostEstimate(flops=10_000_000_000, bytes_accessed=0, transcendentals=0),
     )(parts)
     mine = lax.psum(mine, "space", axis_index_groups=Z_GROUPS)
-    mine, got = lax.optimization_barrier((mine, got))
-    keep, send, spread = pl.pallas_call(
-        shares_last,
+    mine, got, held = lax.optimization_barrier((mine, got, vol))
+    spread = pl.pallas_call(
+        spread_sums,
+        out_shape=jax.ShapeDtypeStruct((16, outs, cols), F32),
+        in_specs=[WHOLE],
+        out_specs=WHOLE,
+        compiler_params=PARAMS,
+    )(mine)
+    keep, send = pl.pallas_call(
+        shares_next,
         out_shape=(
             jax.ShapeDtypeStruct((1,) + block, F32),
             jax.ShapeDtypeStruct((6,) + block, BF16),
-            jax.ShapeDtypeStruct((16, outs, cols), F32),
-        ),
-        in_specs=[WHOLE] * 4,
-        out_specs=(WHOLE,) * 3,
-        compiler_params=PARAMS,
-    )(keep, send, got, mine)
+        ),
+        in_specs=[WHOLE] * 3,
+        out_specs=(WHOLE,) * 2,
+        compiler_params=PARAMS,
+    )(keep, send, got)
     got = lax.ppermute(send, "filt", swap_pairs(SWAPS[2]))
     every = lax.all_to_all(spread, "space", 0, 0, axis_index_groups=XY_GROUPS)
+    part = pl.pallas_call(
+        own_output,
+        out_shape=jax.ShapeDtypeStruct((depth, rows, 3 * outs, cols), F32),
+        in_specs=[SCALAR] + [WHOLE] * 2,
+        out_specs=WHOLE,
+        scratch_shapes=[pltpu.VMEM((depth, rows + 2, chans, cols), BF16)],
+        compiler_params=PARAMS,
+    )(bias, held, taps)
+    every, part = lax.optimization_barrier((every, part))
     output, grad_volume = pl.pallas_call(
         finish,
         out_shape=(
             jax.ShapeDtypeStruct((outs, depth, rows, cols), BF16),
             jax.ShapeDtypeStruct((share, depth, rows, cols), BF16),
         ),
-        in_specs=[SCALAR] + [WHOLE] * 6,
+        in_specs=[WHOLE] * 5,
         out_specs=(WHOLE,) * 2,
         scratch_shapes=[
             pltpu.VMEM((8,) + block, BF16),
-            pltpu.VMEM((depth + 2, rows + 2, chans, cols), BF16),
+            pltpu.VMEM((depth, rows + 2, chans, cols), BF16),
         ],
         compiler_params=PARAMS,
-    )(me, vol, keep, send, got, taps, bias[:, None])
-    every, output, grad_volume = lax.optimization_barrier((every, output, grad_volume))
+    )(part, keep, send, got, taps)
     scale = 1.0 / math.sqrt(depth * lax.axis_size("space") * rows * cols)
     grad_taps, grad_bias = pl.pallas_call(
         lambda *refs: unpack(scale, *refs),
@@ -357,6 +390,7 @@
         in_specs=[WHOLE],
         out_specs=(WHOLE,) * 2,
         compiler_params=PARAMS,
+        cost_estimate=pl.CostEstimate(flops=10_000_000_000, bytes_accessed=0, transcendentals=0),
     )(every)
     return (output, grad_volume, grad_taps.transpose(0, 2, 1), grad_bias.reshape(outs))
 

time: 76.2 us -> 74.4 us (0.976)
  the two profiles are of different devices: /device:TPU:1 before, /device:TPU:32 now
where the time goes in v9:
time: 74.4 us; the launch traced here: 73.8 us
  starting transfers between devices  37.8 us (51%)
  blocking collectives  17.2 us (23%)
  waiting for transfers between devices  10.8 us (15%)
  Pallas kernels  5.66 us (8%)
  local copies, waits for them, and re-layouts  1.57 us (2%)
  between operations  0.81 us (1%)
    psum x1, blocking collectives, local(): mine = lax.psum(mine, 'space', axis_index_groups=Z_GROUPS)  17.2 us
    all_to_all x1, starting transfers between devices, local(): parts = lax.all_to_all(sums, 'space', 0, 0, axis_index_groups=XY_GROUPS)  11.1 us
    all_to_all x1, starting transfers between devices, local(): lax.all_to_all(jnp.broadcast_to(own[None], (8,) + own.shape), 'filt', 0, 0)  8.93 us
    all_to_all x1, waiting for transfers between devices, local(): every = lax.all_to_all(spread, 'space', 0, 0, axis_index_groups=XY_GROUPS)  4.87 us
    ppermute x1, starting transfers between devices, local(): got = lax.ppermute(send, 'filt', swap_pairs(SWAPS[1]))  4.77 us
    all_to_all x1, starting transfers between devices, local(): every = lax.all_to_all(spread, 'space', 0, 0, axis_index_groups=XY_GROUPS)  4.72 us
    ppermute x1, starting transfers between devices, swap_edges(): inner = lax.ppermute(jnp.where(odd, head, tail), 'space', EVEN)  3.63 us
    all_to_all x1, waiting for transfers between devices, local(): parts = lax.all_to_all(sums, 'space', 0, 0, axis_index_groups=XY_GROUPS)  2.99 us
  transfers between devices with their start and end apart: 8, of which 4 were waited for; matrix products, arithmetic and copies ran while one was open for 1% of the time, Pallas kernels for 5%

profile of v9, /device:TPU:32, one launch (start us, length us, event | category | flops | bytes accessed | tf_op | source)
XLA Modules:
  0.0 73.8 jit_solution(12071401586345818016)
XLA Ops:
  0.6 0.0 copy-start.3
  0.6 0.8 %slice_bitcast_fusion.1 = (bf16[16,8,128]{2,1,0:T(8,128)(2,1)S(1)}, bf16[16,8,128]{2,1,0:T(8,128)(2,1)S(1)}) fusion(bf16[16,2,8,128]{3,2,1,0:T(8,128)(2,1)} %grad_ref.1), kind=kLoop, calls=%fused_computation.5 | loop fusion | bytes 131072 | tf_op jit(solution)/shard_map/squeeze | solution.py:281
  1.4 0.0 copy-done.3
  1.5 0.7 collective-permute-start
  2.2 0.7 %broadcast_in_dim.2 = bf16[8,2,8,8,128]{4,3,2,1,0:T(8,128)(2,1)} broadcast(bf16[2,8,8,128]{3,2,1,0:T(8,128)(2,1)S(1)} %copy.8), dimensions={1,2,3,4} | broadcast | bytes 294912 | tf_op jit(solution)/shard_map/broadcast_in_dim | solution.py:284
  2.9 0.0 copy-start.1
  2.9 8.9 %all-to-all-start = ((bf16[8,2,8,8,128]{4,3,2,1,0:T(8,128)(2,1)}), bf16[8,2,8,8,128]{4,3,2,1,0:T(8,128)(2,1)S(1)}, u32[]{:S(2)}, u32[]{:S(2)}) async-start(bf16[8,2,8,8,128]{4,3,2,1,0:T(8,128)(2,1)} %broadcast_in_dim.2), calls=%async_computation | async-start | bytes 524288 | tf_op jit(solution)/shard_map/all_to_all | solution.py:284
  11.8 0.0 copy-start
  11.8 3.6 %collective-permute-start.1 = (bf16[24,8,128]{2,1,0:T(8,128)(2,1)S(1)}, bf16[24,8,128]{2,1,0:T(8,128)(2,1)S(1)}, u32[]{:S(2)}, u32[]{:S(2)}) collective-permute-start(bf16[24,8,128]{2,1,0:T(8,128)(2,1)S(1)} %get-tuple-element.40), channel_id=1, source_target_pairs={{0,8},{8,0},{16,24},{24,16},{32,40},{40,32},{48,56},{56,48},{64,72... | collective-permute-start | bytes 147464 | tf_op jit(solution)/shard_map/ppermute | solution.py:264
  15.5 0.0 collective-permute-done.outer_ref
  15.5 0.0 copy-done.1
  15.5 0.2 shard_map.75
  15.7 2.3 %collective-permute-done.1.inner_ref = bf16[24,8,128]{2,1,0:T(8,128)(2,1)S(1)} collective-permute-done((bf16[24,8,128]{2,1,0:T(8,128)(2,1)S(1)}, bf16[24,8,128]{2,1,0:T(8,128)(2,1)S(1)}, u32[]{:S(2)}, u32[]{:S(2)}) %collective-permute-start.1) | collective-permute-done | bytes 49184 | tf_op jit(solution)/shard_map/ppermute | solution.py:264
  17.9 0.0 copy-done
  17.9 0.6 shard_map.76
  18.5 2.0 %collective-permute-start.2 = (bf16[9,2,8,8,128]{4,3,2,1,0:T(8,128)(2,1)S(1)}, bf16[9,2,8,8,128]{4,3,2,1,0:T(8,128)(2,1)S(1)}, u32[]{:S(2)}, u32[]{:S(2)}) collective-permute-start(bf16[9,2,8,8,128]{4,3,2,1,0:T(8,128)(2,1)S(1)} %get-tuple-element.26.sent_ref), channel_id=1, source_target_pairs={{0,2},{1,3},{2,0},{3,1},{4,6},{5,7},{6,4},{7,5},{8,10},{9,11},{10,... | collective-permute-start | bytes 884744 | tf_op jit(solution)/shard_map/ppermute | solution.py:309
  20.6 0.6 all-to-all-done.vol_ref
  21.2 1.3 %shard_map.77 = f32[16,16,128]{2,1,0:T(8,128)} custom-call(bf16[8,2,8,8,128]{4,3,2,1,0:T(8,128)(2,1)S(1)} %all-to-all-done.vol_ref, bf16[4,10,48,128]{3,2,1,0:T(8,128)(2,1)S(1)} %get-tuple-element.23.gpad, f32[16,64]{1,0:T(8,128)S(1)} %get-tuple-element.24.bias_ref), custom_call_target="tpu_custom_call" | custom-call | flops 6000000000 | tf_op jit(solution)/shard_map/pallas_call | solution.py:310
  22.6 11.1 %all-to-all-start.1 = ((f32[16,16,128]{2,1,0:T(8,128)}), f32[16,16,128]{2,1,0:T(8,128)S(1)}, u32[]{:S(2)}, u32[]{:S(2)}) async-start(f32[16,16,128]{2,1,0:T(8,128)} %shard_map.77), calls=%async_computation.1 | async-start | bytes 262144 | tf_op jit(solution)/shard_map/all_to_all | solution.py:318
  33.7 0.0 collective-permute-done.2.got_ref
  33.7 0.1 shard_map.79
  33.7 4.8 %collective-permute-start.3 = (bf16[6,2,8,8,128]{4,3,2,1,0:T(8,128)(2,1)S(1)}, bf16[6,2,8,8,128]{4,3,2,1,0:T(8,128)(2,1)S(1)}, u32[]{:S(2)}, u32[]{:S(2)}) collective-permute-start(bf16[6,2,8,8,128]{4,3,2,1,0:T(8,128)(2,1)S(1)} %get-tuple-element.27.sent_ref), channel_id=1, source_target_pairs={{0,4},{1,5},{2,6},{3,7},{4,0},{5,1},{6,2},{7,3},{8,12},{9,13},{10,... | collective-permute-start | bytes 589832 | tf_op jit(solution)/shard_map/ppermute | solution.py:330
  38.5 3.0 %all-to-all-done.1.parts_ref = f32[16,16,128]{2,1,0:T(8,128)S(1)} async-done(((f32[16,16,128]{2,1,0:T(8,128)}), f32[16,16,128]{2,1,0:T(8,128)S(1)}, u32[]{:S(2)}, u32[]{:S(2)}) %all-to-all-start.1) | async-done | bytes 131104 | tf_op jit(solution)/shard_map/all_to_all | solution.py:318
  41.5 17.2 %psum.7.mine_ref = f32[16,128]{1,0:T(8,128)S(1)} all-reduce(f32[16,128]{1,0:T(8,128)S(1)} %shard_map.78), channel_id=1, replica_groups={{0,128,256,384},{8,136,264,392},{16,144,272,400},{24,152,280,408},{32,1..., use_global_device_ids=true, to_apply=%region_0.1 | all-reduce | flops 2048 | bytes 16384 | tf_op jit(solution)/shard_map/psum | solution.py:339
  58.7 0.0 collective-permute-done.3.got_ref
  58.7 0.7 shard_map.80
  59.4 4.7 %all-to-all-start.2 = ((f32[16,16,128]{2,1,0:T(8,128)}), f32[16,16,128]{2,1,0:T(8,128)S(1)}, u32[]{:S(2)}, u32[]{:S(2)}) async-start(f32[16,16,128]{2,1,0:T(8,128)} %shard_map.80), calls=%async_computation.2 | async-start | bytes 262144 | tf_op jit(solution)/shard_map/all_to_all | solution.py:359
  64.1 0.0 copy-start.2
  64.1 1.9 %collective-permute-start.4 = (bf16[6,2,8,8,128]{4,3,2,1,0:T(8,128)(2,1)S(1)}, bf16[6,2,8,8,128]{4,3,2,1,0:T(8,128)(2,1)S(1)}, u32[]{:S(2)}, u32[]{:S(2)}) collective-permute-start(bf16[6,2,8,8,128]{4,3,2,1,0:T(8,128)(2,1)S(1)} %get-tuple-element.34.sent_ref), channel_id=1, source_target_pairs={{0,1},{1,0},{2,3},{3,2},{4,5},{5,4},{6,7},{7,6},{8,9},{9,8},{10,11... | collective-permute-start | bytes 589832 | tf_op jit(solution)/shard_map/ppermute | solution.py:358
  66.1 0.0 copy-done.2
  66.1 1.0 %shard_map.81.part_ref = f32[2,8,48,128]{3,2,1,0:T(8,128)S(1)} custom-call(f32[16]{0:T(128)S(1)} %copy-done.2, bf16[8,2,8,8,128]{4,3,2,1,0:T(8,128)(2,1)S(1)} %all-to-all-done.vol_ref, bf16[27,16,64]{2,1,0:T(8,128)(2,1)S(1)} %bitcast.21), custom_call_target="tpu_custom_call" | custom-call | tf_op jit(solution)/shard_map/pallas_call | solution.py:360
  67.1 4.9 %all-to-all-done.2.refs_0_ = f32[16,16,128]{2,1,0:T(8,128)S(1)} async-done(((f32[16,16,128]{2,1,0:T(8,128)}), f32[16,16,128]{2,1,0:T(8,128)S(1)}, u32[]{:S(2)}, u32[]{:S(2)}) %all-to-all-start.2) | async-done | bytes 131104 | tf_op jit(solution)/shard_map/all_to_all | solution.py:359
  71.9 0.8 %shard_map.84 = (f32[27,16,64]{2,1,0:T(8,128)}, f32[1,16]{1,0:T(1,128)}) custom-call(f32[16,16,128]{2,1,0:T(8,128)S(1)} %all-to-all-done.2.refs_0_), custom_call_target="tpu_custom_call" | custom-call | flops 10000000000 | tf_op jit(solution)/shard_map/pallas_call | solution.py:384
  72.8 0.0 collective-permute-done.4.got_ref
  72.8 1.0 %shard_map.83 = (bf16[16,2,8,128]{3,2,1,0:T(8,128)(2,1)}, bf16[8,2,8,128]{3,2,1,0:T(8,128)(2,1)}) custom-call(f32[2,8,48,128]{3,2,1,0:T(8,128)S(1)} %shard_map.81.part_ref, f32[1,2,8,8,128]{4,3,2,1,0:T(8,128)S(1)} %get-tuple-element.33.keep_ref, bf16[6,2,8,8,128]{4,3,2,1,0:T(8,128)(2,1)S(1)} %get-tuple-element.34.sent_ref, ...), custom_call_target="tpu_custom_call" | custom-call | tf_op jit(solution)/shard_map/pallas_call | solution.py:369
  (5 shorter events, 0.1 us)
Async XLA Ops:
  0.6 0.8 %copy-start.3 = (bf16[8,2,8,128]{3,2,1,0:T(8,128)(2,1)S(1)}, bf16[8,2,8,128]{3,2,1,0:T(8,128)(2,1)}, u32[]{:S(2)}) copy-start(bf16[8,2,8,128]{3,2,1,0:T(8,128)(2,1)} %param.4) | copy-start | bytes 98308
  1.5 14.0 %collective-permute-start = (bf16[24,8,128]{2,1,0:T(8,128)(2,1)S(1)}, bf16[24,8,128]{2,1,0:T(8,128)(2,1)S(1)}, u32[]{:S(2)}, u32[]{:S(2)}) collective-permute-start(bf16[24,8,128]{2,1,0:T(8,128)(2,1)S(1)} %get-tuple-element.41), channel_id=1, source_target_pairs={{8,16},{16,8},{24,32},{32,24},{40,48},{48,40},{56,64},{64,56},{72,... | collective-permute-start | bytes 147464 | tf_op jit(solution)/shard_map/ppermute | solution.py:265
  2.9 12.6 %copy-start.1 = (bf16[16,2,8,128]{3,2,1,0:T(8,128)(2,1)S(1)}, bf16[16,2,8,128]{3,2,1,0:T(8,128)(2,1)}, u32[]{:S(2)}) copy-start(bf16[16,2,8,128]{3,2,1,0:T(8,128)(2,1)} %grad_ref.1) | copy-start | bytes 196612
  2.9 18.3 %all-to-all-start = ((bf16[8,2,8,8,128]{4,3,2,1,0:T(8,128)(2,1)}), bf16[8,2,8,8,128]{4,3,2,1,0:T(8,128)(2,1)S(1)}, u32[]{:S(2)}, u32[]{:S(2)}) async-start(bf16[8,2,8,8,128]{4,3,2,1,0:T(8,128)(2,1)} %broadcast_in_dim.2), calls=%async_computation | async-start | bytes 524288 | tf_op jit(solution)/shard_map/all_to_all | solution.py:284
  11.8 6.1 %copy-start = (bf16[27,64,16]{1,2,0:T(8,128)(2,1)S(1)}, bf16[27,64,16]{1,2,0:T(8,128)(2,1)}, u32[]{:S(2)}) copy-start(bf16[27,64,16]{1,2,0:T(8,128)(2,1)} %param.5) | copy-start | bytes 165892
  11.8 6.1 %collective-permute-start.1 = (bf16[24,8,128]{2,1,0:T(8,128)(2,1)S(1)}, bf16[24,8,128]{2,1,0:T(8,128)(2,1)S(1)}, u32[]{:S(2)}, u32[]{:S(2)}) collective-permute-start(bf16[24,8,128]{2,1,0:T(8,128)(2,1)S(1)} %get-tuple-element.40), channel_id=1, source_target_pairs={{0,8},{8,0},{16,24},{24,16},{32,40},{40,32},{48,56},{56,48},{64,72... | collective-permute-start | bytes 147464 | tf_op jit(solution)/shard_map/ppermute | solution.py:264
  18.5 15.1 %collective-permute-start.2 = (bf16[9,2,8,8,128]{4,3,2,1,0:T(8,128)(2,1)S(1)}, bf16[9,2,8,8,128]{4,3,2,1,0:T(8,128)(2,1)S(1)}, u32[]{:S(2)}, u32[]{:S(2)}) collective-permute-start(bf16[9,2,8,8,128]{4,3,2,1,0:T(8,128)(2,1)S(1)} %get-tuple-element.26.sent_ref), channel_id=1, source_target_pairs={{0,2},{1,3},{2,0},{3,1},{4,6},{5,7},{6,4},{7,5},{8,10},{9,11},{10,... | collective-permute-start | bytes 884744 | tf_op jit(solution)/shard_map/ppermute | solution.py:309
  22.6 18.9 %all-to-all-start.1 = ((f32[16,16,128]{2,1,0:T(8,128)}), f32[16,16,128]{2,1,0:T(8,128)S(1)}, u32[]{:S(2)}, u32[]{:S(2)}) async-start(f32[16,16,128]{2,1,0:T(8,128)} %shard_map.77), calls=%async_computation.1 | async-start | bytes 262144 | tf_op jit(solution)/shard_map/all_to_all | solution.py:318
  33.7 25.0 %collective-permute-start.3 = (bf16[6,2,8,8,128]{4,3,2,1,0:T(8,128)(2,1)S(1)}, bf16[6,2,8,8,128]{4,3,2,1,0:T(8,128)(2,1)S(1)}, u32[]{:S(2)}, u32[]{:S(2)}) collective-permute-start(bf16[6,2,8,8,128]{4,3,2,1,0:T(8,128)(2,1)S(1)} %get-tuple-element.27.sent_ref), channel_id=1, source_target_pairs={{0,4},{1,5},{2,6},{3,7},{4,0},{5,1},{6,2},{7,3},{8,12},{9,13},{10,... | collective-permute-start | bytes 589832 | tf_op jit(solution)/shard_map/ppermute | solution.py:330
  59.4 12.6 %all-to-all-start.2 = ((f32[16,16,128]{2,1,0:T(8,128)}), f32[16,16,128]{2,1,0:T(8,128)S(1)}, u32[]{:S(2)}, u32[]{:S(2)}) async-start(f32[16,16,128]{2,1,0:T(8,128)} %shard_map.80), calls=%async_computation.2 | async-start | bytes 262144 | tf_op jit(solution)/shard_map/all_to_all | solution.py:359
  64.1 1.9 %copy-start.2 = (f32[16]{0:T(128)S(1)}, f32[16]{0:T(128)}, u32[]{:S(2)}) copy-start(f32[16]{0:T(128)} %bias_ref.1) | copy-start | bytes 196
  64.1 8.6 %collective-permute-start.4 = (bf16[6,2,8,8,128]{4,3,2,1,0:T(8,128)(2,1)S(1)}, bf16[6,2,8,8,128]{4,3,2,1,0:T(8,128)(2,1)S(1)}, u32[]{:S(2)}, u32[]{:S(2)}) collective-permute-start(bf16[6,2,8,8,128]{4,3,2,1,0:T(8,128)(2,1)S(1)} %get-tuple-element.34.sent_ref), channel_id=1, source_target_pairs={{0,1},{1,0},{2,3},{3,2},{4,5},{5,4},{6,7},{7,6},{8,9},{9,8},{10,11... | collective-permute-start | bytes 589832 | tf_op jit(solution)/shard_map/ppermute | solution.py:358

commit v10 on v9

--- a/solution.py
+++ b/solution.py
@@ -44,7 +44,7 @@
         target[h + 1, 2 * outs : 3 * outs] = slide(wide, -1).astype(BF16)
 
 
-def ready_planes(grad_ref, outer_ref, planes_ref, bias_ref):
+def ready_planes(grad_ref, outer_ref, taps_ref, planes_ref, bias_ref, behind_ref, turned):
     outs, depth, rows, cols = grad_ref.shape
     total = None
     for d in range(depth):
@@ -55,6 +55,17 @@
     shifted(outer_ref[0:outs].astype(F32), planes_ref.at[depth])
     half = cols // 2
     bias_ref[...] = total[:, :half] + total[:, half:]
+    chans = taps_ref.shape[2]
+    share = chans // 8
+    turned[...] = taps_ref[...].reshape(27 * outs, chans).astype(F32).T
+    me = lax.axis_index("filt")
+    behind_ref[...] = jnp.concatenate(
+        [
+            turned[pl.ds(pl.multiple_of(share * jnp.bitwise_xor(me, r), share), share)]
+            for r in ORDER
+        ],
+        axis=0,
+    ).astype(BF16)
 
 
 def weight_sums(vol_ref, gpad, bias_ref, sums_ref):
@@ -98,24 +109,16 @@
 
 
 def shares_first(
-    planes_ref, taps_ref, outer_ref, inner_ref, gpad, keep_ref, send_ref, turned
+    planes_ref, behind_ref, outer_ref, inner_ref, gpad, keep_ref, send_ref
 ):
     _, depth, rows, share, cols = keep_ref.shape
-    outs, chans = taps_ref.shape[1:]
+    outs = inner_ref.shape[0] - share
     for d in range(depth):
         gpad[d + 1] = planes_ref[d]
     parity = jnp.bitwise_and(lax.axis_index("space"), 1)
     gpad[(depth + 1) * parity] = planes_ref[depth]
     shifted(inner_ref[0:outs].astype(F32), gpad.at[(depth + 1) * (1 - parity)])
-    turned[...] = taps_ref[...].reshape(27 * outs, chans).astype(F32).T
-    me = lax.axis_index("filt")
-    behind = jnp.concatenate(
-        [
-            turned[pl.ds(pl.multiple_of(share * jnp.bitwise_xor(me, r), share), share)]
-            for r in ORDER
-        ],
-        axis=0,
-    ).astype(BF16)
+    behind = behind_ref[...]
     for d in range(depth):
         for h in range(0, rows, 2):
             back = dot(behind, moved_rows(gpad, d, h))
@@ -207,11 +210,22 @@
 
 
 def finish(
-    part_ref, keep_ref, sent_ref, got_ref, taps_ref, out_ref, back_ref, halo, vpad
+    sums_ref, part_ref, keep_ref, sent_ref, got_ref, taps_ref,
+    weight_ref, bias_ref, out_ref, back_ref, halo, vpad,
 ):
     depth, rows, _, cols = part_ref.shape
     taps = taps_ref[...]
     outs, chans = taps.shape[1:]
+    half = cols // 2
+    for t in range(27):
+        r, side = t // 2, t % 2
+        weight_ref[t] = sums_ref[r, :, half * side : half * (side + 1)]
+    total = jnp.sum(sums_ref[13, :, half:], axis=1, keepdims=True)
+    wide = jnp.broadcast_to(total, (outs, cols))
+    row = lax.broadcasted_iota(jnp.int32, (outs, cols), 0)
+    lane = lax.broadcasted_iota(jnp.int32, (outs, cols), 1)
+    flat = jnp.sum(jnp.where(row == lane, wide, 0.0), axis=0, keepdims=True)
+    bias_ref[...] = flat[:, :outs]
     me = lax.axis_index("filt")
     first, second, third = SWAPS
     for place, r in enumerate((0, first, second, first ^ second)):
@@ -238,18 +252,8 @@
         back_ref[:, d] = jnp.swapaxes(total, 0, 1).astype(BF16)
 
 
-def unpack(scale, every_ref, weight_ref, bias_ref):
-    outs, cols = every_ref.shape[1:]
-    half = cols // 2
-    for t in range(27):
-        r, side = t // 2, t % 2
-        weight_ref[t] = every_ref[r, :, half * side : half * (side + 1)] * scale
-    total = jnp.sum(every_ref[13, :, half:] * scale, axis=1, keepdims=True)
-    wide = jnp.broadcast_to(total, (outs, cols))
-    row = lax.broadcasted_iota(jnp.int32, (outs, cols), 0)
-    lane = lax.broadcasted_iota(jnp.int32, (outs, cols), 1)
-    flat = jnp.sum(jnp.where(row == lane, wide, 0.0), axis=0, keepdims=True)
-    bias_ref[...] = flat[:, :outs]
+def scaled(scale, every_ref, sums_ref):
+    sums_ref[...] = every_ref[...] * scale
 
 
 SWAPS = (2, 4, 1)
@@ -283,17 +287,19 @@
     inner, outer = swap_edges(odd == 1, head, tail)
     vol = lax.all_to_all(jnp.broadcast_to(own[None], (8,) + own.shape), "filt", 0, 0)
     block = (depth, rows, share, cols)
-    planes, bias_sums = pl.pallas_call(
+    planes, bias_sums, behind = pl.pallas_call(
         ready_planes,
         out_shape=(
             jax.ShapeDtypeStruct((depth + 1, rows + 2, 3 * outs, cols), BF16),
             jax.ShapeDtypeStruct((outs, cols // 2), F32),
+            jax.ShapeDtypeStruct((chans, 27 * outs), BF16),
         ),
-        in_specs=[WHOLE] * 2,
-        out_specs=(WHOLE,) * 2,
+        in_specs=[WHOLE] * 3,
+        out_specs=(WHOLE,) * 3,
+        scratch_shapes=[pltpu.VMEM((chans, 27 * outs), F32)],
         compiler_params=PARAMS,
         cost_estimate=pl.CostEstimate(flops=9_500_000_000, bytes_accessed=0, transcendentals=0),
-    )(grad_out, outer)
+    )(grad_out, outer, taps)
     moved, keep, send = pl.pallas_call(
         shares_first,
         out_shape=(
@@ -303,9 +309,8 @@
         ),
         in_specs=[WHOLE] * 4,
         out_specs=(WHOLE,) * 3,
-        scratch_shapes=[pltpu.VMEM((chans, 27 * outs), F32)],
-        compiler_params=PARAMS,
-    )(planes, taps, outer, inner)
+        compiler_params=PARAMS,
+    )(planes, behind, outer, inner)
     got = lax.ppermute(send, "filt", swap_pairs(SWAPS[0]))
     sums = pl.pallas_call(
         weight_sums,
@@ -366,32 +371,31 @@
         compiler_params=PARAMS,
     )(bias, held, taps)
     every, part = lax.optimization_barrier((every, part))
-    output, grad_volume = pl.pallas_call(
+    scale = 1.0 / math.sqrt(depth * lax.axis_size("space") * rows * cols)
+    every = pl.pallas_call(
+        lambda *refs: scaled(scale, *refs),
+        out_shape=jax.ShapeDtypeStruct((16, outs, cols), F32),
+        in_specs=[WHOLE],
+        out_specs=WHOLE,
+        compiler_params=PARAMS,
+        cost_estimate=pl.CostEstimate(flops=10_000_000_000, bytes_accessed=0, transcendentals=0),
+    )(every)
+    grad_taps, grad_bias, output, grad_volume = pl.pallas_call(
         finish,
         out_shape=(
+            jax.ShapeDtypeStruct((27, outs, cols // 2), F32),
+            jax.ShapeDtypeStruct((1, outs), F32),
             jax.ShapeDtypeStruct((outs, depth, rows, cols), BF16),
             jax.ShapeDtypeStruct((share, depth, rows, cols), BF16),
         ),
-        in_specs=[WHOLE] * 5,
-        out_specs=(WHOLE,) * 2,
+        in_specs=[WHOLE] * 6,
+        out_specs=(WHOLE,) * 4,
         scratch_shapes=[
             pltpu.VMEM((8,) + block, BF16),
             pltpu.VMEM((depth, rows + 2, chans, cols), BF16),
         ],
         compiler_params=PARAMS,
-    )(part, keep, send, got, taps)
-    scale = 1.0 / math.sqrt(depth * lax.axis_size("space") * rows * cols)
-    grad_taps, grad_bias = pl.pallas_call(
-        lambda *refs: unpack(scale, *refs),
-        out_shape=(
-            jax.ShapeDtypeStruct((27, outs, cols // 2), F32),
-            jax.ShapeDtypeStruct((1, outs), F32),
-        ),
-        in_specs=[WHOLE],
-        out_specs=(WHOLE,) * 2,
-        compiler_params=PARAMS,
-        cost_estimate=pl.CostEstimate(flops=10_000_000_000, bytes_accessed=0, transcendentals=0),
-    )(every)
+    )(every, part, keep, send, got, taps)
     return (output, grad_volume, grad_taps.transpose(0, 2, 1), grad_bias.reshape(outs))
 
 

time: 74.4 us -> 73.4 us (0.987)
  Pallas kernels: 5.66 us -> 4.88 us
    pallas_call x2, Pallas kernels: 1.86 us -> 1.06 us  [the longest x1 1.05 us: local(): pl.pallas_call(finish, out_shape=(jax.ShapeDtypeStruct((27, outs, cols //...]
  transfers between devices with their start and end apart: 8 -> 8, of which waited for: 4 -> 4; matrix products, arithmetic and copies ran while one was open for 1% -> 1% of each run, Pallas kernels for 5% -> 4%
where the time goes in v10:
time: 73.4 us; the launch traced here: 72.8 us
  starting transfers between devices  37.5 us (51%)
  blocking collectives  17.2 us (23%)
  waiting for transfers between devices  10.9 us (15%)
  Pallas kernels  4.88 us (7%)
  local copies, waits for them, and re-layouts  1.57 us (2%)
  between operations  0.83 us (1%)
    psum x1, blocking collectives, local(): mine = lax.psum(mine, 'space', axis_index_groups=Z_GROUPS)  17.2 us
    all_to_all x1, starting transfers between devices, local(): parts = lax.all_to_all(sums, 'space', 0, 0, axis_index_groups=XY_GROUPS)  10.9 us
    all_to_all x1, starting transfers between devices, local(): lax.all_to_all(jnp.broadcast_to(own[None], (8,) + own.shape), 'filt', 0, 0)  8.93 us
    all_to_all x1, waiting for transfers between devices, local(): every = lax.all_to_all(spread, 'space', 0, 0, axis_index_groups=XY_GROUPS)  4.87 us
    ppermute x1, starting transfers between devices, local(): got = lax.ppermute(send, 'filt', swap_pairs(SWAPS[1]))  4.77 us
    all_to_all x1, starting transfers between devices, local(): every = lax.all_to_all(spread, 'space', 0, 0, axis_index_groups=XY_GROUPS)  4.72 us
    ppermute x1, starting transfers between devices, swap_edges(): inner = lax.ppermute(jnp.where(odd, head, tail), 'space', EVEN)  3.5 us
    all_to_all x1, waiting for transfers between devices, local(): parts = lax.all_to_all(sums, 'space', 0, 0, axis_index_groups=XY_GROUPS)  2.99 us
  transfers between devices with their start and end apart: 8, of which 4 were waited for; matrix products, arithmetic and copies ran while one was open for 1% of the time, Pallas kernels for 4%

profile of v10, /device:TPU:32, one launch (start us, length us, event | category | flops | bytes accessed | tf_op | source)
XLA Modules:
  0.0 72.8 jit_solution(1878768196138719097)
XLA Ops:
  0.6 0.0 copy-start.3
  0.6 0.8 %slice_bitcast_fusion.1 = (bf16[16,8,128]{2,1,0:T(8,128)(2,1)S(1)}, bf16[16,8,128]{2,1,0:T(8,128)(2,1)S(1)}) fusion(bf16[16,2,8,128]{3,2,1,0:T(8,128)(2,1)} %grad_ref.1), kind=kLoop, calls=%fused_computation.5 | loop fusion | bytes 131072 | tf_op jit(solution)/shard_map/squeeze | solution.py:285
  1.4 0.0 copy-done.3
  1.5 0.7 collective-permute-start
  2.2 0.8 %broadcast_in_dim.2 = bf16[8,2,8,8,128]{4,3,2,1,0:T(8,128)(2,1)} broadcast(bf16[2,8,8,128]{3,2,1,0:T(8,128)(2,1)S(1)} %copy.8), dimensions={1,2,3,4} | broadcast | bytes 294912 | tf_op jit(solution)/shard_map/broadcast_in_dim | solution.py:288
  2.9 0.0 copy-start
  2.9 0.0 copy-start.1
  2.9 8.9 %all-to-all-start = ((bf16[8,2,8,8,128]{4,3,2,1,0:T(8,128)(2,1)}), bf16[8,2,8,8,128]{4,3,2,1,0:T(8,128)(2,1)S(1)}, u32[]{:S(2)}, u32[]{:S(2)}) async-start(bf16[8,2,8,8,128]{4,3,2,1,0:T(8,128)(2,1)} %broadcast_in_dim.2), calls=%async_computation | async-start | bytes 524288 | tf_op jit(solution)/shard_map/all_to_all | solution.py:288
  11.8 3.5 %collective-permute-start.1 = (bf16[24,8,128]{2,1,0:T(8,128)(2,1)S(1)}, bf16[24,8,128]{2,1,0:T(8,128)(2,1)S(1)}, u32[]{:S(2)}, u32[]{:S(2)}) collective-permute-start(bf16[24,8,128]{2,1,0:T(8,128)(2,1)S(1)} %get-tuple-element.42), channel_id=1, source_target_pairs={{0,8},{8,0},{16,24},{24,16},{32,40},{40,32},{48,56},{56,48},{64,72... | collective-permute-start | bytes 147464 | tf_op jit(solution)/shard_map/ppermute | solution.py:268
  15.4 0.0 collective-permute-done.outer_ref
  15.4 0.0 copy-done
  15.4 0.0 copy-done.1
  15.4 0.2 shard_map.75
  15.6 2.2 %collective-permute-done.1.inner_ref = bf16[24,8,128]{2,1,0:T(8,128)(2,1)S(1)} collective-permute-done((bf16[24,8,128]{2,1,0:T(8,128)(2,1)S(1)}, bf16[24,8,128]{2,1,0:T(8,128)(2,1)S(1)}, u32[]{:S(2)}, u32[]{:S(2)}) %collective-permute-start.1) | collective-permute-done | bytes 49184 | tf_op jit(solution)/shard_map/ppermute | solution.py:268
  17.8 0.5 shard_map.76
  18.3 2.0 %collective-permute-start.2 = (bf16[9,2,8,8,128]{4,3,2,1,0:T(8,128)(2,1)S(1)}, bf16[9,2,8,8,128]{4,3,2,1,0:T(8,128)(2,1)S(1)}, u32[]{:S(2)}, u32[]{:S(2)}) collective-permute-start(bf16[9,2,8,8,128]{4,3,2,1,0:T(8,128)(2,1)S(1)} %get-tuple-element.28.sent_ref), channel_id=1, source_target_pairs={{0,2},{1,3},{2,0},{3,1},{4,6},{5,7},{6,4},{7,5},{8,10},{9,11},{10,... | collective-permute-start | bytes 884744 | tf_op jit(solution)/shard_map/ppermute | solution.py:314
  20.4 0.8 %all-to-all-done.vol_ref = bf16[8,2,8,8,128]{4,3,2,1,0:T(8,128)(2,1)S(1)} async-done(((bf16[8,2,8,8,128]{4,3,2,1,0:T(8,128)(2,1)}), bf16[8,2,8,8,128]{4,3,2,1,0:T(8,128)(2,1)S(1)}, u32[]{:S(2)}, u32[]{:S(2)}) %all-to-all-start) | async-done | bytes 262176 | tf_op jit(solution)/shard_map/all_to_all | solution.py:288
  21.2 1.3 %shard_map.77 = f32[16,16,128]{2,1,0:T(8,128)} custom-call(bf16[8,2,8,8,128]{4,3,2,1,0:T(8,128)(2,1)S(1)} %all-to-all-done.vol_ref, bf16[4,10,48,128]{3,2,1,0:T(8,128)(2,1)S(1)} %get-tuple-element.25.gpad, f32[16,64]{1,0:T(8,128)S(1)} %get-tuple-element.26.bias_ref), custom_call_target="tpu_custom_call" | custom-call | flops 6000000000 | tf_op jit(solution)/shard_map/pallas_call | solution.py:315
  22.6 10.9 %all-to-all-start.1 = ((f32[16,16,128]{2,1,0:T(8,128)}), f32[16,16,128]{2,1,0:T(8,128)S(1)}, u32[]{:S(2)}, u32[]{:S(2)}) async-start(f32[16,16,128]{2,1,0:T(8,128)} %shard_map.77), calls=%async_computation.1 | async-start | bytes 262144 | tf_op jit(solution)/shard_map/all_to_all | solution.py:323
  33.5 0.0 collective-permute-done.2.got_ref
  33.5 0.1 shard_map.79
  33.6 4.8 %collective-permute-start.3 = (bf16[6,2,8,8,128]{4,3,2,1,0:T(8,128)(2,1)S(1)}, bf16[6,2,8,8,128]{4,3,2,1,0:T(8,128)(2,1)S(1)}, u32[]{:S(2)}, u32[]{:S(2)}) collective-permute-start(bf16[6,2,8,8,128]{4,3,2,1,0:T(8,128)(2,1)S(1)} %get-tuple-element.29.sent_ref), channel_id=1, source_target_pairs={{0,4},{1,5},{2,6},{3,7},{4,0},{5,1},{6,2},{7,3},{8,12},{9,13},{10,... | collective-permute-start | bytes 589832 | tf_op jit(solution)/shard_map/ppermute | solution.py:335
  38.3 3.0 %all-to-all-done.1.parts_ref = f32[16,16,128]{2,1,0:T(8,128)S(1)} async-done(((f32[16,16,128]{2,1,0:T(8,128)}), f32[16,16,128]{2,1,0:T(8,128)S(1)}, u32[]{:S(2)}, u32[]{:S(2)}) %all-to-all-start.1) | async-done | bytes 131104 | tf_op jit(solution)/shard_map/all_to_all | solution.py:323
  41.3 17.2 %psum.7.mine_ref = f32[16,128]{1,0:T(8,128)S(1)} all-reduce(f32[16,128]{1,0:T(8,128)S(1)} %shard_map.78), channel_id=1, replica_groups={{0,128,256,384},{8,136,264,392},{16,144,272,400},{24,152,280,408},{32,1..., use_global_device_ids=true, to_apply=%region_0.1 | all-reduce | flops 2048 | bytes 16384 | tf_op jit(solution)/shard_map/psum | solution.py:344
  58.5 0.0 collective-permute-done.3.got_ref
  58.5 0.7 shard_map.80
  59.2 4.7 %all-to-all-start.2 = ((f32[16,16,128]{2,1,0:T(8,128)}), f32[16,16,128]{2,1,0:T(8,128)S(1)}, u32[]{:S(2)}, u32[]{:S(2)}) async-start(f32[16,16,128]{2,1,0:T(8,128)} %shard_map.80), calls=%async_computation.2 | async-start | bytes 262144 | tf_op jit(solution)/shard_map/all_to_all | solution.py:364
  64.0 0.0 copy-start.2
  64.0 1.9 %collective-permute-start.4 = (bf16[6,2,8,8,128]{4,3,2,1,0:T(8,128)(2,1)S(1)}, bf16[6,2,8,8,128]{4,3,2,1,0:T(8,128)(2,1)S(1)}, u32[]{:S(2)}, u32[]{:S(2)}) collective-permute-start(bf16[6,2,8,8,128]{4,3,2,1,0:T(8,128)(2,1)S(1)} %get-tuple-element.37.sent_ref), channel_id=1, source_target_pairs={{0,1},{1,0},{2,3},{3,2},{4,5},{5,4},{6,7},{7,6},{8,9},{9,8},{10,11... | collective-permute-start | bytes 589832 | tf_op jit(solution)/shard_map/ppermute | solution.py:363
  65.9 0.0 copy-done.2
  65.9 1.0 %shard_map.81.part_ref = f32[2,8,48,128]{3,2,1,0:T(8,128)S(1)} custom-call(f32[16]{0:T(128)S(1)} %copy-done.2, bf16[8,2,8,8,128]{4,3,2,1,0:T(8,128)(2,1)S(1)} %all-to-all-done.vol_ref, bf16[27,16,64]{2,1,0:T(8,128)(2,1)S(1)} %bitcast.21), custom_call_target="tpu_custom_call" | custom-call | tf_op jit(solution)/shard_map/pallas_call | solution.py:365
  66.9 4.9 %all-to-all-done.2.refs_0_ = f32[16,16,128]{2,1,0:T(8,128)S(1)} async-done(((f32[16,16,128]{2,1,0:T(8,128)}), f32[16,16,128]{2,1,0:T(8,128)S(1)}, u32[]{:S(2)}, u32[]{:S(2)}) %all-to-all-start.2) | async-done | bytes 131104 | tf_op jit(solution)/shard_map/all_to_all | solution.py:364
  71.8 0.0 collective-permute-done.4.got_ref
  71.8 1.0 %shard_map.84 = (f32[27,16,64]{2,1,0:T(8,128)}, f32[1,16]{1,0:T(1,128)}, bf16[16,2,8,128]{3,2,1,0:T(8,128)(2,1)}, bf16[8,2,8,128]{3,2,1,0:T(8,128)(2,1)}) custom-call(f32[16,16,128]{2,1,0:T(8,128)S(1)} %shard_map.82.sums_ref, f32[2,8,48,128]{3,2,1,0:T(8,128)S(1)} %shard_map.81.part_ref, f32[1,2,8,8,128]{4,3,2,1,0:T(8,128)S(1)} %get-tuple-element.36.keep_ref, ...), custom_call_target="tpu_custom_call" | custom-call | tf_op jit(solution)/shard_map/pallas_call | solution.py:383
  (6 shorter events, 0.1 us)
Async XLA Ops:
  0.6 0.8 %copy-start.3 = (bf16[8,2,8,128]{3,2,1,0:T(8,128)(2,1)S(1)}, bf16[8,2,8,128]{3,2,1,0:T(8,128)(2,1)}, u32[]{:S(2)}) copy-start(bf16[8,2,8,128]{3,2,1,0:T(8,128)(2,1)} %param.4) | copy-start | bytes 98308
  1.5 13.9 %collective-permute-start = (bf16[24,8,128]{2,1,0:T(8,128)(2,1)S(1)}, bf16[24,8,128]{2,1,0:T(8,128)(2,1)S(1)}, u32[]{:S(2)}, u32[]{:S(2)}) collective-permute-start(bf16[24,8,128]{2,1,0:T(8,128)(2,1)S(1)} %get-tuple-element.43), channel_id=1, source_target_pairs={{8,16},{16,8},{24,32},{32,24},{40,48},{48,40},{56,64},{64,56},{72,... | collective-permute-start | bytes 147464 | tf_op jit(solution)/shard_map/ppermute | solution.py:269
  2.9 12.5 %copy-start = (bf16[27,64,16]{1,2,0:T(8,128)(2,1)S(1)}, bf16[27,64,16]{1,2,0:T(8,128)(2,1)}, u32[]{:S(2)}) copy-start(bf16[27,64,16]{1,2,0:T(8,128)(2,1)} %param.5) | copy-start | bytes 165892
  2.9 12.5 %copy-start.1 = (bf16[16,2,8,128]{3,2,1,0:T(8,128)(2,1)S(1)}, bf16[16,2,8,128]{3,2,1,0:T(8,128)(2,1)}, u32[]{:S(2)}) copy-start(bf16[16,2,8,128]{3,2,1,0:T(8,128)(2,1)} %grad_ref.1) | copy-start | bytes 196612
  2.9 18.3 %all-to-all-start = ((bf16[8,2,8,8,128]{4,3,2,1,0:T(8,128)(2,1)}), bf16[8,2,8,8,128]{4,3,2,1,0:T(8,128)(2,1)S(1)}, u32[]{:S(2)}, u32[]{:S(2)}) async-start(bf16[8,2,8,8,128]{4,3,2,1,0:T(8,128)(2,1)} %broadcast_in_dim.2), calls=%async_computation | async-start | bytes 524288 | tf_op jit(solution)/shard_map/all_to_all | solution.py:288
  11.8 6.0 %collective-permute-start.1 = (bf16[24,8,128]{2,1,0:T(8,128)(2,1)S(1)}, bf16[24,8,128]{2,1,0:T(8,128)(2,1)S(1)}, u32[]{:S(2)}, u32[]{:S(2)}) collective-permute-start(bf16[24,8,128]{2,1,0:T(8,128)(2,1)S(1)} %get-tuple-element.42), channel_id=1, source_target_pairs={{0,8},{8,0},{16,24},{24,16},{32,40},{40,32},{48,56},{56,48},{64,72... | collective-permute-start | bytes 147464 | tf_op jit(solution)/shard_map/ppermute | solution.py:268
  18.3 15.1 %collective-permute-start.2 = (bf16[9,2,8,8,128]{4,3,2,1,0:T(8,128)(2,1)S(1)}, bf16[9,2,8,8,128]{4,3,2,1,0:T(8,128)(2,1)S(1)}, u32[]{:S(2)}, u32[]{:S(2)}) collective-permute-start(bf16[9,2,8,8,128]{4,3,2,1,0:T(8,128)(2,1)S(1)} %get-tuple-element.28.sent_ref), channel_id=1, source_target_pairs={{0,2},{1,3},{2,0},{3,1},{4,6},{5,7},{6,4},{7,5},{8,10},{9,11},{10,... | collective-permute-start | bytes 884744 | tf_op jit(solution)/shard_map/ppermute | solution.py:314
  22.6 18.8 %all-to-all-start.1 = ((f32[16,16,128]{2,1,0:T(8,128)}), f32[16,16,128]{2,1,0:T(8,128)S(1)}, u32[]{:S(2)}, u32[]{:S(2)}) async-start(f32[16,16,128]{2,1,0:T(8,128)} %shard_map.77), calls=%async_computation.1 | async-start | bytes 262144 | tf_op jit(solution)/shard_map/all_to_all | solution.py:323
  33.6 25.0 %collective-permute-start.3 = (bf16[6,2,8,8,128]{4,3,2,1,0:T(8,128)(2,1)S(1)}, bf16[6,2,8,8,128]{4,3,2,1,0:T(8,128)(2,1)S(1)}, u32[]{:S(2)}, u32[]{:S(2)}) collective-permute-start(bf16[6,2,8,8,128]{4,3,2,1,0:T(8,128)(2,1)S(1)} %get-tuple-element.29.sent_ref), channel_id=1, source_target_pairs={{0,4},{1,5},{2,6},{3,7},{4,0},{5,1},{6,2},{7,3},{8,12},{9,13},{10,... | collective-permute-start | bytes 589832 | tf_op jit(solution)/shard_map/ppermute | solution.py:335
  59.2 12.6 %all-to-all-start.2 = ((f32[16,16,128]{2,1,0:T(8,128)}), f32[16,16,128]{2,1,0:T(8,128)S(1)}, u32[]{:S(2)}, u32[]{:S(2)}) async-start(f32[16,16,128]{2,1,0:T(8,128)} %shard_map.80), calls=%async_computation.2 | async-start | bytes 262144 | tf_op jit(solution)/shard_map/all_to_all | solution.py:364
  64.0 1.9 %copy-start.2 = (f32[16]{0:T(128)S(1)}, f32[16]{0:T(128)}, u32[]{:S(2)}) copy-start(f32[16]{0:T(128)} %bias_ref.1) | copy-start | bytes 196
  64.0 7.8 %collective-permute-start.4 = (bf16[6,2,8,8,128]{4,3,2,1,0:T(8,128)(2,1)S(1)}, bf16[6,2,8,8,128]{4,3,2,1,0:T(8,128)(2,1)S(1)}, u32[]{:S(2)}, u32[]{:S(2)}) collective-permute-start(bf16[6,2,8,8,128]{4,3,2,1,0:T(8,128)(2,1)S(1)} %get-tuple-element.37.sent_ref), channel_id=1, source_target_pairs={{0,1},{1,0},{2,3},{3,2},{4,5},{5,4},{6,7},{7,6},{8,9},{9,8},{10,11... | collective-permute-start | bytes 589832 | tf_op jit(solution)/shard_map/ppermute | solution.py:363

commit v11 on v10

--- a/solution.py
+++ b/solution.py
@@ -44,28 +44,39 @@
         target[h + 1, 2 * outs : 3 * outs] = slide(wide, -1).astype(BF16)
 
 
-def ready_planes(grad_ref, outer_ref, taps_ref, planes_ref, bias_ref, behind_ref, turned):
+def ready_planes(
+    grad_ref, outer_ref, taps_ref, planes_ref, bias_ref, edge_ref, back_ref, turned
+):
     outs, depth, rows, cols = grad_ref.shape
+    odd = jnp.bitwise_and(lax.axis_index("space"), 1)
+    planes_ref[(depth + 1) * (1 - odd)] = jnp.zeros(planes_ref.shape[1:], BF16)
     total = None
     for d in range(depth):
         plane = grad_ref[:, d].astype(F32)
-        shifted(plane, planes_ref.at[d])
+        shifted(plane, planes_ref.at[d + 1])
         part = jnp.sum(plane, axis=1)
         total = part if total is None else total + part
-    shifted(outer_ref[0:outs].astype(F32), planes_ref.at[depth])
+    shifted(outer_ref[0:outs].astype(F32), planes_ref.at[(depth + 1) * odd])
     half = cols // 2
     bias_ref[...] = total[:, :half] + total[:, half:]
     chans = taps_ref.shape[2]
     share = chans // 8
     turned[...] = taps_ref[...].reshape(27 * outs, chans).astype(F32).T
     me = lax.axis_index("filt")
-    behind_ref[...] = jnp.concatenate(
+    behind = jnp.concatenate(
         [
             turned[pl.ds(pl.multiple_of(share * jnp.bitwise_xor(me, r), share), share)]
             for r in ORDER
         ],
         axis=0,
-    ).astype(BF16)
+    )
+    edge_ref[...] = jnp.where(odd == 1, behind[:, 18 * outs :], behind[:, : 9 * outs]).astype(BF16)
+    behind = behind.astype(BF16)
+    for d in range(depth):
+        for h in range(0, rows, 2):
+            back = dot(behind, moved_rows(planes_ref, d, h))
+            for k in range(2):
+                back_ref[d, h + k] = back[:, k * cols : (k + 1) * cols]
 
 
 def weight_sums(vol_ref, gpad, bias_ref, sums_ref):
@@ -109,22 +120,32 @@
 
 
 def shares_first(
-    planes_ref, behind_ref, outer_ref, inner_ref, gpad, keep_ref, send_ref
+    planes_ref, edge_ref, back_ref, outer_ref, inner_ref, gpad, keep_ref, send_ref
 ):
     _, depth, rows, share, cols = keep_ref.shape
     outs = inner_ref.shape[0] - share
-    for d in range(depth):
-        gpad[d + 1] = planes_ref[d]
     parity = jnp.bitwise_and(lax.axis_index("space"), 1)
-    gpad[(depth + 1) * parity] = planes_ref[depth]
-    shifted(inner_ref[0:outs].astype(F32), gpad.at[(depth + 1) * (1 - parity)])
-    behind = behind_ref[...]
-    for d in range(depth):
-        for h in range(0, rows, 2):
-            back = dot(behind, moved_rows(gpad, d, h))
-            for k in range(2):
+    gpad[...] = planes_ref[...]
+    even = gpad.at[(depth + 1) * (1 - parity)]
+    shifted(inner_ref[0:outs].astype(F32), even)
+    edge = edge_ref[...]
+    near = (depth - 1) * (1 - parity)
+    for h in range(0, rows, 2):
+        moved = jnp.concatenate(
+            [
+                jnp.concatenate([even[h + k + 2 - b] for b in range(3)], axis=0)
+                for k in range(2)
+            ],
+            axis=1,
+        )
+        part = dot(edge, moved)
+        for k in range(2):
+            for d, back in (
+                (near, back_ref[near, h + k] + part[:, k * cols : (k + 1) * cols]),
+                (depth - 1 - near, back_ref[depth - 1 - near, h + k]),
+            ):
                 for r in range(8):
-                    value = back[share * r : share * (r + 1), k * cols : (k + 1) * cols]
+                    value = back[share * r : share * (r + 1)]
                     if r < 4:
                         keep_ref[r, d, h + k] = value
                     else:
@@ -287,15 +308,16 @@
     inner, outer = swap_edges(odd == 1, head, tail)
     vol = lax.all_to_all(jnp.broadcast_to(own[None], (8,) + own.shape), "filt", 0, 0)
     block = (depth, rows, share, cols)
-    planes, bias_sums, behind = pl.pallas_call(
+    planes, bias_sums, edge, known = pl.pallas_call(
         ready_planes,
         out_shape=(
-            jax.ShapeDtypeStruct((depth + 1, rows + 2, 3 * outs, cols), BF16),
+            jax.ShapeDtypeStruct((depth + 2, rows + 2, 3 * outs, cols), BF16),
             jax.ShapeDtypeStruct((outs, cols // 2), F32),
-            jax.ShapeDtypeStruct((chans, 27 * outs), BF16),
+            jax.ShapeDtypeStruct((chans, 9 * outs), BF16),
+            jax.ShapeDtypeStruct((depth, rows, chans, cols), F32),
         ),
         in_specs=[WHOLE] * 3,
-        out_specs=(WHOLE,) * 3,
+        out_specs=(WHOLE,) * 4,
         scratch_shapes=[pltpu.VMEM((chans, 27 * outs), F32)],
         compiler_params=PARAMS,
         cost_estimate=pl.CostEstimate(flops=9_500_000_000, bytes_accessed=0, transcendentals=0),
@@ -307,10 +329,10 @@
             jax.ShapeDtypeStruct((4,) + block, F32),
             jax.ShapeDtypeStruct((9,) + block, BF16),
         ),
-        in_specs=[WHOLE] * 4,
+        in_specs=[WHOLE] * 5,
         out_specs=(WHOLE,) * 3,
         compiler_params=PARAMS,
-    )(planes, behind, outer, inner)
+    )(planes, edge, known, outer, inner)
     got = lax.ppermute(send, "filt", swap_pairs(SWAPS[0]))
     sums = pl.pallas_call(
         weight_sums,

time: 73.4 us -> 73.2 us (level)
  transfers between devices with their start and end apart: 8 -> 8, of which waited for: 4 -> 4; matrix products, arithmetic and copies ran while one was open for 1% -> 1% of each run, Pallas kernels for 4% -> 5%
where the time goes in v11:
time: 73.2 us; the launch traced here: 72.6 us
  starting transfers between devices  37.3 us (51%)
  blocking collectives  17.2 us (23%)
  waiting for transfers between devices  10.7 us (15%)
  Pallas kernels  5.07 us (7%)
  local copies, waits for them, and re-layouts  1.57 us (2%)
  between operations  0.84 us (1%)
    psum x1, blocking collectives, local(): mine = lax.psum(mine, 'space', axis_index_groups=Z_GROUPS)  17.2 us
    all_to_all x1, starting transfers between devices, local(): parts = lax.all_to_all(sums, 'space', 0, 0, axis_index_groups=XY_GROUPS)  10.7 us
    all_to_all x1, starting transfers between devices, local(): lax.all_to_all(jnp.broadcast_to(own[None], (8,) + own.shape), 'filt', 0, 0)  8.93 us
    all_to_all x1, waiting for transfers between devices, local(): every = lax.all_to_all(spread, 'space', 0, 0, axis_index_groups=XY_GROUPS)  4.87 us
    ppermute x1, starting transfers between devices, local(): got = lax.ppermute(send, 'filt', swap_pairs(SWAPS[1]))  4.76 us
    all_to_all x1, starting transfers between devices, local(): every = lax.all_to_all(spread, 'space', 0, 0, axis_index_groups=XY_GROUPS)  4.72 us
    ppermute x1, starting transfers between devices, swap_edges(): inner = lax.ppermute(jnp.where(odd, head, tail), 'space', EVEN)  3.5 us
    all_to_all x1, waiting for transfers between devices, local(): parts = lax.all_to_all(sums, 'space', 0, 0, axis_index_groups=XY_GROUPS)  3 us
  transfers between devices with their start and end apart: 8, of which 4 were waited for; matrix products, arithmetic and copies ran while one was open for 1% of the time, Pallas kernels for 5%

profile of v11, /device:TPU:32, one launch (start us, length us, event | category | flops | bytes accessed | tf_op | source)
XLA Modules:
  0.0 72.6 jit_solution(12113228345861804193)
XLA Ops:
  0.6 0.0 copy-start.3
  0.6 0.8 %slice_bitcast_fusion.1 = (bf16[16,8,128]{2,1,0:T(8,128)(2,1)S(1)}, bf16[16,8,128]{2,1,0:T(8,128)(2,1)S(1)}) fusion(bf16[16,2,8,128]{3,2,1,0:T(8,128)(2,1)} %grad_ref.1), kind=kLoop, calls=%fused_computation.5 | loop fusion | bytes 131072 | tf_op jit(solution)/shard_map/squeeze | solution.py:306
  1.4 0.0 copy-done.3
  1.5 0.7 collective-permute-start
  2.2 0.8 %broadcast_in_dim.2 = bf16[8,2,8,8,128]{4,3,2,1,0:T(8,128)(2,1)} broadcast(bf16[2,8,8,128]{3,2,1,0:T(8,128)(2,1)S(1)} %copy.8), dimensions={1,2,3,4} | broadcast | bytes 294912 | tf_op jit(solution)/shard_map/broadcast_in_dim | solution.py:309
  2.9 0.0 copy-start
  2.9 0.0 copy-start.1
  2.9 8.9 %all-to-all-start = ((bf16[8,2,8,8,128]{4,3,2,1,0:T(8,128)(2,1)}), bf16[8,2,8,8,128]{4,3,2,1,0:T(8,128)(2,1)S(1)}, u32[]{:S(2)}, u32[]{:S(2)}) async-start(bf16[8,2,8,8,128]{4,3,2,1,0:T(8,128)(2,1)} %broadcast_in_dim.2), calls=%async_computation | async-start | bytes 524288 | tf_op jit(solution)/shard_map/all_to_all | solution.py:309
  11.8 3.5 %collective-permute-start.1 = (bf16[24,8,128]{2,1,0:T(8,128)(2,1)S(1)}, bf16[24,8,128]{2,1,0:T(8,128)(2,1)S(1)}, u32[]{:S(2)}, u32[]{:S(2)}) collective-permute-start(bf16[24,8,128]{2,1,0:T(8,128)(2,1)S(1)} %get-tuple-element.44), channel_id=1, source_target_pairs={{0,8},{8,0},{16,24},{24,16},{32,40},{40,32},{48,56},{56,48},{64,72... | collective-permute-start | bytes 147464 | tf_op jit(solution)/shard_map/ppermute | solution.py:289
  15.4 0.0 collective-permute-done.outer_ref
  15.4 0.0 copy-done
  15.4 0.0 copy-done.1
  15.4 0.6 shard_map.75
  16.0 1.8 %collective-permute-done.1.inner_ref = bf16[24,8,128]{2,1,0:T(8,128)(2,1)S(1)} collective-permute-done((bf16[24,8,128]{2,1,0:T(8,128)(2,1)S(1)}, bf16[24,8,128]{2,1,0:T(8,128)(2,1)S(1)}, u32[]{:S(2)}, u32[]{:S(2)}) %collective-permute-start.1) | collective-permute-done | bytes 49184 | tf_op jit(solution)/shard_map/ppermute | solution.py:289
  17.8 0.3 shard_map.76
  18.1 2.1 %collective-permute-start.2 = (bf16[9,2,8,8,128]{4,3,2,1,0:T(8,128)(2,1)S(1)}, bf16[9,2,8,8,128]{4,3,2,1,0:T(8,128)(2,1)S(1)}, u32[]{:S(2)}, u32[]{:S(2)}) collective-permute-start(bf16[9,2,8,8,128]{4,3,2,1,0:T(8,128)(2,1)S(1)} %get-tuple-element.30.sent_ref), channel_id=1, source_target_pairs={{0,2},{1,3},{2,0},{3,1},{4,6},{5,7},{6,4},{7,5},{8,10},{9,11},{10,... | collective-permute-start | bytes 884744 | tf_op jit(solution)/shard_map/ppermute | solution.py:336
  20.2 1.0 %all-to-all-done.vol_ref = bf16[8,2,8,8,128]{4,3,2,1,0:T(8,128)(2,1)S(1)} async-done(((bf16[8,2,8,8,128]{4,3,2,1,0:T(8,128)(2,1)}), bf16[8,2,8,8,128]{4,3,2,1,0:T(8,128)(2,1)S(1)}, u32[]{:S(2)}, u32[]{:S(2)}) %all-to-all-start) | async-done | bytes 262176 | tf_op jit(solution)/shard_map/all_to_all | solution.py:309
  21.2 1.3 %shard_map.77 = f32[16,16,128]{2,1,0:T(8,128)} custom-call(bf16[8,2,8,8,128]{4,3,2,1,0:T(8,128)(2,1)S(1)} %all-to-all-done.vol_ref, bf16[4,10,48,128]{3,2,1,0:T(8,128)(2,1)S(1)} %get-tuple-element.27.gpad, f32[16,64]{1,0:T(8,128)S(1)} %get-tuple-element.28.bias_ref), custom_call_target="tpu_custom_call" | custom-call | flops 6000000000 | tf_op jit(solution)/shard_map/pallas_call | solution.py:337
  22.6 10.7 %all-to-all-start.1 = ((f32[16,16,128]{2,1,0:T(8,128)}), f32[16,16,128]{2,1,0:T(8,128)S(1)}, u32[]{:S(2)}, u32[]{:S(2)}) async-start(f32[16,16,128]{2,1,0:T(8,128)} %shard_map.77), calls=%async_computation.1 | async-start | bytes 262144 | tf_op jit(solution)/shard_map/all_to_all | solution.py:345
  33.3 0.0 collective-permute-done.2.got_ref
  33.3 0.1 shard_map.79
  33.4 4.8 %collective-permute-start.3 = (bf16[6,2,8,8,128]{4,3,2,1,0:T(8,128)(2,1)S(1)}, bf16[6,2,8,8,128]{4,3,2,1,0:T(8,128)(2,1)S(1)}, u32[]{:S(2)}, u32[]{:S(2)}) collective-permute-start(bf16[6,2,8,8,128]{4,3,2,1,0:T(8,128)(2,1)S(1)} %get-tuple-element.31.sent_ref), channel_id=1, source_target_pairs={{0,4},{1,5},{2,6},{3,7},{4,0},{5,1},{6,2},{7,3},{8,12},{9,13},{10,... | collective-permute-start | bytes 589832 | tf_op jit(solution)/shard_map/ppermute | solution.py:357
  38.1 3.0 %all-to-all-done.1.parts_ref = f32[16,16,128]{2,1,0:T(8,128)S(1)} async-done(((f32[16,16,128]{2,1,0:T(8,128)}), f32[16,16,128]{2,1,0:T(8,128)S(1)}, u32[]{:S(2)}, u32[]{:S(2)}) %all-to-all-start.1) | async-done | bytes 131104 | tf_op jit(solution)/shard_map/all_to_all | solution.py:345
  41.1 17.2 %psum.7.mine_ref = f32[16,128]{1,0:T(8,128)S(1)} all-reduce(f32[16,128]{1,0:T(8,128)S(1)} %shard_map.78), channel_id=1, replica_groups={{0,128,256,384},{8,136,264,392},{16,144,272,400},{24,152,280,408},{32,1..., use_global_device_ids=true, to_apply=%region_0.1 | all-reduce | flops 2048 | bytes 16384 | tf_op jit(solution)/shard_map/psum | solution.py:366
  58.3 0.0 collective-permute-done.3.got_ref
  58.3 0.7 shard_map.80
  59.0 4.7 %all-to-all-start.2 = ((f32[16,16,128]{2,1,0:T(8,128)}), f32[16,16,128]{2,1,0:T(8,128)S(1)}, u32[]{:S(2)}, u32[]{:S(2)}) async-start(f32[16,16,128]{2,1,0:T(8,128)} %shard_map.80), calls=%async_computation.2 | async-start | bytes 262144 | tf_op jit(solution)/shard_map/all_to_all | solution.py:386
  63.8 0.0 copy-start.2
  63.8 1.9 %collective-permute-start.4 = (bf16[6,2,8,8,128]{4,3,2,1,0:T(8,128)(2,1)S(1)}, bf16[6,2,8,8,128]{4,3,2,1,0:T(8,128)(2,1)S(1)}, u32[]{:S(2)}, u32[]{:S(2)}) collective-permute-start(bf16[6,2,8,8,128]{4,3,2,1,0:T(8,128)(2,1)S(1)} %get-tuple-element.39.sent_ref), channel_id=1, source_target_pairs={{0,1},{1,0},{2,3},{3,2},{4,5},{5,4},{6,7},{7,6},{8,9},{9,8},{10,11... | collective-permute-start | bytes 589832 | tf_op jit(solution)/shard_map/ppermute | solution.py:385
  65.7 0.0 copy-done.2
  65.7 1.0 %shard_map.81.part_ref = f32[2,8,48,128]{3,2,1,0:T(8,128)S(1)} custom-call(f32[16]{0:T(128)S(1)} %copy-done.2, bf16[8,2,8,8,128]{4,3,2,1,0:T(8,128)(2,1)S(1)} %all-to-all-done.vol_ref, bf16[27,16,64]{2,1,0:T(8,128)(2,1)S(1)} %bitcast.21), custom_call_target="tpu_custom_call" | custom-call | tf_op jit(solution)/shard_map/pallas_call | solution.py:387
  66.7 4.9 %all-to-all-done.2.refs_0_ = f32[16,16,128]{2,1,0:T(8,128)S(1)} async-done(((f32[16,16,128]{2,1,0:T(8,128)}), f32[16,16,128]{2,1,0:T(8,128)S(1)}, u32[]{:S(2)}, u32[]{:S(2)}) %all-to-all-start.2) | async-done | bytes 131104 | tf_op jit(solution)/shard_map/all_to_all | solution.py:386
  71.6 0.0 collective-permute-done.4.got_ref
  71.6 1.0 %shard_map.84 = (f32[27,16,64]{2,1,0:T(8,128)}, f32[1,16]{1,0:T(1,128)}, bf16[16,2,8,128]{3,2,1,0:T(8,128)(2,1)}, bf16[8,2,8,128]{3,2,1,0:T(8,128)(2,1)}) custom-call(f32[16,16,128]{2,1,0:T(8,128)S(1)} %shard_map.82.sums_ref, f32[2,8,48,128]{3,2,1,0:T(8,128)S(1)} %shard_map.81.part_ref, f32[1,2,8,8,128]{4,3,2,1,0:T(8,128)S(1)} %get-tuple-element.38.keep_ref, ...), custom_call_target="tpu_custom_call" | custom-call | tf_op jit(solution)/shard_map/pallas_call | solution.py:405
  (6 shorter events, 0.1 us)
Async XLA Ops:
  0.6 0.8 %copy-start.3 = (bf16[8,2,8,128]{3,2,1,0:T(8,128)(2,1)S(1)}, bf16[8,2,8,128]{3,2,1,0:T(8,128)(2,1)}, u32[]{:S(2)}) copy-start(bf16[8,2,8,128]{3,2,1,0:T(8,128)(2,1)} %param.4) | copy-start | bytes 98308
  1.5 13.9 %collective-permute-start = (bf16[24,8,128]{2,1,0:T(8,128)(2,1)S(1)}, bf16[24,8,128]{2,1,0:T(8,128)(2,1)S(1)}, u32[]{:S(2)}, u32[]{:S(2)}) collective-permute-start(bf16[24,8,128]{2,1,0:T(8,128)(2,1)S(1)} %get-tuple-element.45), channel_id=1, source_target_pairs={{8,16},{16,8},{24,32},{32,24},{40,48},{48,40},{56,64},{64,56},{72,... | collective-permute-start | bytes 147464 | tf_op jit(solution)/shard_map/ppermute | solution.py:290
  2.9 12.5 %copy-start = (bf16[27,64,16]{1,2,0:T(8,128)(2,1)S(1)}, bf16[27,64,16]{1,2,0:T(8,128)(2,1)}, u32[]{:S(2)}) copy-start(bf16[27,64,16]{1,2,0:T(8,128)(2,1)} %param.5) | copy-start | bytes 165892
  2.9 12.5 %copy-start.1 = (bf16[16,2,8,128]{3,2,1,0:T(8,128)(2,1)S(1)}, bf16[16,2,8,128]{3,2,1,0:T(8,128)(2,1)}, u32[]{:S(2)}) copy-start(bf16[16,2,8,128]{3,2,1,0:T(8,128)(2,1)} %grad_ref.1) | copy-start | bytes 196612
  2.9 18.3 %all-to-all-start = ((bf16[8,2,8,8,128]{4,3,2,1,0:T(8,128)(2,1)}), bf16[8,2,8,8,128]{4,3,2,1,0:T(8,128)(2,1)S(1)}, u32[]{:S(2)}, u32[]{:S(2)}) async-start(bf16[8,2,8,8,128]{4,3,2,1,0:T(8,128)(2,1)} %broadcast_in_dim.2), calls=%async_computation | async-start | bytes 524288 | tf_op jit(solution)/shard_map/all_to_all | solution.py:309
  11.8 6.0 %collective-permute-start.1 = (bf16[24,8,128]{2,1,0:T(8,128)(2,1)S(1)}, bf16[24,8,128]{2,1,0:T(8,128)(2,1)S(1)}, u32[]{:S(2)}, u32[]{:S(2)}) collective-permute-start(bf16[24,8,128]{2,1,0:T(8,128)(2,1)S(1)} %get-tuple-element.44), channel_id=1, source_target_pairs={{0,8},{8,0},{16,24},{24,16},{32,40},{40,32},{48,56},{56,48},{64,72... | collective-permute-start | bytes 147464 | tf_op jit(solution)/shard_map/ppermute | solution.py:289
  18.1 15.1 %collective-permute-start.2 = (bf16[9,2,8,8,128]{4,3,2,1,0:T(8,128)(2,1)S(1)}, bf16[9,2,8,8,128]{4,3,2,1,0:T(8,128)(2,1)S(1)}, u32[]{:S(2)}, u32[]{:S(2)}) collective-permute-start(bf16[9,2,8,8,128]{4,3,2,1,0:T(8,128)(2,1)S(1)} %get-tuple-element.30.sent_ref), channel_id=1, source_target_pairs={{0,2},{1,3},{2,0},{3,1},{4,6},{5,7},{6,4},{7,5},{8,10},{9,11},{10,... | collective-permute-start | bytes 884744 | tf_op jit(solution)/shard_map/ppermute | solution.py:336
  22.6 18.6 %all-to-all-start.1 = ((f32[16,16,128]{2,1,0:T(8,128)}), f32[16,16,128]{2,1,0:T(8,128)S(1)}, u32[]{:S(2)}, u32[]{:S(2)}) async-start(f32[16,16,128]{2,1,0:T(8,128)} %shard_map.77), calls=%async_computation.1 | async-start | bytes 262144 | tf_op jit(solution)/shard_map/all_to_all | solution.py:345
  33.4 25.0 %collective-permute-start.3 = (bf16[6,2,8,8,128]{4,3,2,1,0:T(8,128)(2,1)S(1)}, bf16[6,2,8,8,128]{4,3,2,1,0:T(8,128)(2,1)S(1)}, u32[]{:S(2)}, u32[]{:S(2)}) collective-permute-start(bf16[6,2,8,8,128]{4,3,2,1,0:T(8,128)(2,1)S(1)} %get-tuple-element.31.sent_ref), channel_id=1, source_target_pairs={{0,4},{1,5},{2,6},{3,7},{4,0},{5,1},{6,2},{7,3},{8,12},{9,13},{10,... | collective-permute-start | bytes 589832 | tf_op jit(solution)/shard_map/ppermute | solution.py:357
  59.0 12.6 %all-to-all-start.2 = ((f32[16,16,128]{2,1,0:T(8,128)}), f32[16,16,128]{2,1,0:T(8,128)S(1)}, u32[]{:S(2)}, u32[]{:S(2)}) async-start(f32[16,16,128]{2,1,0:T(8,128)} %shard_map.80), calls=%async_computation.2 | async-start | bytes 262144 | tf_op jit(solution)/shard_map/all_to_all | solution.py:386
  63.8 1.9 %copy-start.2 = (f32[16]{0:T(128)S(1)}, f32[16]{0:T(128)}, u32[]{:S(2)}) copy-start(f32[16]{0:T(128)} %bias_ref.1) | copy-start | bytes 196
  63.8 7.8 %collective-permute-start.4 = (bf16[6,2,8,8,128]{4,3,2,1,0:T(8,128)(2,1)S(1)}, bf16[6,2,8,8,128]{4,3,2,1,0:T(8,128)(2,1)S(1)}, u32[]{:S(2)}, u32[]{:S(2)}) collective-permute-start(bf16[6,2,8,8,128]{4,3,2,1,0:T(8,128)(2,1)S(1)} %get-tuple-element.39.sent_ref), channel_id=1, source_target_pairs={{0,1},{1,0},{2,3},{3,2},{4,5},{5,4},{6,7},{7,6},{8,9},{9,8},{10,11... | collective-permute-start | bytes 589832 | tf_op jit(solution)/shard_map/ppermute | solution.py:385

commit v12 on v11

--- a/solution.py
+++ b/solution.py
@@ -83,17 +83,19 @@
     peers, depth, rows, share, cols = vol_ref.shape
     outs = bias_ref.shape[0]
     chans = peers * share
-    acc = jnp.zeros((27 * outs, chans), F32)
-    for d in range(depth):
-        for h in range(0, rows, 2):
-            cells = jnp.concatenate(
-                [
-                    jnp.concatenate([vol_ref[s, d, h + k] for s in range(peers)], axis=0)
-                    for k in range(2)
-                ],
-                axis=1,
-            )
-            acc = acc + dot_lanes(moved_rows(gpad, d, h), cells)
+    acc = None
+    for places in [[(d, h) for h in range(0, rows, 2)] for d in range(depth)]:
+        cells = jnp.concatenate(
+            [
+                jnp.concatenate([vol_ref[s, d, h + k] for s in range(peers)], axis=0)
+                for d, h in places
+                for k in range(2)
+            ],
+            axis=1,
+        )
+        moved = jnp.concatenate([moved_rows(gpad, d, h) for d, h in places], axis=1)
+        part = dot_lanes(moved, cells)
+        acc = part if acc is None else acc + part
     for r in range(14):
         first = acc[2 * r * outs : (2 * r + 1) * outs]
         second = bias_ref[...] if r == 13 else acc[(2 * r + 1) * outs : (2 * r + 2) * outs]
@@ -205,7 +207,7 @@
     )
 
 
-def own_output(bias_ref, vol_ref, taps_ref, part_ref, vpad):
+def own_output(bias_ref, vol_ref, taps_ref, part_ref, edges_ref, vpad, turned):
     peers, depth, rows, _, cols = vol_ref.shape
     taps = taps_ref[...]
     outs, chans = taps.shape[1:]
@@ -228,15 +230,30 @@
             part = dot(ahead, stack) + bias
             for k in range(2):
                 part_ref[d, h + k] = part[:, k * cols : (k + 1) * cols]
+    share = chans // peers
+    turned[...] = taps.reshape(27 * outs, chans).astype(F32).T
+    me = lax.axis_index("filt")
+    first, second, third = SWAPS
+    near = (0, first, second, first ^ second)
+    lines = jnp.concatenate(
+        [
+            turned[pl.ds(pl.multiple_of(share * jnp.bitwise_xor(me, r), share), share)]
+            for r in near + tuple(r ^ third for r in near)
+        ],
+        axis=0,
+    ).T.astype(BF16)
+    lines = [lines[outs * t : outs * (t + 1)] for t in range(27)]
+    for d in range(depth):
+        edges_ref[d] = weights_ahead(lines, [2 * d])
 
 
 def finish(
-    sums_ref, part_ref, keep_ref, sent_ref, got_ref, taps_ref,
-    weight_ref, bias_ref, out_ref, back_ref, halo, vpad,
+    sums_ref, part_ref, keep_ref, sent_ref, got_ref, edges_ref,
+    weight_ref, bias_ref, out_ref, back_ref, vpad,
 ):
     depth, rows, _, cols = part_ref.shape
-    taps = taps_ref[...]
-    outs, chans = taps.shape[1:]
+    outs = sums_ref.shape[1]
+    chans = vpad.shape[2]
     half = cols // 2
     for t in range(27):
         r, side = t // 2, t % 2
@@ -247,14 +264,10 @@
     lane = lax.broadcasted_iota(jnp.int32, (outs, cols), 1)
     flat = jnp.sum(jnp.where(row == lane, wide, 0.0), axis=0, keepdims=True)
     bias_ref[...] = flat[:, :outs]
-    me = lax.axis_index("filt")
-    first, second, third = SWAPS
-    for place, r in enumerate((0, first, second, first ^ second)):
-        halo[jnp.bitwise_xor(me, r)] = sent_ref[2 + place]
-        halo[jnp.bitwise_xor(me, r ^ third)] = got_ref[2 + place]
-    for d in range(depth):
-        padded_plane(vpad.at[d], [[halo[s, d, h] for s in range(8)] for h in range(rows)])
-        ahead = weights_ahead(taps, [2 * d])
+    for d in range(depth):
+        blocks = [ref.at[2 + n, d] for ref in (sent_ref, got_ref) for n in range(4)]
+        padded_plane(vpad.at[d], [[block[h] for block in blocks] for h in range(rows)])
+        ahead = edges_ref[d]
         lines = []
         for h in range(0, rows, 2):
             stack = jnp.concatenate(
@@ -384,12 +397,18 @@
     )(keep, send, got)
     got = lax.ppermute(send, "filt", swap_pairs(SWAPS[2]))
     every = lax.all_to_all(spread, "space", 0, 0, axis_index_groups=XY_GROUPS)
-    part = pl.pallas_call(
+    part, edges = pl.pallas_call(
         own_output,
-        out_shape=jax.ShapeDtypeStruct((depth, rows, 3 * outs, cols), F32),
+        out_shape=(
+            jax.ShapeDtypeStruct((depth, rows, 3 * outs, cols), F32),
+            jax.ShapeDtypeStruct((depth, 3 * outs, 3 * chans), BF16),
+        ),
         in_specs=[SCALAR] + [WHOLE] * 2,
-        out_specs=WHOLE,
-        scratch_shapes=[pltpu.VMEM((depth, rows + 2, chans, cols), BF16)],
+        out_specs=(WHOLE,) * 2,
+        scratch_shapes=[
+            pltpu.VMEM((depth, rows + 2, chans, cols), BF16),
+            pltpu.VMEM((chans, 27 * outs), F32),
+        ],
         compiler_params=PARAMS,
     )(bias, held, taps)
     every, part = lax.optimization_barrier((every, part))
@@ -412,12 +431,9 @@
         ),
         in_specs=[WHOLE] * 6,
         out_specs=(WHOLE,) * 4,
-        scratch_shapes=[
-            pltpu.VMEM((8,) + block, BF16),
-            pltpu.VMEM((depth, rows + 2, chans, cols), BF16),
-        ],
-        compiler_params=PARAMS,
-    )(every, part, keep, send, got, taps)
+        scratch_shapes=[pltpu.VMEM((depth, rows + 2, chans, cols), BF16)],
+        compiler_params=PARAMS,
+    )(every, part, keep, send, got, edges)
     return (output, grad_volume, grad_taps.transpose(0, 2, 1), grad_bias.reshape(outs))
 
 

time: 73.2 us -> 73.2 us (level)
  no operation moved by 1% of the time
where the time goes in v12:
time: 73.2 us; the launch traced here: 72.6 us
  starting transfers between devices  37.3 us (51%)
  blocking collectives  17.2 us (23%)
  waiting for transfers between devices  10.7 us (15%)
  Pallas kernels  5.07 us (7%)
  local copies, waits for them, and re-layouts  1.57 us (2%)
  between operations  0.84 us (1%)
    psum x1, blocking collectives, local(): mine = lax.psum(mine, 'space', axis_index_groups=Z_GROUPS)  17.2 us
    all_to_all x1, starting transfers between devices, local(): parts = lax.all_to_all(sums, 'space', 0, 0, axis_index_groups=XY_GROUPS)  10.7 us
    all_to_all x1, starting transfers between devices, local(): lax.all_to_all(jnp.broadcast_to(own[None], (8,) + own.shape), 'filt', 0, 0)  8.93 us
    all_to_all x1, waiting for transfers between devices, local(): every = lax.all_to_all(spread, 'space', 0, 0, axis_index_groups=XY_GROUPS)  4.86 us
    ppermute x1, starting transfers between devices, local(): got = lax.ppermute(send, 'filt', swap_pairs(SWAPS[1]))  4.77 us
    all_to_all x1, starting transfers between devices, local(): every = lax.all_to_all(spread, 'space', 0, 0, axis_index_groups=XY_GROUPS)  4.72 us
    ppermute x1, starting transfers between devices, swap_edges(): inner = lax.ppermute(jnp.where(odd, head, tail), 'space', EVEN)  3.5 us
    all_to_all x1, waiting for transfers between devices, local(): parts = lax.all_to_all(sums, 'space', 0, 0, axis_index_groups=XY_GROUPS)  2.99 us
  transfers between devices with their start and end apart: 8, of which 4 were waited for; matrix products, arithmetic and copies ran while one was open for 1% of the time, Pallas kernels for 5%

profile of v12, /device:TPU:32, one launch (start us, length us, event | category | flops | bytes accessed | tf_op | source)
XLA Modules:
  0.0 72.6 jit_solution(14977521229272028993)
XLA Ops:
  0.6 0.0 copy-start.3
  0.6 0.8 %slice_bitcast_fusion.1 = (bf16[16,8,128]{2,1,0:T(8,128)(2,1)S(1)}, bf16[16,8,128]{2,1,0:T(8,128)(2,1)S(1)}) fusion(bf16[16,2,8,128]{3,2,1,0:T(8,128)(2,1)} %grad_ref.1), kind=kLoop, calls=%fused_computation.5 | loop fusion | bytes 131072 | tf_op jit(solution)/shard_map/squeeze | solution.py:319
  1.4 0.0 copy-done.3
  1.5 0.7 collective-permute-start
  2.2 0.7 %broadcast_in_dim.2 = bf16[8,2,8,8,128]{4,3,2,1,0:T(8,128)(2,1)} broadcast(bf16[2,8,8,128]{3,2,1,0:T(8,128)(2,1)S(1)} %copy.8), dimensions={1,2,3,4} | broadcast | bytes 294912 | tf_op jit(solution)/shard_map/broadcast_in_dim | solution.py:322
  2.9 0.0 copy-start
  2.9 0.0 copy-start.1
  2.9 8.9 %all-to-all-start = ((bf16[8,2,8,8,128]{4,3,2,1,0:T(8,128)(2,1)}), bf16[8,2,8,8,128]{4,3,2,1,0:T(8,128)(2,1)S(1)}, u32[]{:S(2)}, u32[]{:S(2)}) async-start(bf16[8,2,8,8,128]{4,3,2,1,0:T(8,128)(2,1)} %broadcast_in_dim.2), calls=%async_computation | async-start | bytes 524288 | tf_op jit(solution)/shard_map/all_to_all | solution.py:322
  11.8 3.5 %collective-permute-start.1 = (bf16[24,8,128]{2,1,0:T(8,128)(2,1)S(1)}, bf16[24,8,128]{2,1,0:T(8,128)(2,1)S(1)}, u32[]{:S(2)}, u32[]{:S(2)}) collective-permute-start(bf16[24,8,128]{2,1,0:T(8,128)(2,1)S(1)} %get-tuple-element.48), channel_id=1, source_target_pairs={{0,8},{8,0},{16,24},{24,16},{32,40},{40,32},{48,56},{56,48},{64,72... | collective-permute-start | bytes 147464 | tf_op jit(solution)/shard_map/ppermute | solution.py:302
  15.3 0.0 collective-permute-done.outer_ref
  15.4 0.0 copy-done
  15.4 0.0 copy-done.1
  15.4 0.6 shard_map.75
  16.0 1.8 %collective-permute-done.1.inner_ref = bf16[24,8,128]{2,1,0:T(8,128)(2,1)S(1)} collective-permute-done((bf16[24,8,128]{2,1,0:T(8,128)(2,1)S(1)}, bf16[24,8,128]{2,1,0:T(8,128)(2,1)S(1)}, u32[]{:S(2)}, u32[]{:S(2)}) %collective-permute-start.1) | collective-permute-done | bytes 49184 | tf_op jit(solution)/shard_map/ppermute | solution.py:302
  17.8 0.3 shard_map.76
  18.1 2.0 %collective-permute-start.2 = (bf16[9,2,8,8,128]{4,3,2,1,0:T(8,128)(2,1)S(1)}, bf16[9,2,8,8,128]{4,3,2,1,0:T(8,128)(2,1)S(1)}, u32[]{:S(2)}, u32[]{:S(2)}) collective-permute-start(bf16[9,2,8,8,128]{4,3,2,1,0:T(8,128)(2,1)S(1)} %get-tuple-element.32.sent_ref), channel_id=1, source_target_pairs={{0,2},{1,3},{2,0},{3,1},{4,6},{5,7},{6,4},{7,5},{8,10},{9,11},{10,... | collective-permute-start | bytes 884744 | tf_op jit(solution)/shard_map/ppermute | solution.py:349
  20.2 1.0 %all-to-all-done.vol_ref = bf16[8,2,8,8,128]{4,3,2,1,0:T(8,128)(2,1)S(1)} async-done(((bf16[8,2,8,8,128]{4,3,2,1,0:T(8,128)(2,1)}), bf16[8,2,8,8,128]{4,3,2,1,0:T(8,128)(2,1)S(1)}, u32[]{:S(2)}, u32[]{:S(2)}) %all-to-all-start) | async-done | bytes 262176 | tf_op jit(solution)/shard_map/all_to_all | solution.py:322
  21.2 1.3 %shard_map.77 = f32[16,16,128]{2,1,0:T(8,128)} custom-call(bf16[8,2,8,8,128]{4,3,2,1,0:T(8,128)(2,1)S(1)} %all-to-all-done.vol_ref, bf16[4,10,48,128]{3,2,1,0:T(8,128)(2,1)S(1)} %get-tuple-element.29.gpad, f32[16,64]{1,0:T(8,128)S(1)} %get-tuple-element.30.bias_ref), custom_call_target="tpu_custom_call" | custom-call | flops 6000000000 | tf_op jit(solution)/shard_map/pallas_call | solution.py:350
  22.6 10.7 %all-to-all-start.1 = ((f32[16,16,128]{2,1,0:T(8,128)}), f32[16,16,128]{2,1,0:T(8,128)S(1)}, u32[]{:S(2)}, u32[]{:S(2)}) async-start(f32[16,16,128]{2,1,0:T(8,128)} %shard_map.77), calls=%async_computation.1 | async-start | bytes 262144 | tf_op jit(solution)/shard_map/all_to_all | solution.py:358
  33.3 0.0 collective-permute-done.2.got_ref
  33.3 0.1 shard_map.79
  33.3 4.8 %collective-permute-start.3 = (bf16[6,2,8,8,128]{4,3,2,1,0:T(8,128)(2,1)S(1)}, bf16[6,2,8,8,128]{4,3,2,1,0:T(8,128)(2,1)S(1)}, u32[]{:S(2)}, u32[]{:S(2)}) collective-permute-start(bf16[6,2,8,8,128]{4,3,2,1,0:T(8,128)(2,1)S(1)} %get-tuple-element.33.sent_ref), channel_id=1, source_target_pairs={{0,4},{1,5},{2,6},{3,7},{4,0},{5,1},{6,2},{7,3},{8,12},{9,13},{10,... | collective-permute-start | bytes 589832 | tf_op jit(solution)/shard_map/ppermute | solution.py:370
  38.1 3.0 %all-to-all-done.1.parts_ref = f32[16,16,128]{2,1,0:T(8,128)S(1)} async-done(((f32[16,16,128]{2,1,0:T(8,128)}), f32[16,16,128]{2,1,0:T(8,128)S(1)}, u32[]{:S(2)}, u32[]{:S(2)}) %all-to-all-start.1) | async-done | bytes 131104 | tf_op jit(solution)/shard_map/all_to_all | solution.py:358
  41.1 17.2 %psum.7.mine_ref = f32[16,128]{1,0:T(8,128)S(1)} all-reduce(f32[16,128]{1,0:T(8,128)S(1)} %shard_map.78), channel_id=1, replica_groups={{0,128,256,384},{8,136,264,392},{16,144,272,400},{24,152,280,408},{32,1..., use_global_device_ids=true, to_apply=%region_0.1 | all-reduce | flops 2048 | bytes 16384 | tf_op jit(solution)/shard_map/psum | solution.py:379
  58.3 0.0 collective-permute-done.3.got_ref
  58.3 0.7 shard_map.80
  59.0 4.7 %all-to-all-start.2 = ((f32[16,16,128]{2,1,0:T(8,128)}), f32[16,16,128]{2,1,0:T(8,128)S(1)}, u32[]{:S(2)}, u32[]{:S(2)}) async-start(f32[16,16,128]{2,1,0:T(8,128)} %shard_map.80), calls=%async_computation.2 | async-start | bytes 262144 | tf_op jit(solution)/shard_map/all_to_all | solution.py:399
  63.7 0.0 copy-start.2
  63.8 1.9 %collective-permute-start.4 = (bf16[6,2,8,8,128]{4,3,2,1,0:T(8,128)(2,1)S(1)}, bf16[6,2,8,8,128]{4,3,2,1,0:T(8,128)(2,1)S(1)}, u32[]{:S(2)}, u32[]{:S(2)}) collective-permute-start(bf16[6,2,8,8,128]{4,3,2,1,0:T(8,128)(2,1)S(1)} %get-tuple-element.42.sent_ref), channel_id=1, source_target_pairs={{0,1},{1,0},{2,3},{3,2},{4,5},{5,4},{6,7},{7,6},{8,9},{9,8},{10,11... | collective-permute-start | bytes 589832 | tf_op jit(solution)/shard_map/ppermute | solution.py:398
  65.7 0.0 copy-done.2
  65.7 1.0 %shard_map.81 = (f32[2,8,48,128]{3,2,1,0:T(8,128)S(1)}, bf16[2,48,192]{2,1,0:T(8,128)(2,1)S(1)}) custom-call(f32[16]{0:T(128)S(1)} %copy-done.2, bf16[8,2,8,8,128]{4,3,2,1,0:T(8,128)(2,1)S(1)} %all-to-all-done.vol_ref, bf16[27,16,64]{2,1,0:T(8,128)(2,1)S(1)} %bitcast.21), custom_call_target="tpu_custom_call" | custom-call | tf_op jit(solution)/shard_map/pallas_call | solution.py:400
  66.7 4.9 %all-to-all-done.2.refs_0_ = f32[16,16,128]{2,1,0:T(8,128)S(1)} async-done(((f32[16,16,128]{2,1,0:T(8,128)}), f32[16,16,128]{2,1,0:T(8,128)S(1)}, u32[]{:S(2)}, u32[]{:S(2)}) %all-to-all-start.2) | async-done | bytes 131104 | tf_op jit(solution)/shard_map/all_to_all | solution.py:399
  71.6 0.0 collective-permute-done.4.got_ref
  71.6 1.0 %shard_map.84 = (f32[27,16,64]{2,1,0:T(8,128)}, f32[1,16]{1,0:T(1,128)}, bf16[16,2,8,128]{3,2,1,0:T(8,128)(2,1)}, bf16[8,2,8,128]{3,2,1,0:T(8,128)(2,1)}) custom-call(f32[16,16,128]{2,1,0:T(8,128)S(1)} %shard_map.82.sums_ref, f32[2,8,48,128]{3,2,1,0:T(8,128)S(1)} %get-tuple-element.38.part_ref, f32[1,2,8,8,128]{4,3,2,1,0:T(8,128)S(1)} %get-tuple-element.41.keep_ref, ...), custom_call_target="tpu_custom_call" | custom-call | tf_op jit(solution)/shard_map/pallas_call | solution.py:424
  (6 shorter events, 0.1 us)
Async XLA Ops:
  0.6 0.8 %copy-start.3 = (bf16[8,2,8,128]{3,2,1,0:T(8,128)(2,1)S(1)}, bf16[8,2,8,128]{3,2,1,0:T(8,128)(2,1)}, u32[]{:S(2)}) copy-start(bf16[8,2,8,128]{3,2,1,0:T(8,128)(2,1)} %param.4) | copy-start | bytes 98308
  1.5 13.9 %collective-permute-start = (bf16[24,8,128]{2,1,0:T(8,128)(2,1)S(1)}, bf16[24,8,128]{2,1,0:T(8,128)(2,1)S(1)}, u32[]{:S(2)}, u32[]{:S(2)}) collective-permute-start(bf16[24,8,128]{2,1,0:T(8,128)(2,1)S(1)} %get-tuple-element.49), channel_id=1, source_target_pairs={{8,16},{16,8},{24,32},{32,24},{40,48},{48,40},{56,64},{64,56},{72,... | collective-permute-start | bytes 147464 | tf_op jit(solution)/shard_map/ppermute | solution.py:303
  2.9 12.5 %copy-start = (bf16[27,64,16]{1,2,0:T(8,128)(2,1)S(1)}, bf16[27,64,16]{1,2,0:T(8,128)(2,1)}, u32[]{:S(2)}) copy-start(bf16[27,64,16]{1,2,0:T(8,128)(2,1)} %param.5) | copy-start | bytes 165892
  2.9 12.5 %copy-start.1 = (bf16[16,2,8,128]{3,2,1,0:T(8,128)(2,1)S(1)}, bf16[16,2,8,128]{3,2,1,0:T(8,128)(2,1)}, u32[]{:S(2)}) copy-start(bf16[16,2,8,128]{3,2,1,0:T(8,128)(2,1)} %grad_ref.1) | copy-start | bytes 196612
  2.9 18.3 %all-to-all-start = ((bf16[8,2,8,8,128]{4,3,2,1,0:T(8,128)(2,1)}), bf16[8,2,8,8,128]{4,3,2,1,0:T(8,128)(2,1)S(1)}, u32[]{:S(2)}, u32[]{:S(2)}) async-start(bf16[8,2,8,8,128]{4,3,2,1,0:T(8,128)(2,1)} %broadcast_in_dim.2), calls=%async_computation | async-start | bytes 524288 | tf_op jit(solution)/shard_map/all_to_all | solution.py:322
  11.8 6.0 %collective-permute-start.1 = (bf16[24,8,128]{2,1,0:T(8,128)(2,1)S(1)}, bf16[24,8,128]{2,1,0:T(8,128)(2,1)S(1)}, u32[]{:S(2)}, u32[]{:S(2)}) collective-permute-start(bf16[24,8,128]{2,1,0:T(8,128)(2,1)S(1)} %get-tuple-element.48), channel_id=1, source_target_pairs={{0,8},{8,0},{16,24},{24,16},{32,40},{40,32},{48,56},{56,48},{64,72... | collective-permute-start | bytes 147464 | tf_op jit(solution)/shard_map/ppermute | solution.py:302
  18.1 15.1 %collective-permute-start.2 = (bf16[9,2,8,8,128]{4,3,2,1,0:T(8,128)(2,1)S(1)}, bf16[9,2,8,8,128]{4,3,2,1,0:T(8,128)(2,1)S(1)}, u32[]{:S(2)}, u32[]{:S(2)}) collective-permute-start(bf16[9,2,8,8,128]{4,3,2,1,0:T(8,128)(2,1)S(1)} %get-tuple-element.32.sent_ref), channel_id=1, source_target_pairs={{0,2},{1,3},{2,0},{3,1},{4,6},{5,7},{6,4},{7,5},{8,10},{9,11},{10,... | collective-permute-start | bytes 884744 | tf_op jit(solution)/shard_map/ppermute | solution.py:349
  22.6 18.6 %all-to-all-start.1 = ((f32[16,16,128]{2,1,0:T(8,128)}), f32[16,16,128]{2,1,0:T(8,128)S(1)}, u32[]{:S(2)}, u32[]{:S(2)}) async-start(f32[16,16,128]{2,1,0:T(8,128)} %shard_map.77), calls=%async_computation.1 | async-start | bytes 262144 | tf_op jit(solution)/shard_map/all_to_all | solution.py:358
  33.3 25.0 %collective-permute-start.3 = (bf16[6,2,8,8,128]{4,3,2,1,0:T(8,128)(2,1)S(1)}, bf16[6,2,8,8,128]{4,3,2,1,0:T(8,128)(2,1)S(1)}, u32[]{:S(2)}, u32[]{:S(2)}) collective-permute-start(bf16[6,2,8,8,128]{4,3,2,1,0:T(8,128)(2,1)S(1)} %get-tuple-element.33.sent_ref), channel_id=1, source_target_pairs={{0,4},{1,5},{2,6},{3,7},{4,0},{5,1},{6,2},{7,3},{8,12},{9,13},{10,... | collective-permute-start | bytes 589832 | tf_op jit(solution)/shard_map/ppermute | solution.py:370
  59.0 12.6 %all-to-all-start.2 = ((f32[16,16,128]{2,1,0:T(8,128)}), f32[16,16,128]{2,1,0:T(8,128)S(1)}, u32[]{:S(2)}, u32[]{:S(2)}) async-start(f32[16,16,128]{2,1,0:T(8,128)} %shard_map.80), calls=%async_computation.2 | async-start | bytes 262144 | tf_op jit(solution)/shard_map/all_to_all | solution.py:399
  63.7 1.9 %copy-start.2 = (f32[16]{0:T(128)S(1)}, f32[16]{0:T(128)}, u32[]{:S(2)}) copy-start(f32[16]{0:T(128)} %bias_ref.1) | copy-start | bytes 196
  63.8 7.8 %collective-permute-start.4 = (bf16[6,2,8,8,128]{4,3,2,1,0:T(8,128)(2,1)S(1)}, bf16[6,2,8,8,128]{4,3,2,1,0:T(8,128)(2,1)S(1)}, u32[]{:S(2)}, u32[]{:S(2)}) collective-permute-start(bf16[6,2,8,8,128]{4,3,2,1,0:T(8,128)(2,1)S(1)} %get-tuple-element.42.sent_ref), channel_id=1, source_target_pairs={{0,1},{1,0},{2,3},{3,2},{4,5},{5,4},{6,7},{7,6},{8,9},{9,8},{10,11... | collective-permute-start | bytes 589832 | tf_op jit(solution)/shard_map/ppermute | solution.py:398

commit v13 on v11

--- a/solution.py
+++ b/solution.py
@@ -285,12 +285,6 @@
 ODD = [(i, ((i + 1) ^ 1) - 1) for i in range(1, 63)]
 
 
-def swap_edges(odd, head, tail):
-    inner = lax.ppermute(jnp.where(odd, head, tail), "space", EVEN)
-    outer = lax.ppermute(jnp.where(odd, tail, head), "space", ODD)
-    return inner, outer
-
-
 def swap_pairs(bit):
     return [(f, f ^ bit) for f in range(8)]
 
@@ -302,10 +296,20 @@
     taps = weight.transpose(0, 2, 1)
     own = volume.transpose(1, 2, 0, 3)
     odd = jnp.bitwise_and(lax.axis_index("space").astype(jnp.int32), 1)
-    head, tail = (
-        jnp.concatenate([grad_out[:, d], volume[:, d]], axis=0) for d in (0, depth - 1)
-    )
-    inner, outer = swap_edges(odd == 1, head, tail)
+    inner, outer = (
+        lax.ppermute(
+            jnp.concatenate(
+                [
+                    lax.dynamic_index_in_dim(cells, plane, axis=1, keepdims=False)
+                    for cells in (grad_out, volume)
+                ],
+                axis=0,
+            ),
+            "space",
+            pairs,
+        )
+        for plane, pairs in (((depth - 1) * (1 - odd), EVEN), ((depth - 1) * odd, ODD))
+    )
     vol = lax.all_to_all(jnp.broadcast_to(own[None], (8,) + own.shape), "filt", 0, 0)
     block = (depth, rows, share, cols)
     planes, bias_sums, edge, known = pl.pallas_call(

time: 73.2 us -> 73.4 us (level)
  no operation moved by 1% of the time
where the time goes in v13:
time: 73.4 us; the launch traced here: 72.8 us
  starting transfers between devices  37.5 us (51%)
  blocking collectives  17.1 us (23%)
  waiting for transfers between devices  10.6 us (14%)
  Pallas kernels  5.07 us (7%)
  local copies, waits for them, and re-layouts  1.57 us (2%)
  between operations  0.84 us (1%)
    psum x1, blocking collectives, local(): mine = lax.psum(mine, 'space', axis_index_groups=Z_GROUPS)  17.1 us
    all_to_all x1, starting transfers between devices, local(): parts = lax.all_to_all(sums, 'space', 0, 0, axis_index_groups=XY_GROUPS)  10.9 us
    all_to_all x1, starting transfers between devices, local(): lax.all_to_all(jnp.broadcast_to(own[None], (8,) + own.shape), 'filt', 0, 0)  8.93 us
    all_to_all x1, waiting for transfers between devices, local(): every = lax.all_to_all(spread, 'space', 0, 0, axis_index_groups=XY_GROUPS)  4.87 us
    ppermute x1, starting transfers between devices, local(): got = lax.ppermute(send, 'filt', swap_pairs(SWAPS[1]))  4.77 us
    all_to_all x1, starting transfers between devices, local(): every = lax.all_to_all(spread, 'space', 0, 0, axis_index_groups=XY_GROUPS)  4.73 us
    ppermute x2, starting transfers between devices, local(): lax.ppermute(jnp.concatenate([lax.dynamic_index_in_dim(cells, plane, axis...  4.31 us
    all_to_all x1, waiting for transfers between devices, local(): parts = lax.all_to_all(sums, 'space', 0, 0, axis_index_groups=XY_GROUPS)  2.99 us
  transfers between devices with their start and end apart: 8, of which 4 were waited for; matrix products, arithmetic and copies ran while one was open for 1% of the time, Pallas kernels for 5%

profile of v13, /device:TPU:32, one launch (start us, length us, event | category | flops | bytes accessed | tf_op | source)
XLA Modules:
  0.0 72.8 jit_solution(17789889579216204715)
XLA Ops:
  0.6 0.0 copy-start.3
  0.6 0.8 %dynamic-slice_bitcast_fusion = (bf16[16,8,128]{2,1,0:T(8,128)(2,1)S(1)}, bf16[16,8,128]{2,1,0:T(8,128)(2,1)S(1)}) fusion(bf16[16,2,8,128]{3,2,1,0:T(8,128)(2,1)} %grad_ref.1, s32[]{:T(128)S(6)} %select_n.11, s32[]{:T(128)S(6)} %select_n.10), kind=kLoop, calls=%fused_computation.2 | loop fusion | bytes 131080 | tf_op jit(solution)/shard_map/jit(dynamic_index_in_dim)/squeeze | solution.py:303
  1.4 0.0 copy-done.3
  1.5 0.7 collective-permute-start
  2.2 0.7 %broadcast_in_dim.2 = bf16[8,2,8,8,128]{4,3,2,1,0:T(8,128)(2,1)} broadcast(bf16[2,8,8,128]{3,2,1,0:T(8,128)(2,1)S(1)} %copy.8), dimensions={1,2,3,4} | broadcast | bytes 294912 | tf_op jit(solution)/shard_map/broadcast_in_dim | solution.py:313
  2.9 0.0 copy-start
  2.9 8.9 %all-to-all-start = ((bf16[8,2,8,8,128]{4,3,2,1,0:T(8,128)(2,1)}), bf16[8,2,8,8,128]{4,3,2,1,0:T(8,128)(2,1)S(1)}, u32[]{:S(2)}, u32[]{:S(2)}) async-start(bf16[8,2,8,8,128]{4,3,2,1,0:T(8,128)(2,1)} %broadcast_in_dim.2), calls=%async_computation | async-start | bytes 524288 | tf_op jit(solution)/shard_map/all_to_all | solution.py:313
  11.8 0.0 copy-start.1
  11.8 3.6 %collective-permute-start.1 = (bf16[24,8,128]{2,1,0:T(8,128)(2,1)S(1)}, bf16[24,8,128]{2,1,0:T(8,128)(2,1)S(1)}, u32[]{:S(2)}, u32[]{:S(2)}) collective-permute-start(bf16[24,8,128]{2,1,0:T(8,128)(2,1)S(1)} %pad_maximum_fusion.1), channel_id=1, source_target_pairs={{0,8},{8,0},{16,24},{24,16},{32,40},{40,32},{48,56},{56,48},{64,72... | collective-permute-start | bytes 147464 | tf_op jit(solution)/shard_map/ppermute | solution.py:300
  15.5 0.0 collective-permute-done.outer_ref
  15.5 0.0 copy-done
  15.5 0.0 copy-done.1
  15.5 0.6 shard_map.75
  16.2 1.8 %collective-permute-done.1.inner_ref = bf16[24,8,128]{2,1,0:T(8,128)(2,1)S(1)} collective-permute-done((bf16[24,8,128]{2,1,0:T(8,128)(2,1)S(1)}, bf16[24,8,128]{2,1,0:T(8,128)(2,1)S(1)}, u32[]{:S(2)}, u32[]{:S(2)}) %collective-permute-start.1) | collective-permute-done | bytes 49184 | tf_op jit(solution)/shard_map/ppermute | solution.py:300
  18.0 0.3 shard_map.76
  18.3 2.0 %collective-permute-start.2 = (bf16[9,2,8,8,128]{4,3,2,1,0:T(8,128)(2,1)S(1)}, bf16[9,2,8,8,128]{4,3,2,1,0:T(8,128)(2,1)S(1)}, u32[]{:S(2)}, u32[]{:S(2)}) collective-permute-start(bf16[9,2,8,8,128]{4,3,2,1,0:T(8,128)(2,1)S(1)} %get-tuple-element.30.sent_ref), channel_id=1, source_target_pairs={{0,2},{1,3},{2,0},{3,1},{4,6},{5,7},{6,4},{7,5},{8,10},{9,11},{10,... | collective-permute-start | bytes 884744 | tf_op jit(solution)/shard_map/ppermute | solution.py:340
  20.3 1.0 %all-to-all-done.vol_ref = bf16[8,2,8,8,128]{4,3,2,1,0:T(8,128)(2,1)S(1)} async-done(((bf16[8,2,8,8,128]{4,3,2,1,0:T(8,128)(2,1)}), bf16[8,2,8,8,128]{4,3,2,1,0:T(8,128)(2,1)S(1)}, u32[]{:S(2)}, u32[]{:S(2)}) %all-to-all-start) | async-done | bytes 262176 | tf_op jit(solution)/shard_map/all_to_all | solution.py:313
  21.2 1.3 %shard_map.77 = f32[16,16,128]{2,1,0:T(8,128)} custom-call(bf16[8,2,8,8,128]{4,3,2,1,0:T(8,128)(2,1)S(1)} %all-to-all-done.vol_ref, bf16[4,10,48,128]{3,2,1,0:T(8,128)(2,1)S(1)} %get-tuple-element.27.gpad, f32[16,64]{1,0:T(8,128)S(1)} %get-tuple-element.28.bias_ref), custom_call_target="tpu_custom_call" | custom-call | flops 6000000000 | tf_op jit(solution)/shard_map/pallas_call | solution.py:341
  22.6 10.9 %all-to-all-start.1 = ((f32[16,16,128]{2,1,0:T(8,128)}), f32[16,16,128]{2,1,0:T(8,128)S(1)}, u32[]{:S(2)}, u32[]{:S(2)}) async-start(f32[16,16,128]{2,1,0:T(8,128)} %shard_map.77), calls=%async_computation.1 | async-start | bytes 262144 | tf_op jit(solution)/shard_map/all_to_all | solution.py:349
  33.4 0.0 collective-permute-done.2.got_ref
  33.4 0.1 shard_map.79
  33.5 4.8 %collective-permute-start.3 = (bf16[6,2,8,8,128]{4,3,2,1,0:T(8,128)(2,1)S(1)}, bf16[6,2,8,8,128]{4,3,2,1,0:T(8,128)(2,1)S(1)}, u32[]{:S(2)}, u32[]{:S(2)}) collective-permute-start(bf16[6,2,8,8,128]{4,3,2,1,0:T(8,128)(2,1)S(1)} %get-tuple-element.31.sent_ref), channel_id=1, source_target_pairs={{0,4},{1,5},{2,6},{3,7},{4,0},{5,1},{6,2},{7,3},{8,12},{9,13},{10,... | collective-permute-start | bytes 589832 | tf_op jit(solution)/shard_map/ppermute | solution.py:361
  38.3 3.0 %all-to-all-done.1.parts_ref = f32[16,16,128]{2,1,0:T(8,128)S(1)} async-done(((f32[16,16,128]{2,1,0:T(8,128)}), f32[16,16,128]{2,1,0:T(8,128)S(1)}, u32[]{:S(2)}, u32[]{:S(2)}) %all-to-all-start.1) | async-done | bytes 131104 | tf_op jit(solution)/shard_map/all_to_all | solution.py:349
  41.3 17.1 %psum.7.mine_ref = f32[16,128]{1,0:T(8,128)S(1)} all-reduce(f32[16,128]{1,0:T(8,128)S(1)} %shard_map.78), channel_id=1, replica_groups={{0,128,256,384},{8,136,264,392},{16,144,272,400},{24,152,280,408},{32,1..., use_global_device_ids=true, to_apply=%region_0.1 | all-reduce | flops 2048 | bytes 16384 | tf_op jit(solution)/shard_map/psum | solution.py:370
  58.4 0.0 collective-permute-done.3.got_ref
  58.5 0.7 shard_map.80
  59.1 4.7 %all-to-all-start.2 = ((f32[16,16,128]{2,1,0:T(8,128)}), f32[16,16,128]{2,1,0:T(8,128)S(1)}, u32[]{:S(2)}, u32[]{:S(2)}) async-start(f32[16,16,128]{2,1,0:T(8,128)} %shard_map.80), calls=%async_computation.2 | async-start | bytes 262144 | tf_op jit(solution)/shard_map/all_to_all | solution.py:390
  63.9 0.0 copy-start.2
  63.9 1.9 %collective-permute-start.4 = (bf16[6,2,8,8,128]{4,3,2,1,0:T(8,128)(2,1)S(1)}, bf16[6,2,8,8,128]{4,3,2,1,0:T(8,128)(2,1)S(1)}, u32[]{:S(2)}, u32[]{:S(2)}) collective-permute-start(bf16[6,2,8,8,128]{4,3,2,1,0:T(8,128)(2,1)S(1)} %get-tuple-element.39.sent_ref), channel_id=1, source_target_pairs={{0,1},{1,0},{2,3},{3,2},{4,5},{5,4},{6,7},{7,6},{8,9},{9,8},{10,11... | collective-permute-start | bytes 589832 | tf_op jit(solution)/shard_map/ppermute | solution.py:389
  65.8 0.0 copy-done.2
  65.8 1.0 %shard_map.81.part_ref = f32[2,8,48,128]{3,2,1,0:T(8,128)S(1)} custom-call(f32[16]{0:T(128)S(1)} %copy-done.2, bf16[8,2,8,8,128]{4,3,2,1,0:T(8,128)(2,1)S(1)} %all-to-all-done.vol_ref, bf16[27,16,64]{2,1,0:T(8,128)(2,1)S(1)} %bitcast.13), custom_call_target="tpu_custom_call" | custom-call | tf_op jit(solution)/shard_map/pallas_call | solution.py:391
  66.8 4.9 %all-to-all-done.2.refs_0_ = f32[16,16,128]{2,1,0:T(8,128)S(1)} async-done(((f32[16,16,128]{2,1,0:T(8,128)}), f32[16,16,128]{2,1,0:T(8,128)S(1)}, u32[]{:S(2)}, u32[]{:S(2)}) %all-to-all-start.2) | async-done | bytes 131104 | tf_op jit(solution)/shard_map/all_to_all | solution.py:390
  71.7 0.0 collective-permute-done.4.got_ref
  71.7 1.0 %shard_map.84 = (f32[27,16,64]{2,1,0:T(8,128)}, f32[1,16]{1,0:T(1,128)}, bf16[16,2,8,128]{3,2,1,0:T(8,128)(2,1)}, bf16[8,2,8,128]{3,2,1,0:T(8,128)(2,1)}) custom-call(f32[16,16,128]{2,1,0:T(8,128)S(1)} %shard_map.82.sums_ref, f32[2,8,48,128]{3,2,1,0:T(8,128)S(1)} %shard_map.81.part_ref, f32[1,2,8,8,128]{4,3,2,1,0:T(8,128)S(1)} %get-tuple-element.38.keep_ref, ...), custom_call_target="tpu_custom_call" | custom-call | tf_op jit(solution)/shard_map/pallas_call | solution.py:409
  (7 shorter events, 0.1 us)
Async XLA Ops:
  0.6 0.8 %copy-start.3 = (bf16[8,2,8,128]{3,2,1,0:T(8,128)(2,1)S(1)}, bf16[8,2,8,128]{3,2,1,0:T(8,128)(2,1)}, u32[]{:S(2)}) copy-start(bf16[8,2,8,128]{3,2,1,0:T(8,128)(2,1)} %param.4) | copy-start | bytes 98308
  1.5 14.0 %collective-permute-start = (bf16[24,8,128]{2,1,0:T(8,128)(2,1)S(1)}, bf16[24,8,128]{2,1,0:T(8,128)(2,1)S(1)}, u32[]{:S(2)}, u32[]{:S(2)}) collective-permute-start(bf16[24,8,128]{2,1,0:T(8,128)(2,1)S(1)} %pad_maximum_fusion), channel_id=1, source_target_pairs={{8,16},{16,8},{24,32},{32,24},{40,48},{48,40},{56,64},{64,56},{72,... | collective-permute-start | bytes 147464 | tf_op jit(solution)/shard_map/ppermute | solution.py:300
  2.9 12.6 %copy-start = (bf16[27,64,16]{1,2,0:T(8,128)(2,1)S(1)}, bf16[27,64,16]{1,2,0:T(8,128)(2,1)}, u32[]{:S(2)}) copy-start(bf16[27,64,16]{1,2,0:T(8,128)(2,1)} %param.5) | copy-start | bytes 165892
  2.9 18.3 %all-to-all-start = ((bf16[8,2,8,8,128]{4,3,2,1,0:T(8,128)(2,1)}), bf16[8,2,8,8,128]{4,3,2,1,0:T(8,128)(2,1)S(1)}, u32[]{:S(2)}, u32[]{:S(2)}) async-start(bf16[8,2,8,8,128]{4,3,2,1,0:T(8,128)(2,1)} %broadcast_in_dim.2), calls=%async_computation | async-start | bytes 524288 | tf_op jit(solution)/shard_map/all_to_all | solution.py:313
  11.8 3.7 %copy-start.1 = (bf16[16,2,8,128]{3,2,1,0:T(8,128)(2,1)S(1)}, bf16[16,2,8,128]{3,2,1,0:T(8,128)(2,1)}, u32[]{:S(2)}) copy-start(bf16[16,2,8,128]{3,2,1,0:T(8,128)(2,1)} %grad_ref.1) | copy-start | bytes 196612
  11.8 6.1 %collective-permute-start.1 = (bf16[24,8,128]{2,1,0:T(8,128)(2,1)S(1)}, bf16[24,8,128]{2,1,0:T(8,128)(2,1)S(1)}, u32[]{:S(2)}, u32[]{:S(2)}) collective-permute-start(bf16[24,8,128]{2,1,0:T(8,128)(2,1)S(1)} %pad_maximum_fusion.1), channel_id=1, source_target_pairs={{0,8},{8,0},{16,24},{24,16},{32,40},{40,32},{48,56},{56,48},{64,72... | collective-permute-start | bytes 147464 | tf_op jit(solution)/shard_map/ppermute | solution.py:300
  18.3 15.1 %collective-permute-start.2 = (bf16[9,2,8,8,128]{4,3,2,1,0:T(8,128)(2,1)S(1)}, bf16[9,2,8,8,128]{4,3,2,1,0:T(8,128)(2,1)S(1)}, u32[]{:S(2)}, u32[]{:S(2)}) collective-permute-start(bf16[9,2,8,8,128]{4,3,2,1,0:T(8,128)(2,1)S(1)} %get-tuple-element.30.sent_ref), channel_id=1, source_target_pairs={{0,2},{1,3},{2,0},{3,1},{4,6},{5,7},{6,4},{7,5},{8,10},{9,11},{10,... | collective-permute-start | bytes 884744 | tf_op jit(solution)/shard_map/ppermute | solution.py:340
  22.6 18.7 %all-to-all-start.1 = ((f32[16,16,128]{2,1,0:T(8,128)}), f32[16,16,128]{2,1,0:T(8,128)S(1)}, u32[]{:S(2)}, u32[]{:S(2)}) async-start(f32[16,16,128]{2,1,0:T(8,128)} %shard_map.77), calls=%async_computation.1 | async-start | bytes 262144 | tf_op jit(solution)/shard_map/all_to_all | solution.py:349
  33.5 24.9 %collective-permute-start.3 = (bf16[6,2,8,8,128]{4,3,2,1,0:T(8,128)(2,1)S(1)}, bf16[6,2,8,8,128]{4,3,2,1,0:T(8,128)(2,1)S(1)}, u32[]{:S(2)}, u32[]{:S(2)}) collective-permute-start(bf16[6,2,8,8,128]{4,3,2,1,0:T(8,128)(2,1)S(1)} %get-tuple-element.31.sent_ref), channel_id=1, source_target_pairs={{0,4},{1,5},{2,6},{3,7},{4,0},{5,1},{6,2},{7,3},{8,12},{9,13},{10,... | collective-permute-start | bytes 589832 | tf_op jit(solution)/shard_map/ppermute | solution.py:361
  59.1 12.6 %all-to-all-start.2 = ((f32[16,16,128]{2,1,0:T(8,128)}), f32[16,16,128]{2,1,0:T(8,128)S(1)}, u32[]{:S(2)}, u32[]{:S(2)}) async-start(f32[16,16,128]{2,1,0:T(8,128)} %shard_map.80), calls=%async_computation.2 | async-start | bytes 262144 | tf_op jit(solution)/shard_map/all_to_all | solution.py:390
  63.9 1.9 %copy-start.2 = (f32[16]{0:T(128)S(1)}, f32[16]{0:T(128)}, u32[]{:S(2)}) copy-start(f32[16]{0:T(128)} %bias_ref.1) | copy-start | bytes 196
  63.9 7.8 %collective-permute-start.4 = (bf16[6,2,8,8,128]{4,3,2,1,0:T(8,128)(2,1)S(1)}, bf16[6,2,8,8,128]{4,3,2,1,0:T(8,128)(2,1)S(1)}, u32[]{:S(2)}, u32[]{:S(2)}) collective-permute-start(bf16[6,2,8,8,128]{4,3,2,1,0:T(8,128)(2,1)S(1)} %get-tuple-element.39.sent_ref), channel_id=1, source_target_pairs={{0,1},{1,0},{2,3},{3,2},{4,5},{5,4},{6,7},{7,6},{8,9},{9,8},{10,11... | collective-permute-start | bytes 589832 | tf_op jit(solution)/shard_map/ppermute | solution.py:389

commit v14 on v11

--- a/solution.py
+++ b/solution.py
@@ -83,17 +83,19 @@
     peers, depth, rows, share, cols = vol_ref.shape
     outs = bias_ref.shape[0]
     chans = peers * share
-    acc = jnp.zeros((27 * outs, chans), F32)
-    for d in range(depth):
-        for h in range(0, rows, 2):
-            cells = jnp.concatenate(
-                [
-                    jnp.concatenate([vol_ref[s, d, h + k] for s in range(peers)], axis=0)
-                    for k in range(2)
-                ],
-                axis=1,
-            )
-            acc = acc + dot_lanes(moved_rows(gpad, d, h), cells)
+    acc = None
+    for places in [[(d, h) for h in range(0, rows, 2)] for d in range(depth)]:
+        cells = jnp.concatenate(
+            [
+                jnp.concatenate([vol_ref[s, d, h + k] for s in range(peers)], axis=0)
+                for d, h in places
+                for k in range(2)
+            ],
+            axis=1,
+        )
+        moved = jnp.concatenate([moved_rows(gpad, d, h) for d, h in places], axis=1)
+        part = dot_lanes(moved, cells)
+        acc = part if acc is None else acc + part
     for r in range(14):
         first = acc[2 * r * outs : (2 * r + 1) * outs]
         second = bias_ref[...] if r == 13 else acc[(2 * r + 1) * outs : (2 * r + 2) * outs]

time: 73.2 us -> 73.2 us (level)
  no operation moved by 1% of the time
where the time goes in v14:
time: 73.2 us; the launch traced here: 72.6 us
  starting transfers between devices  37.3 us (51%)
  blocking collectives  17.2 us (23%)
  waiting for transfers between devices  10.7 us (15%)
  Pallas kernels  5.08 us (7%)
  local copies, waits for them, and re-layouts  1.57 us (2%)
  between operations  0.84 us (1%)
    psum x1, blocking collectives, local(): mine = lax.psum(mine, 'space', axis_index_groups=Z_GROUPS)  17.2 us
    all_to_all x1, starting transfers between devices, local(): parts = lax.all_to_all(sums, 'space', 0, 0, axis_index_groups=XY_GROUPS)  10.7 us
    all_to_all x1, starting transfers between devices, local(): lax.all_to_all(jnp.broadcast_to(own[None], (8,) + own.shape), 'filt', 0, 0)  8.93 us
    all_to_all x1, waiting for transfers between devices, local(): every = lax.all_to_all(spread, 'space', 0, 0, axis_index_groups=XY_GROUPS)  4.87 us
    ppermute x1, starting transfers between devices, local(): got = lax.ppermute(send, 'filt', swap_pairs(SWAPS[1]))  4.77 us
    all_to_all x1, starting transfers between devices, local(): every = lax.all_to_all(spread, 'space', 0, 0, axis_index_groups=XY_GROUPS)  4.72 us
    ppermute x1, starting transfers between devices, swap_edges(): inner = lax.ppermute(jnp.where(odd, head, tail), 'space', EVEN)  3.5 us
    all_to_all x1, waiting for transfers between devices, local(): parts = lax.all_to_all(sums, 'space', 0, 0, axis_index_groups=XY_GROUPS)  2.99 us
  transfers between devices with their start and end apart: 8, of which 4 were waited for; matrix products, arithmetic and copies ran while one was open for 1% of the time, Pallas kernels for 5%

profile of v14, /device:TPU:32, one launch (start us, length us, event | category | flops | bytes accessed | tf_op | source)
XLA Modules:
  0.0 72.6 jit_solution(627860937050828424)
XLA Ops:
  0.6 0.0 copy-start.3
  0.6 0.8 %slice_bitcast_fusion.1 = (bf16[16,8,128]{2,1,0:T(8,128)(2,1)S(1)}, bf16[16,8,128]{2,1,0:T(8,128)(2,1)S(1)}) fusion(bf16[16,2,8,128]{3,2,1,0:T(8,128)(2,1)} %grad_ref.1), kind=kLoop, calls=%fused_computation.5 | loop fusion | bytes 131072 | tf_op jit(solution)/shard_map/squeeze | solution.py:308
  1.4 0.0 copy-done.3
  1.5 0.7 collective-permute-start
  2.2 0.8 %broadcast_in_dim.2 = bf16[8,2,8,8,128]{4,3,2,1,0:T(8,128)(2,1)} broadcast(bf16[2,8,8,128]{3,2,1,0:T(8,128)(2,1)S(1)} %copy.8), dimensions={1,2,3,4} | broadcast | bytes 294912 | tf_op jit(solution)/shard_map/broadcast_in_dim | solution.py:311
  2.9 0.0 copy-start
  2.9 0.0 copy-start.1
  2.9 8.9 %all-to-all-start = ((bf16[8,2,8,8,128]{4,3,2,1,0:T(8,128)(2,1)}), bf16[8,2,8,8,128]{4,3,2,1,0:T(8,128)(2,1)S(1)}, u32[]{:S(2)}, u32[]{:S(2)}) async-start(bf16[8,2,8,8,128]{4,3,2,1,0:T(8,128)(2,1)} %broadcast_in_dim.2), calls=%async_computation | async-start | bytes 524288 | tf_op jit(solution)/shard_map/all_to_all | solution.py:311
  11.8 3.5 %collective-permute-start.1 = (bf16[24,8,128]{2,1,0:T(8,128)(2,1)S(1)}, bf16[24,8,128]{2,1,0:T(8,128)(2,1)S(1)}, u32[]{:S(2)}, u32[]{:S(2)}) collective-permute-start(bf16[24,8,128]{2,1,0:T(8,128)(2,1)S(1)} %get-tuple-element.44), channel_id=1, source_target_pairs={{0,8},{8,0},{16,24},{24,16},{32,40},{40,32},{48,56},{56,48},{64,72... | collective-permute-start | bytes 147464 | tf_op jit(solution)/shard_map/ppermute | solution.py:291
  15.4 0.0 collective-permute-done.outer_ref
  15.4 0.0 copy-done
  15.4 0.0 copy-done.1
  15.4 0.6 shard_map.75
  16.0 1.8 %collective-permute-done.1.inner_ref = bf16[24,8,128]{2,1,0:T(8,128)(2,1)S(1)} collective-permute-done((bf16[24,8,128]{2,1,0:T(8,128)(2,1)S(1)}, bf16[24,8,128]{2,1,0:T(8,128)(2,1)S(1)}, u32[]{:S(2)}, u32[]{:S(2)}) %collective-permute-start.1) | collective-permute-done | bytes 49184 | tf_op jit(solution)/shard_map/ppermute | solution.py:291
  17.8 0.3 shard_map.76
  18.1 2.1 %collective-permute-start.2 = (bf16[9,2,8,8,128]{4,3,2,1,0:T(8,128)(2,1)S(1)}, bf16[9,2,8,8,128]{4,3,2,1,0:T(8,128)(2,1)S(1)}, u32[]{:S(2)}, u32[]{:S(2)}) collective-permute-start(bf16[9,2,8,8,128]{4,3,2,1,0:T(8,128)(2,1)S(1)} %get-tuple-element.30.sent_ref), channel_id=1, source_target_pairs={{0,2},{1,3},{2,0},{3,1},{4,6},{5,7},{6,4},{7,5},{8,10},{9,11},{10,... | collective-permute-start | bytes 884744 | tf_op jit(solution)/shard_map/ppermute | solution.py:338
  20.2 1.0 %all-to-all-done.vol_ref = bf16[8,2,8,8,128]{4,3,2,1,0:T(8,128)(2,1)S(1)} async-done(((bf16[8,2,8,8,128]{4,3,2,1,0:T(8,128)(2,1)}), bf16[8,2,8,8,128]{4,3,2,1,0:T(8,128)(2,1)S(1)}, u32[]{:S(2)}, u32[]{:S(2)}) %all-to-all-start) | async-done | bytes 262176 | tf_op jit(solution)/shard_map/all_to_all | solution.py:311
  21.2 1.3 %shard_map.77 = f32[16,16,128]{2,1,0:T(8,128)} custom-call(bf16[8,2,8,8,128]{4,3,2,1,0:T(8,128)(2,1)S(1)} %all-to-all-done.vol_ref, bf16[4,10,48,128]{3,2,1,0:T(8,128)(2,1)S(1)} %get-tuple-element.27.gpad, f32[16,64]{1,0:T(8,128)S(1)} %get-tuple-element.28.bias_ref), custom_call_target="tpu_custom_call" | custom-call | flops 6000000000 | tf_op jit(solution)/shard_map/pallas_call | solution.py:339
  22.6 10.7 %all-to-all-start.1 = ((f32[16,16,128]{2,1,0:T(8,128)}), f32[16,16,128]{2,1,0:T(8,128)S(1)}, u32[]{:S(2)}, u32[]{:S(2)}) async-start(f32[16,16,128]{2,1,0:T(8,128)} %shard_map.77), calls=%async_computation.1 | async-start | bytes 262144 | tf_op jit(solution)/shard_map/all_to_all | solution.py:347
  33.3 0.0 collective-permute-done.2.got_ref
  33.3 0.1 shard_map.79
  33.4 4.8 %collective-permute-start.3 = (bf16[6,2,8,8,128]{4,3,2,1,0:T(8,128)(2,1)S(1)}, bf16[6,2,8,8,128]{4,3,2,1,0:T(8,128)(2,1)S(1)}, u32[]{:S(2)}, u32[]{:S(2)}) collective-permute-start(bf16[6,2,8,8,128]{4,3,2,1,0:T(8,128)(2,1)S(1)} %get-tuple-element.31.sent_ref), channel_id=1, source_target_pairs={{0,4},{1,5},{2,6},{3,7},{4,0},{5,1},{6,2},{7,3},{8,12},{9,13},{10,... | collective-permute-start | bytes 589832 | tf_op jit(solution)/shard_map/ppermute | solution.py:359
  38.1 3.0 %all-to-all-done.1.parts_ref = f32[16,16,128]{2,1,0:T(8,128)S(1)} async-done(((f32[16,16,128]{2,1,0:T(8,128)}), f32[16,16,128]{2,1,0:T(8,128)S(1)}, u32[]{:S(2)}, u32[]{:S(2)}) %all-to-all-start.1) | async-done | bytes 131104 | tf_op jit(solution)/shard_map/all_to_all | solution.py:347
  41.1 17.2 %psum.7.mine_ref = f32[16,128]{1,0:T(8,128)S(1)} all-reduce(f32[16,128]{1,0:T(8,128)S(1)} %shard_map.78), channel_id=1, replica_groups={{0,128,256,384},{8,136,264,392},{16,144,272,400},{24,152,280,408},{32,1..., use_global_device_ids=true, to_apply=%region_0.1 | all-reduce | flops 2048 | bytes 16384 | tf_op jit(solution)/shard_map/psum | solution.py:368
  58.3 0.0 collective-permute-done.3.got_ref
  58.3 0.7 shard_map.80
  59.0 4.7 %all-to-all-start.2 = ((f32[16,16,128]{2,1,0:T(8,128)}), f32[16,16,128]{2,1,0:T(8,128)S(1)}, u32[]{:S(2)}, u32[]{:S(2)}) async-start(f32[16,16,128]{2,1,0:T(8,128)} %shard_map.80), calls=%async_computation.2 | async-start | bytes 262144 | tf_op jit(solution)/shard_map/all_to_all | solution.py:388
  63.8 0.0 copy-start.2
  63.8 1.9 %collective-permute-start.4 = (bf16[6,2,8,8,128]{4,3,2,1,0:T(8,128)(2,1)S(1)}, bf16[6,2,8,8,128]{4,3,2,1,0:T(8,128)(2,1)S(1)}, u32[]{:S(2)}, u32[]{:S(2)}) collective-permute-start(bf16[6,2,8,8,128]{4,3,2,1,0:T(8,128)(2,1)S(1)} %get-tuple-element.39.sent_ref), channel_id=1, source_target_pairs={{0,1},{1,0},{2,3},{3,2},{4,5},{5,4},{6,7},{7,6},{8,9},{9,8},{10,11... | collective-permute-start | bytes 589832 | tf_op jit(solution)/shard_map/ppermute | solution.py:387
  65.7 0.0 copy-done.2
  65.7 1.0 %shard_map.81.part_ref = f32[2,8,48,128]{3,2,1,0:T(8,128)S(1)} custom-call(f32[16]{0:T(128)S(1)} %copy-done.2, bf16[8,2,8,8,128]{4,3,2,1,0:T(8,128)(2,1)S(1)} %all-to-all-done.vol_ref, bf16[27,16,64]{2,1,0:T(8,128)(2,1)S(1)} %bitcast.21), custom_call_target="tpu_custom_call" | custom-call | tf_op jit(solution)/shard_map/pallas_call | solution.py:389
  66.7 4.9 %all-to-all-done.2.refs_0_ = f32[16,16,128]{2,1,0:T(8,128)S(1)} async-done(((f32[16,16,128]{2,1,0:T(8,128)}), f32[16,16,128]{2,1,0:T(8,128)S(1)}, u32[]{:S(2)}, u32[]{:S(2)}) %all-to-all-start.2) | async-done | bytes 131104 | tf_op jit(solution)/shard_map/all_to_all | solution.py:388
  71.6 0.0 collective-permute-done.4.got_ref
  71.6 1.0 %shard_map.84 = (f32[27,16,64]{2,1,0:T(8,128)}, f32[1,16]{1,0:T(1,128)}, bf16[16,2,8,128]{3,2,1,0:T(8,128)(2,1)}, bf16[8,2,8,128]{3,2,1,0:T(8,128)(2,1)}) custom-call(f32[16,16,128]{2,1,0:T(8,128)S(1)} %shard_map.82.sums_ref, f32[2,8,48,128]{3,2,1,0:T(8,128)S(1)} %shard_map.81.part_ref, f32[1,2,8,8,128]{4,3,2,1,0:T(8,128)S(1)} %get-tuple-element.38.keep_ref, ...), custom_call_target="tpu_custom_call" | custom-call | tf_op jit(solution)/shard_map/pallas_call | solution.py:407
  (6 shorter events, 0.1 us)
Async XLA Ops:
  0.6 0.8 %copy-start.3 = (bf16[8,2,8,128]{3,2,1,0:T(8,128)(2,1)S(1)}, bf16[8,2,8,128]{3,2,1,0:T(8,128)(2,1)}, u32[]{:S(2)}) copy-start(bf16[8,2,8,128]{3,2,1,0:T(8,128)(2,1)} %param.4) | copy-start | bytes 98308
  1.5 13.9 %collective-permute-start = (bf16[24,8,128]{2,1,0:T(8,128)(2,1)S(1)}, bf16[24,8,128]{2,1,0:T(8,128)(2,1)S(1)}, u32[]{:S(2)}, u32[]{:S(2)}) collective-permute-start(bf16[24,8,128]{2,1,0:T(8,128)(2,1)S(1)} %get-tuple-element.45), channel_id=1, source_target_pairs={{8,16},{16,8},{24,32},{32,24},{40,48},{48,40},{56,64},{64,56},{72,... | collective-permute-start | bytes 147464 | tf_op jit(solution)/shard_map/ppermute | solution.py:292
  2.9 12.5 %copy-start = (bf16[27,64,16]{1,2,0:T(8,128)(2,1)S(1)}, bf16[27,64,16]{1,2,0:T(8,128)(2,1)}, u32[]{:S(2)}) copy-start(bf16[27,64,16]{1,2,0:T(8,128)(2,1)} %param.5) | copy-start | bytes 165892
  2.9 12.5 %copy-start.1 = (bf16[16,2,8,128]{3,2,1,0:T(8,128)(2,1)S(1)}, bf16[16,2,8,128]{3,2,1,0:T(8,128)(2,1)}, u32[]{:S(2)}) copy-start(bf16[16,2,8,128]{3,2,1,0:T(8,128)(2,1)} %grad_ref.1) | copy-start | bytes 196612
  2.9 18.3 %all-to-all-start = ((bf16[8,2,8,8,128]{4,3,2,1,0:T(8,128)(2,1)}), bf16[8,2,8,8,128]{4,3,2,1,0:T(8,128)(2,1)S(1)}, u32[]{:S(2)}, u32[]{:S(2)}) async-start(bf16[8,2,8,8,128]{4,3,2,1,0:T(8,128)(2,1)} %broadcast_in_dim.2), calls=%async_computation | async-start | bytes 524288 | tf_op jit(solution)/shard_map/all_to_all | solution.py:311
  11.8 6.0 %collective-permute-start.1 = (bf16[24,8,128]{2,1,0:T(8,128)(2,1)S(1)}, bf16[24,8,128]{2,1,0:T(8,128)(2,1)S(1)}, u32[]{:S(2)}, u32[]{:S(2)}) collective-permute-start(bf16[24,8,128]{2,1,0:T(8,128)(2,1)S(1)} %get-tuple-element.44), channel_id=1, source_target_pairs={{0,8},{8,0},{16,24},{24,16},{32,40},{40,32},{48,56},{56,48},{64,72... | collective-permute-start | bytes 147464 | tf_op jit(solution)/shard_map/ppermute | solution.py:291
  18.1 15.1 %collective-permute-start.2 = (bf16[9,2,8,8,128]{4,3,2,1,0:T(8,128)(2,1)S(1)}, bf16[9,2,8,8,128]{4,3,2,1,0:T(8,128)(2,1)S(1)}, u32[]{:S(2)}, u32[]{:S(2)}) collective-permute-start(bf16[9,2,8,8,128]{4,3,2,1,0:T(8,128)(2,1)S(1)} %get-tuple-element.30.sent_ref), channel_id=1, source_target_pairs={{0,2},{1,3},{2,0},{3,1},{4,6},{5,7},{6,4},{7,5},{8,10},{9,11},{10,... | collective-permute-start | bytes 884744 | tf_op jit(solution)/shard_map/ppermute | solution.py:338
  22.6 18.6 %all-to-all-start.1 = ((f32[16,16,128]{2,1,0:T(8,128)}), f32[16,16,128]{2,1,0:T(8,128)S(1)}, u32[]{:S(2)}, u32[]{:S(2)}) async-start(f32[16,16,128]{2,1,0:T(8,128)} %shard_map.77), calls=%async_computation.1 | async-start | bytes 262144 | tf_op jit(solution)/shard_map/all_to_all | solution.py:347
  33.4 25.0 %collective-permute-start.3 = (bf16[6,2,8,8,128]{4,3,2,1,0:T(8,128)(2,1)S(1)}, bf16[6,2,8,8,128]{4,3,2,1,0:T(8,128)(2,1)S(1)}, u32[]{:S(2)}, u32[]{:S(2)}) collective-permute-start(bf16[6,2,8,8,128]{4,3,2,1,0:T(8,128)(2,1)S(1)} %get-tuple-element.31.sent_ref), channel_id=1, source_target_pairs={{0,4},{1,5},{2,6},{3,7},{4,0},{5,1},{6,2},{7,3},{8,12},{9,13},{10,... | collective-permute-start | bytes 589832 | tf_op jit(solution)/shard_map/ppermute | solution.py:359
  59.0 12.6 %all-to-all-start.2 = ((f32[16,16,128]{2,1,0:T(8,128)}), f32[16,16,128]{2,1,0:T(8,128)S(1)}, u32[]{:S(2)}, u32[]{:S(2)}) async-start(f32[16,16,128]{2,1,0:T(8,128)} %shard_map.80), calls=%async_computation.2 | async-start | bytes 262144 | tf_op jit(solution)/shard_map/all_to_all | solution.py:388
  63.8 1.9 %copy-start.2 = (f32[16]{0:T(128)S(1)}, f32[16]{0:T(128)}, u32[]{:S(2)}) copy-start(f32[16]{0:T(128)} %bias_ref.1) | copy-start | bytes 196
  63.8 7.8 %collective-permute-start.4 = (bf16[6,2,8,8,128]{4,3,2,1,0:T(8,128)(2,1)S(1)}, bf16[6,2,8,8,128]{4,3,2,1,0:T(8,128)(2,1)S(1)}, u32[]{:S(2)}, u32[]{:S(2)}) collective-permute-start(bf16[6,2,8,8,128]{4,3,2,1,0:T(8,128)(2,1)S(1)} %get-tuple-element.39.sent_ref), channel_id=1, source_target_pairs={{0,1},{1,0},{2,3},{3,2},{4,5},{5,4},{6,7},{7,6},{8,9},{9,8},{10,11... | collective-permute-start | bytes 589832 | tf_op jit(solution)/shard_map/ppermute | solution.py:387
